TPU v7x, 128 devices: a whole 4x4x4 slice. The times are simulated.
128 devices in a mesh: fx: 8 (over x, core), fy: 16 (over y, z).
Axes of the slice: x: 4, y: 4, z: 4, core: 2. Of those that a mesh axis runs over, the one named last changes fastest.
Arguments:
- ll_blocks: bfloat16 [8192, 8192], P(('fx', 'fy')), may hold values from -6 to 6
- dest_dev: int32 [8192, 2], P(('fx', 'fy')), may hold values from 0 to 127, as said below
- dest_pos: int32 [8192, 2], P(('fx', 'fy')), may hold values from 0 to 63, as said below
- fwd_id: int32 [8192, 2], P(('fx', 'fy')), may hold values from 0 to 63
- back_id: int32 [8192, 2], P(('fx', 'fy')), may hold values from 0 to 63
- fwd_table: bfloat16 [64, 128, 128], replicated, may hold values from -0.5 to 0.5
- back_table: bfloat16 [64, 128, 128], replicated, may hold values from -0.5 to 0.5
- kernel_one: bfloat16 [3, 3, 64, 64], replicated, may hold values from -0.25 to 0.25
- bias_one: float32 [64], replicated, may hold values from -3 to 3
- kernel_two: bfloat16 [3, 3, 64, 64], replicated, may hold values from -0.25 to 0.25
- bias_two: float32 [64], replicated, may hold values from -3 to 3
Outputs:
- ll_out: bfloat16 [8192, 8192], P(('fx', 'fy'))
Inputs may be any that keep to these rules, and one draw needn't show every extreme that they name: `dest_dev`: among the rows of one device no device is named more than 2 times, and that many is reached; each device is named in route 0 by exactly 64 rows; a row's two routes may name the same device. `dest_pos`: the route-0 rows that name a device name each of its 64 blocks exactly once.
All inputs are finite; a program needn't handle non-finite values.
Results may differ from a plain program's by a relative error of at most 0.015.
Values may be sent and summed in bfloat16 or wider, within the bound.
No kernel may reach another device: no remote copies, remote signals or barrier semaphores. Data moves between devices by JAX's collectives and lax.ppermute only.
A program may use at most 128 MiB of HBM per device.

v0:
```python
import jax
import jax.numpy as jnp
from jax import lax
from jax.experimental import pallas as pl
from jax.experimental.pallas import tpu as pltpu
from jax.sharding import PartitionSpec as P

CAP = 2
AXES = ("fx", "fy")
F32 = jnp.float32
BF16 = jnp.bfloat16
VMEM_LIMIT = 48 * 1024 * 1024

META = 8
NT = (((1,), (1,)), ((), ()))


def code_of(dev, pos, fwd, back):
    return ((dev * 64 + pos) * 64 + fwd) * 64 + back


def code_dev(code):
    return lax.shift_right_logical(code, 18)


def code_pos(code):
    return lax.shift_right_logical(code, 12) & 63


def code_fwd(code):
    return lax.shift_right_logical(code, 6) & 63


def code_back(code):
    return code & 63


def smem():
    return pl.BlockSpec(memory_space=pltpu.SMEM)


def vmem():
    return pl.BlockSpec(memory_space=pltpu.VMEM)


def forward_kernel(code_ref, x_ref, table_ref, send_ref, slot_ref, rows_ref, count_ref, pos_ref):
    blocks, width = x_ref.shape
    seg = table_ref.shape[1]
    chans = width // seg
    devices = count_ref.shape[0]

    def clear(d, carry):
        count_ref[d] = 0
        pos_ref[CAP * d] = -1
        pos_ref[CAP * d + 1] = -1
        return carry

    lax.fori_loop(0, devices, clear, 0, unroll=4)
    for c in range(chans):
        rows_ref[c * blocks : (c + 1) * blocks, :] = x_ref[:, c * seg : (c + 1) * seg].astype(F32)

    def one_block(b, carry):
        codes = [code_ref[b, t] for t in range(2)]
        x = rows_ref[pl.ds(b, chans, stride=blocks), :].astype(BF16)
        weights = jnp.concatenate([table_ref[code_fwd(code)] for code in codes], axis=0)
        product = lax.dot_general(x, weights, NT, preferred_element_type=F32)
        for t, code in enumerate(codes):
            dev = code_dev(code)
            rank = count_ref[dev]
            count_ref[dev] = rank + 1
            slot_ref[b, t] = dev * CAP + rank
            pos_ref[dev * CAP + rank] = code_pos(code)
            at = pl.multiple_of(rank * chans, chans)
            send_ref[dev, pl.ds(at, chans), :] = product[:, t * seg : (t + 1) * seg].astype(BF16)
        return carry

    lax.fori_loop(0, blocks, one_block, 0, unroll=4)
    half = lax.broadcasted_iota(jnp.int32, (META, seg), 0) < META // 2

    def positions(d, carry):
        both = jnp.where(half, pos_ref[CAP * d], pos_ref[CAP * d + 1])
        send_ref[d, CAP * chans :, :] = both.astype(F32).astype(BF16)
        return carry

    lax.fori_loop(0, devices, positions, 0, unroll=4)


def forward_remap(codes, ll_blocks, fwd_table, devices):
    blocks, width = ll_blocks.shape
    seg = fwd_table.shape[1]
    chans = width // seg
    return pl.pallas_call(
        forward_kernel,
        out_shape=(
            jax.ShapeDtypeStruct((devices, CAP * chans + META, seg), BF16),
            jax.ShapeDtypeStruct((blocks, 2), jnp.int32),
        ),
        in_specs=[smem(), vmem(), vmem()],
        out_specs=(vmem(), smem()),
        scratch_shapes=[
            pltpu.VMEM((chans * blocks, seg), F32),
            pltpu.SMEM((devices,), jnp.int32),
            pltpu.SMEM((devices * CAP,), jnp.int32),
        ],
        compiler_params=pltpu.CompilerParams(vmem_limit_bytes=VMEM_LIMIT),
        cost_estimate=pl.CostEstimate(
            flops=4 * blocks * width * seg, bytes_accessed=8 << 20, transcendentals=0
        ),
    )(codes, ll_blocks, fwd_table)


def field_kernel(pos_ref, got_ref, field_ref, edge_left_ref, edge_right_ref, sum_ref, edge_ref):
    step = pl.program_id(0)
    part = got_ref.shape[0]
    pairs, cols, lanes = field_ref.shape
    chans = lanes // 2
    spare = 2 * pairs

    @pl.when(step == 0)
    def _():
        def clear(r, carry):
            sum_ref[r] = jnp.zeros(sum_ref.shape[1:], F32)
            return carry

        lax.fori_loop(0, spare, clear, 0, unroll=4)

    def add(n, carry):
        for rank in range(CAP):
            pos = pos_ref[step * part + n, rank]
            row = jnp.where(pos < 0, spare, pos)
            block = got_ref[n, rank * chans : (rank + 1) * chans, :]
            sum_ref[row] = sum_ref[row] + block.astype(F32)
        return carry

    lax.fori_loop(0, part, add, 0, unroll=4)

    @pl.when(step == pl.num_programs(0) - 1)
    def _():
        def one_pair(g, carry):
            both = sum_ref[pl.ds(2 * g, 2)].reshape(2 * chans, cols)
            turned = both.T
            field_ref[g] = turned.astype(BF16)
            for n, k in enumerate((0, 1, cols - 2, cols - 1)):
                edge_ref[pl.ds(n * pairs + g, 1), :] = turned[k : k + 1, :]
            return carry

        lax.fori_loop(0, pairs, one_pair, 0, unroll=2)
        edge_left_ref[...] = edge_ref[0 : 2 * pairs, :].astype(BF16)
        edge_right_ref[...] = edge_ref[2 * pairs : 4 * pairs, :].astype(BF16)


def sum_field(positions, got, hblocks):
    devices, depth, cols = got.shape
    chans = (depth - META) // CAP
    pairs = hblocks // 2
    parts = 8
    part = devices // parts
    return pl.pallas_call(
        field_kernel,
        grid=(parts,),
        out_shape=(
            jax.ShapeDtypeStruct((pairs, cols, 2 * chans), BF16),
            jax.ShapeDtypeStruct((2 * pairs, 2 * chans), BF16),
            jax.ShapeDtypeStruct((2 * pairs, 2 * chans), BF16),
        ),
        in_specs=[smem(), pl.BlockSpec((part, depth, cols), lambda s: (s, 0, 0))],
        out_specs=(vmem(), vmem(), vmem()),
        scratch_shapes=[
            pltpu.VMEM((hblocks + 1, chans, cols), F32),
            pltpu.VMEM((4 * pairs, 2 * chans), F32),
        ],
        compiler_params=pltpu.CompilerParams(vmem_limit_bytes=VMEM_LIMIT),
    )(positions, got)


def gelu(x):
    return 0.5 * x * (1.0 + jnp.tanh(0.7978845608028654 * (x + 0.044715 * (x * x * x))))


def conv_kernel(
    pos_ref,
    place_ref,
    field_ref,
    above_ref,
    below_ref,
    left_ref,
    right_ref,
    k1_ref,
    b1_ref,
    k2_ref,
    b2_ref,
    send_ref,
    ext_ref,
    hid_ref,
    side_ref,
    halo_ref,
    state_ref,
):
    pairs, cols, lanes = field_ref.shape
    chans = lanes // 2
    slots = send_ref.shape[0]
    groups = pairs + 1
    ext_ref[0] = above_ref[0:cols, :]
    ext_ref[pl.ds(1, pairs)] = field_ref[...]
    ext_ref[pairs + 1] = below_ref[0:cols, :]
    above = above_ref[cols:, :].astype(F32)
    below = below_ref[cols:, :].astype(F32)
    left = left_ref[...].astype(F32)
    right = right_ref[...].astype(F32)
    for n, (source, at) in enumerate(((left, 0), (left, 1), (right, 0), (right, 1))):
        k = (0, 1, 4, 5)[n]
        side_ref[k, 0:1, :] = above[n : n + 1, :]
        side_ref[k, 1 : pairs + 1, :] = source[at * pairs : (at + 1) * pairs, :]
        side_ref[k, pairs + 1 : pairs + 2, :] = below[n : n + 1, :]

    def inner_side(g, carry):
        block = ext_ref[g]
        side_ref[2, pl.ds(g, 1), :] = block[0:16, :].astype(F32)[0:1, :]
        side_ref[3, pl.ds(g, 1), :] = block[cols - 16 : cols, :].astype(F32)[15:16, :]
        return carry

    lax.fori_loop(0, pairs + 2, inner_side, 0, unroll=2)

    def paired(k):
        return jnp.concatenate(
            [side_ref[k, 0:groups, :], side_ref[k, 1 : groups + 1, :]], axis=1
        ).astype(BF16)

    def taps(x, weights_ref, d):
        return jnp.dot(
            x, weights_ref[:, d * lanes : (d + 1) * lanes], preferred_element_type=F32
        )

    b1 = b1_ref[...]
    b2 = b2_ref[...]
    c = [paired(k) for k in range(6)]
    halo_ref[0, 0:groups, :] = taps(c[1], k1_ref, 0)
    halo_ref[1, 0:groups, :] = taps(c[4], k1_ref, 2)
    before = taps(c[0], k1_ref, 0) + taps(c[1], k1_ref, 1) + taps(c[2], k1_ref, 2) + b1
    after = taps(c[3], k1_ref, 0) + taps(c[4], k1_ref, 1) + taps(c[5], k1_ref, 2) + b1
    before = jnp.where(place_ref[0] > 0, gelu(before), 0.0)
    after = jnp.where(place_ref[1] > 0, gelu(after), 0.0)
    for n, (column, d) in enumerate(((before, 0), (after, 2))):
        side_ref[n, 0:groups, :] = column
        both = jnp.concatenate(
            [side_ref[n, 0:pairs, :], side_ref[n, 1 : pairs + 1, :]], axis=1
        ).astype(BF16)
        halo_ref[2 + n, 0:pairs, :] = taps(both, k2_ref, d)

    column = lax.broadcasted_iota(jnp.int32, (cols, lanes), 0)

    def convolve(source_ref, g, weights_ref, bias, h):
        rows = jnp.concatenate([source_ref[g], source_ref[g + 1]], axis=1)
        product = jnp.dot(rows, weights_ref[...], preferred_element_type=F32)
        ahead = pltpu.roll(product[:, 0:lanes], 1, axis=0)
        behind = pltpu.roll(product[:, 2 * lanes :], cols - 1, axis=0)
        ahead = jnp.where(column == 0, halo_ref[h, pl.ds(g, 1), :], ahead)
        behind = jnp.where(column == cols - 1, halo_ref[h + 1, pl.ds(g, 1), :], behind)
        return product[:, lanes : 2 * lanes] + ahead + behind + bias

    def first(g, carry):
        hid_ref[g] = gelu(convolve(ext_ref, g, k1_ref, b1, 0)).astype(BF16)
        return carry

    lax.fori_loop(0, groups, first, 0, unroll=3)

    def second(g, carry):
        state = convolve(hid_ref, g, k2_ref, b2, 2) + ext_ref[g + 1].astype(F32)
        state_ref[pl.ds(2 * g, 2)] = state.T.astype(BF16).reshape(2, chans, cols)
        return carry

    lax.fori_loop(0, pairs, second, 0, unroll=2)

    def pick(n, carry):
        pos = jnp.maximum(pos_ref[n // CAP, n % CAP], 0)
        send_ref[n] = state_ref[pos]
        return carry

    lax.fori_loop(0, slots, pick, 0, unroll=4)


def convolutions(positions, place, field, above, below, left, right, k1, b1, k2, b2):
    pairs, cols, lanes = field.shape
    chans = lanes // 2
    slots = positions.shape[0] * CAP
    return pl.pallas_call(
        conv_kernel,
        out_shape=jax.ShapeDtypeStruct((slots, chans, cols), BF16),
        in_specs=[smem(), smem()] + [vmem()] * 9,
        out_specs=vmem(),
        scratch_shapes=[
            pltpu.VMEM((pairs + 2, cols, lanes), BF16),
            pltpu.VMEM((pairs + 1, cols, lanes), BF16),
            pltpu.VMEM((6, pairs + 8, lanes), F32),
            pltpu.VMEM((4, pairs + 8, lanes), F32),
            pltpu.VMEM((2 * pairs, chans, cols), BF16),
        ],
        compiler_params=pltpu.CompilerParams(vmem_limit_bytes=VMEM_LIMIT),
    )(positions, place, field, above, below, left, right, k1, b1, k2, b2)


def backward_kernel(slot_ref, code_ref, got_ref, table_ref, out_ref, rows_ref):
    blocks, width = out_ref.shape
    seg = table_ref.shape[1]
    chans = width // seg

    def one_block(b, carry):
        state = jnp.concatenate([got_ref[slot_ref[b, 0]], got_ref[slot_ref[b, 1]]], axis=1)
        weights = jnp.concatenate(
            [table_ref[code_back(code_ref[b, t])] for t in range(2)], axis=1
        )
        rows_ref[pl.ds(b, chans, stride=blocks), :] = lax.dot_general(
            state, weights, NT, preferred_element_type=F32
        )
        return carry

    lax.fori_loop(0, blocks, one_block, 0, unroll=4)
    for c in range(chans):
        out_ref[:, c * seg : (c + 1) * seg] = rows_ref[c * blocks : (c + 1) * blocks, :].astype(BF16)


def backward_remap(slots, codes, got, back_table):
    blocks = slots.shape[0]
    _, chans, seg = got.shape
    return pl.pallas_call(
        backward_kernel,
        out_shape=jax.ShapeDtypeStruct((blocks, chans * seg), BF16),
        in_specs=[smem(), smem(), vmem(), vmem()],
        out_specs=vmem(),
        scratch_shapes=[pltpu.VMEM((chans * blocks, seg), F32)],
        compiler_params=pltpu.CompilerParams(vmem_limit_bytes=VMEM_LIMIT),
    )(slots, codes, got, back_table)


def row_pair_weights(kernel):
    none = jnp.zeros((1,) + kernel.shape[1:], kernel.dtype)
    upper = jnp.concatenate([kernel, none], axis=0)
    lower = jnp.concatenate([none, kernel], axis=0)
    both = jnp.stack([upper, lower], axis=3)
    both = both.transpose(0, 2, 1, 3, 4)
    chans = kernel.shape[2]
    return both.reshape(4 * chans, 3 * 2 * kernel.shape[3])


def exchange(buffer):
    return lax.all_to_all(buffer, AXES, split_axis=0, concat_axis=0, tiled=True)


def local(
    ll_blocks,
    dest_dev,
    dest_pos,
    fwd_id,
    back_id,
    fwd_table,
    back_table,
    kernel_one,
    bias_one,
    kernel_two,
    bias_two,
):
    n_fx = lax.axis_size("fx")
    n_fy = lax.axis_size("fy")
    devices = n_fx * n_fy
    hblocks = 64
    pairs = hblocks // 2
    codes = code_of(dest_dev, dest_pos, fwd_id, back_id)
    send, slots = forward_remap(codes, ll_blocks, fwd_table, devices)
    got = exchange(send)
    positions = got[:, got.shape[1] - META :: META // 2, 0].astype(jnp.int32)
    field, edge_left, edge_right = sum_field(positions, got, hblocks)

    right_going = [(j, j + 1) for j in range(n_fy - 1)]
    left_going = [(j + 1, j) for j in range(n_fy - 1)]
    down_going = [(i, (i + 1) % n_fx) for i in range(n_fx)]
    up_going = [((i + 1) % n_fx, i) for i in range(n_fx)]
    left = lax.ppermute(edge_right, "fy", right_going)
    right = lax.ppermute(edge_left, "fy", left_going)

    def row_message(g):
        corners = [side[at * pairs + g][None] for side in (left, right) for at in (0, 1)]
        rest = jnp.zeros((12, field.shape[2]), BF16)
        return jnp.concatenate([field[g]] + corners + [rest], axis=0)

    above = lax.ppermute(row_message(pairs - 1), "fx", down_going)
    below = lax.ppermute(row_message(0), "fx", up_going)
    j = lax.axis_index("fy")
    place = jnp.stack([(j > 0).astype(jnp.int32), (j < n_fy - 1).astype(jnp.int32)])
    send_back = convolutions(
        positions,
        place,
        field,
        above,
        below,
        left,
        right,
        row_pair_weights(kernel_one),
        jnp.tile(bias_one, 2)[None],
        row_pair_weights(kernel_two),
        jnp.tile(bias_two, 2)[None],
    )
    slot_shape = send_back.shape
    got_back = exchange(send_back.reshape(devices, -1, slot_shape[2])).reshape(slot_shape)
    return backward_remap(slots, codes, got_back, back_table)


def solution(mesh):
    blocked = P(AXES, None)
    in_specs = (blocked,) * 5 + (P(),) * 6
    return jax.shard_map(
        local, mesh=mesh, in_specs=in_specs, out_specs=P(AXES, None), check_vma=False
    )
```

profile of v0, /device:TPU:6, one launch (start us, length us, event | category | flops | bytes accessed | tf_op | source)
XLA Modules:
  0.0 186.2 jit_solution(17937720977430760568)
XLA Ops:
  0.0 0.7 multiply_add_fusion
  0.7 0.1 copy.33.code_ref
  0.8 0.0 copy-start.1
  0.8 1.6 copy-done.1
  2.4 0.0 copy-start.2
  2.4 1.2 copy-done.2
  3.7 7.6 %shard_map.109 = (bf16[128,136,128]{2,1,0:T(8,128)(2,1)}, s32[64,2]{1,0:T(8,128)S(1)}) custom-call(s32[64,2]{1,0:T(8,128)S(1)} %copy.33.code_ref, bf16[64,8192]{1,0:T(8,128)(2,1)S(1)} %copy-done.2, bf16[64,128,128]{2,1,0:T(8,128)(2,1)S(1)} %copy-done.1), custom_call_target="tpu_custom_call" | custom-call | flops 268435456 | bytes 8388608 | tf_op jit(solution)/shard_map/pallas_call | solution.py:92
  11.3 0.0 copy-start.3
  11.3 0.0 copy-start.4
  11.3 10.9 %all-to-all-start = ((bf16[128,136,128]{2,1,0:T(8,128)(2,1)}), bf16[128,136,128]{2,1,0:T(8,128)(2,1)}, u32[]{:S(2)}, u32[]{:S(2)}) async-start(bf16[128,136,128]{2,1,0:T(8,128)(2,1)} %get-tuple-element.11), calls=%async_computation | async-start | bytes 8912896 | tf_op jit(solution)/shard_map/all_to_all | solution.py:346
  22.2 0.0 copy-done.3
  22.2 0.1 pad_bitcast_fusion.3
  22.3 0.0 copy-done.4
  22.3 0.1 pad_bitcast_fusion.1
  22.4 0.0 copy-start.5
  22.4 0.1 maximum_bitcast_fusion
  22.5 0.0 copy-start.6
  22.5 0.1 maximum_bitcast_fusion.1
  22.6 55.6 %all-to-all-done.got_ref = bf16[128,136,128]{2,1,0:T(8,128)(2,1)} async-done(((bf16[128,136,128]{2,1,0:T(8,128)(2,1)}), bf16[128,136,128]{2,1,0:T(8,128)(2,1)}, u32[]{:S(2)}, u32[]{:S(2)}) %all-to-all-start) | async-done | bytes 4456480 | tf_op jit(solution)/shard_map/all_to_all | solution.py:346
  78.2 2.7 %slice.33 = bf16[128,2,1]{2,1,0:T(2,128)(2,1)S(1)} slice(bf16[128,136,128]{2,1,0:T(8,128)(2,1)} %all-to-all-done.got_ref), slice={[0:128:1], [128:136:4], [0:1:1]} | slice | bytes 1024 | tf_op jit(solution)/shard_map/slice | solution.py:370
  80.9 0.9 copy.38
  81.8 7.7 %shard_map.110 = (bf16[32,128,128]{2,1,0:T(8,128)(2,1)S(1)}, bf16[64,128]{1,0:T(8,128)(2,1)S(1)}, bf16[64,128]{1,0:T(8,128)(2,1)S(1)}) custom-call(s32[128,2]{1,0:T(8,128)S(1)} %bitcast_convert_fusion.pos_ref, bf16[128,136,128]{2,1,0:T(8,128)(2,1)} %all-to-all-done.got_ref), custom_call_target="tpu_custom_call" | custom-call | tf_op jit(solution)/shard_map/pallas_call | solution.py:158
  89.4 1.5 collective-permute-start
  90.9 1.3 collective-permute-start.1
  92.2 0.1 collective-permute-done.left_ref
  92.4 4.2 %collective-permute-done.1.right_ref = bf16[64,128]{1,0:T(8,128)(2,1)S(1)} collective-permute-done((bf16[64,128]{1,0:T(8,128)(2,1)S(1)}, bf16[64,128]{1,0:T(8,128)(2,1)S(1)}, u32[]{:S(2)}, u32[]{:S(2)}) %collective-permute-start.1) | collective-permute-done | bytes 16416 | tf_op jit(solution)/shard_map/ppermute | solution.py:378
  96.6 0.2 concatenate.18
  96.8 0.0 collective-permute-start.2
  96.8 0.2 concatenate.19
  96.9 1.7 collective-permute-start.3
  98.7 0.1 add_convert_fusion.place_ref
  98.8 0.4 copy.35
  99.2 0.3 reshape.16.k1_ref
  99.4 0.0 copy-done.5
  99.5 0.1 broadcast_in_dim_tile.6.b1_ref
  99.5 0.4 copy.36
  100.0 0.3 reshape.17.k2_ref
  100.2 0.0 copy-done.6
  100.2 0.1 broadcast_in_dim_tile.7.b2_ref
  100.3 0.0 collective-permute-done.2.above_ref
  100.3 0.0 collective-permute-done.3.below_ref
  100.3 13.0 %shard_map.111 = bf16[256,64,128]{2,1,0:T(8,128)(2,1)S(1)} custom-call(s32[128,2]{1,0:T(8,128)S(1)} %bitcast_convert_fusion.pos_ref, s32[2]{0:T(128)S(1)} %add_convert_fusion.place_ref, bf16[32,128,128]{2,1,0:T(8,128)(2,1)S(1)} %get-tuple-element.12.field_ref, bf16[144,128]{1,0:T(8,128)(2,1)S(1)} %collective-permute-done.2.above_ref, ...), custom_call_target="tpu_custom_call" | custom-call | tf_op jit(solution)/shard_map/pallas_call | solution.py:286
  113.4 0.0 copy-start
  113.4 65.4 %all_to_all.10 = bf16[128,128,128]{2,1,0:T(8,128)(2,1)} all-to-all(bf16[128,128,128]{2,1,0:T(8,128)(2,1)S(1)} %bitcast.23), channel_id=1, replica_groups=mesh['fx'=8,'fy'=16] {'fx','fy'}, dimensions={0} | all-to-all | bytes 8388608 | tf_op jit(solution)/shard_map/all_to_all | solution.py:346
  178.8 0.0 copy-done
  178.8 7.4 %shard_map.112 = bf16[64,8192]{1,0:T(8,128)(2,1)} custom-call(s32[64,2]{1,0:T(8,128)S(1)} %get-tuple-element.10.slot_ref, s32[64,2]{1,0:T(8,128)S(1)} %copy.33.code_ref, bf16[256,64,128]{2,1,0:T(8,128)(2,1)} %bitcast.24, bf16[64,128,128]{2,1,0:T(8,128)(2,1)S(1)} %copy-done), custom_call_target="tpu_custom_call" | custom-call | tf_op jit(solution)/shard_map/pallas_call | solution.py:325
  (7 shorter events, 0.0 us)
Async XLA Ops:
  0.8 1.6 copy-start.1
  2.4 1.2 copy-start.2
  11.3 10.9 %copy-start.3 = (bf16[3,3,64,64]{3,2,1,0:T(8,128)(2,1)S(1)}, bf16[3,3,64,64]{3,2,1,0:T(8,128)(2,1)}, u32[]{:S(2)}) copy-start(bf16[3,3,64,64]{3,2,1,0:T(8,128)(2,1)} %param.18) | copy-start | bytes 221188
  11.3 11.0 %copy-start.4 = (bf16[3,3,64,64]{3,2,1,0:T(8,128)(2,1)S(1)}, bf16[3,3,64,64]{3,2,1,0:T(8,128)(2,1)}, u32[]{:S(2)}) copy-start(bf16[3,3,64,64]{3,2,1,0:T(8,128)(2,1)} %param.20) | copy-start | bytes 221188
  11.3 66.9 %all-to-all-start = ((bf16[128,136,128]{2,1,0:T(8,128)(2,1)}), bf16[128,136,128]{2,1,0:T(8,128)(2,1)}, u32[]{:S(2)}, u32[]{:S(2)}) async-start(bf16[128,136,128]{2,1,0:T(8,128)(2,1)} %get-tuple-element.11), calls=%async_computation | async-start | bytes 8912896 | tf_op jit(solution)/shard_map/all_to_all | solution.py:346
  22.4 77.1 %copy-start.5 = (f32[64]{0:T(128)S(1)}, f32[64]{0:T(128)}, u32[]{:S(2)}) copy-start(f32[64]{0:T(128)} %param.19) | copy-start | bytes 772
  22.5 77.7 %copy-start.6 = (f32[64]{0:T(128)S(1)}, f32[64]{0:T(128)}, u32[]{:S(2)}) copy-start(f32[64]{0:T(128)} %param.21) | copy-start | bytes 772
  89.4 2.9 %collective-permute-start = (bf16[64,128]{1,0:T(8,128)(2,1)S(1)}, bf16[64,128]{1,0:T(8,128)(2,1)S(1)}, u32[]{:S(2)}, u32[]{:S(2)}) collective-permute-start(bf16[64,128]{1,0:T(8,128)(2,1)S(1)} %get-tuple-element.13), channel_id=1, source_target_pairs={{0,1},{1,2},{2,3},{3,4},{4,5},{5,6},{6,7},{7,8},{8,9},{9,10},{10,1... | collective-permute-start | bytes 49160 | tf_op jit(solution)/shard_map/ppermute | solution.py:377
  90.9 5.6 %collective-permute-start.1 = (bf16[64,128]{1,0:T(8,128)(2,1)S(1)}, bf16[64,128]{1,0:T(8,128)(2,1)S(1)}, u32[]{:S(2)}, u32[]{:S(2)}) collective-permute-start(bf16[64,128]{1,0:T(8,128)(2,1)S(1)} %get-tuple-element.14), channel_id=1, source_target_pairs={{1,0},{2,1},{3,2},{4,3},{5,4},{6,5},{7,6},{8,7},{9,8},{10,9},{11,1... | collective-permute-start | bytes 49160 | tf_op jit(solution)/shard_map/ppermute | solution.py:378
  96.8 3.6 %collective-permute-start.2 = (bf16[144,128]{1,0:T(8,128)(2,1)S(1)}, bf16[144,128]{1,0:T(8,128)(2,1)S(1)}, u32[]{:S(2)}, u32[]{:S(2)}) collective-permute-start(bf16[144,128]{1,0:T(8,128)(2,1)S(1)} %concatenate.18), channel_id=1, source_target_pairs={{0,16},{16,32},{32,48},{48,64},{64,80},{80,96},{96,112},{112,0},{1... | collective-permute-start | bytes 110600 | tf_op jit(solution)/shard_map/ppermute | solution.py:385
  96.9 3.4 %collective-permute-start.3 = (bf16[144,128]{1,0:T(8,128)(2,1)S(1)}, bf16[144,128]{1,0:T(8,128)(2,1)S(1)}, u32[]{:S(2)}, u32[]{:S(2)}) collective-permute-start(bf16[144,128]{1,0:T(8,128)(2,1)S(1)} %concatenate.19), channel_id=1, source_target_pairs={{16,0},{32,16},{48,32},{64,48},{80,64},{96,80},{112,96},{0,112},{1... | collective-permute-start | bytes 110600 | tf_op jit(solution)/shard_map/ppermute | solution.py:386
  113.4 65.4 %copy-start = (bf16[64,128,128]{2,1,0:T(8,128)(2,1)S(1)}, bf16[64,128,128]{2,1,0:T(8,128)(2,1)}, u32[]{:S(2)}) copy-start(bf16[64,128,128]{2,1,0:T(8,128)(2,1)} %table_ref.3) | copy-start | bytes 6291460
where the time goes:
time: 187 us; the launch traced here: 186 us
  blocking collectives  65.4 us (35%)
  waiting for transfers between devices  59.9 us (32%)
  Pallas kernels  35.8 us (19%)
  starting transfers between devices  15.4 us (8%)
  local copies, waits for them, and re-layouts  8.45 us (5%)
    all_to_all x1, blocking collectives, exchange(): return lax.all_to_all(buffer, AXES, split_axis=0, concat_axis=0, tiled=True)  65.4 us
    all_to_all x1, waiting for transfers between devices, exchange(): return lax.all_to_all(buffer, AXES, split_axis=0, concat_axis=0, tiled=True)  55.6 us
    pallas_call x1, Pallas kernels, convolutions(): pl.pallas_call(conv_kernel, out_shape=jax.ShapeDtypeStruct((slots, chans,...  13 us
    all_to_all x1, starting transfers between devices, exchange(): return lax.all_to_all(buffer, AXES, split_axis=0, concat_axis=0, tiled=True)  10.9 us
    pallas_call x1, Pallas kernels, sum_field(): pl.pallas_call(field_kernel, grid=(parts,), out_shape=(jax.ShapeDtypeStru...  7.65 us
    pallas_call x1, Pallas kernels, forward_remap(): pl.pallas_call(forward_kernel, out_shape=(jax.ShapeDtypeStruct((devices,...  7.62 us
    pallas_call x1, Pallas kernels, backward_remap(): pl.pallas_call(backward_kernel, out_shape=jax.ShapeDtypeStruct((blocks, c...  7.43 us
    ppermute x1, waiting for transfers between devices, local(): right = lax.ppermute(edge_left, 'fy', left_going)  4.22 us
  transfers between devices with their start and end apart: 5, of which 3 were waited for; matrix products, arithmetic and copies ran while one was open for 1% of the time, Pallas kernels for 0%

commit v1 on v0

v1 whole, which is shorter than its diff:
```python
import functools

import jax
import jax.numpy as jnp
from jax import lax
from jax.experimental import pallas as pl
from jax.experimental.pallas import tpu as pltpu
from jax.sharding import PartitionSpec as P

CAP = 2
META = 8
AXES = ("fx", "fy")
F32 = jnp.float32
BF16 = jnp.bfloat16
VMEM_LIMIT = 48 * 1024 * 1024
NT = (((1,), (1,)), ((), ()))


def code_of(dev, pos, fwd, back):
    return ((dev * 64 + pos) * 64 + fwd) * 64 + back


def code_dev(code):
    return lax.shift_right_logical(code, 18)


def code_pos(code):
    return lax.shift_right_logical(code, 12) & 63


def code_fwd(code):
    return lax.shift_right_logical(code, 6) & 63


def code_back(code):
    return code & 63


def smem():
    return pl.BlockSpec(memory_space=pltpu.SMEM)


def vmem():
    return pl.BlockSpec(memory_space=pltpu.VMEM)


def hbm():
    return pl.BlockSpec(memory_space=pl.ANY)


def params():
    return pltpu.CompilerParams(vmem_limit_bytes=VMEM_LIMIT)


def lane_iota(shape):
    return lax.broadcasted_iota(jnp.int32, shape, len(shape) - 1)


def forward_kernel(
    n_fy,
    code_ref,
    x_hbm,
    table_hbm,
    send_ref,
    slot_ref,
    x_ref,
    table_ref,
    rows_ref,
    edge_ref,
    stage_ref,
    meta_ref,
    packed_ref,
    count_ref,
    x_sem,
    table_sem,
    out_sem,
    meta_sem,
):
    blocks, width = x_ref.shape
    tables, seg, _ = table_ref.shape
    chans = width // seg
    devices = count_ref.shape[0]
    parts = x_sem.shape[0]
    wide = width // parts
    pieces = table_sem.shape[0]
    deep = tables // pieces
    x_copies = [
        pltpu.make_async_copy(
            x_hbm.at[:, pl.ds(q * wide, wide)], x_ref.at[:, pl.ds(q * wide, wide)], x_sem.at[q]
        )
        for q in range(parts)
    ]
    table_copies = [
        pltpu.make_async_copy(
            table_hbm.at[pl.ds(q * deep, deep)], table_ref.at[pl.ds(q * deep, deep)], table_sem.at[q]
        )
        for q in range(pieces)
    ]
    for copy in x_copies + table_copies:
        copy.start()

    def clear(d, carry):
        count_ref[d] = 0
        return carry

    lax.fori_loop(0, devices, clear, 0, unroll=8)
    meta_ref[...] = jnp.zeros_like(meta_ref)
    for q, copy in enumerate(x_copies):
        copy.wait()
        for c in range(q * wide // seg, (q + 1) * wide // seg):
            rows_ref[c * blocks : (c + 1) * blocks, :] = x_ref[:, c * seg : (c + 1) * seg].astype(F32)
    for q, copy in enumerate(table_copies):
        copy.wait()

        def edges(n, carry):
            edge_ref[n, 0:2, :] = table_ref[n, seg - 16 : seg, :].astype(F32)[14:16, :]
            edge_ref[n, 2:4, :] = table_ref[n, 0:16, :].astype(F32)[0:2, :]
            return carry

        lax.fori_loop(q * deep, (q + 1) * deep, edges, 0, unroll=4)
    lane = lane_iota((1, seg))

    def one_block(b, carry):
        codes = [code_ref[b, t] for t in range(2)]
        x = rows_ref[pl.ds(b, chans, stride=blocks), :].astype(BF16)
        weights = jnp.concatenate([table_ref[code_fwd(code)] for code in codes], axis=0)
        product = lax.dot_general(x, weights, NT, preferred_element_type=F32)
        tips = jnp.concatenate([edge_ref[code_fwd(code)] for code in codes], axis=0).astype(BF16)
        ends = lax.dot_general(tips, x, NT, preferred_element_type=F32)
        ends = jnp.concatenate([ends, ends], axis=1)
        for t, code in enumerate(codes):
            dev = code_dev(code)
            pos = (code_pos(code) + 1).astype(F32)
            rank = count_ref[dev]
            count_ref[dev] = rank + 1
            slot_ref[b, t] = dev * CAP + rank
            route = 2 * b + t
            stage_ref[route] = product[:, t * seg : (t + 1) * seg].astype(BF16)
            at = pl.multiple_of(rank * chans, chans)
            pltpu.make_async_copy(
                stage_ref.at[route], send_ref.at[dev, pl.ds(at, chans), :], out_sem
            ).start()
            meta_ref[dev, pl.ds(4 + rank, 1), :] = jnp.full((1, seg), pos, F32)
            col = lax.rem(dev, n_fy)
            mine = (lane >= chans) == (rank == 1)
            for side in range(2):
                inside = (col < n_fy - 1) if side == 0 else (col > 0)
                near = jnp.where(inside, dev + 1 - 2 * side, devices)
                first = t * 4 + side * 2
                meta_ref[near, pl.ds(2 * side + rank, 1), :] = jnp.where(
                    lane < chans, ends[first : first + 1, :], ends[first + 1 : first + 2, :]
                )
                old = meta_ref[near, 6 + side : 7 + side, :]
                meta_ref[near, 6 + side : 7 + side, :] = jnp.where(mine, pos, old)
        return carry

    lax.fori_loop(0, blocks, one_block, 0, unroll=8)
    packed_ref[...] = meta_ref[0:devices].astype(BF16)
    meta_copy = pltpu.make_async_copy(
        packed_ref, send_ref.at[:, pl.ds(CAP * chans, META), :], meta_sem
    )
    meta_copy.start()
    pltpu.make_async_copy(stage_ref, send_ref.at[:, pl.ds(0, chans), :], out_sem).wait()
    meta_copy.wait()


def forward_remap(codes, ll_blocks, fwd_table, devices, n_fy):
    blocks, width = ll_blocks.shape
    tables, seg, _ = fwd_table.shape
    chans = width // seg
    return pl.pallas_call(
        functools.partial(forward_kernel, n_fy),
        out_shape=(
            jax.ShapeDtypeStruct((devices, CAP * chans + META, seg), BF16),
            jax.ShapeDtypeStruct((blocks, 2), jnp.int32),
        ),
        in_specs=[smem(), hbm(), hbm()],
        out_specs=(hbm(), smem()),
        scratch_shapes=[
            pltpu.VMEM((blocks, width), BF16),
            pltpu.VMEM((tables, seg, seg), BF16),
            pltpu.VMEM((chans * blocks, seg), F32),
            pltpu.VMEM((tables, 4, seg), F32),
            pltpu.VMEM((2 * blocks, chans, seg), BF16),
            pltpu.VMEM((devices + 1, META, seg), F32),
            pltpu.VMEM((devices, META, seg), BF16),
            pltpu.SMEM((devices,), jnp.int32),
            pltpu.SemaphoreType.DMA((4,)),
            pltpu.SemaphoreType.DMA((8,)),
            pltpu.SemaphoreType.DMA,
            pltpu.SemaphoreType.DMA,
        ],
        compiler_params=params(),
    )(codes, ll_blocks, fwd_table)


def sum_kernel(
    got_hbm,
    field_ref,
    up_ref,
    down_ref,
    side_ref,
    pos_ref,
    got_ref,
    meta_ref,
    rows_ref,
    sum_ref,
    spot_ref,
    meta_sem,
    got_sem,
    spot_sem,
):
    devices, _, cols = got_ref.shape
    hblocks, chans, _ = field_ref.shape
    pairs = hblocks // 2
    lanes = 2 * chans
    parts = got_sem.shape[0]
    part = devices // parts
    meta_copy = pltpu.make_async_copy(
        got_hbm.at[:, pl.ds(CAP * chans, META), :], meta_ref, meta_sem
    )
    meta_copy.start()
    copies = [
        pltpu.make_async_copy(
            got_hbm.at[pl.ds(q * part, part), pl.ds(0, CAP * chans), :],
            got_ref.at[pl.ds(q * part, part)],
            got_sem.at[q],
        )
        for q in range(parts)
    ]
    for copy in copies:
        copy.start()

    def clear(r, carry):
        for rank in range(CAP):
            sum_ref[rank, r] = jnp.zeros((chans, cols), F32)
        return carry

    lax.fori_loop(0, hblocks, clear, 0, unroll=4)
    meta_copy.wait()
    rows_ref[...] = meta_ref[...].reshape(devices * META, lanes).astype(F32)

    def meta_row(n):
        return rows_ref[pl.ds(n, devices, stride=META), :]

    lane = lane_iota((devices, lanes))
    table = jnp.where(lane % 2 == 0, meta_row(4), meta_row(5))
    beside = [meta_row(6), meta_row(7)]
    for side in range(2):
        turned_half = pltpu.roll(beside[side], chans, axis=1)
        for rank in range(CAP):
            here = lane == 2 + 2 * side + rank
            table = jnp.where(here, beside[side] if rank == 0 else turned_half, table)
    spots = table.T[0:8, :].astype(jnp.int32) - 1
    pos_ref[...] = spots
    spot_copy = pltpu.make_async_copy(pos_ref, spot_ref, spot_sem)
    spot_copy.start()
    block = lax.broadcasted_iota(jnp.int32, (pairs, devices), 0)
    low = lane_iota((pairs, lanes)) < chans
    for side in range(2):
        sums = []
        for parity in range(2):
            total = jnp.zeros((pairs, lanes), F32)
            for rank in range(CAP):
                n = 2 + 2 * side + rank
                hit = (spots[n : n + 1, :] == 2 * block + parity).astype(F32).astype(BF16)
                total += jnp.dot(
                    hit, meta_row(2 * side + rank).astype(BF16), preferred_element_type=F32
                )
            sums.append(total)
        even, odd = sums
        side_ref[2 * side] = jnp.where(low, even, pltpu.roll(odd, chans, axis=1))
        side_ref[2 * side + 1] = jnp.where(low, pltpu.roll(even, chans, axis=1), odd)
    spot_copy.wait()
    for q, copy in enumerate(copies):
        copy.wait()

        def add(d, carry):
            for rank in range(CAP):
                pos = spot_ref[rank, d]
                row = jnp.where(pos < 0, hblocks, pos)
                block = got_ref[d, rank * chans : (rank + 1) * chans, :]
                sum_ref[rank, row] = sum_ref[rank, row] + block.astype(F32)
            return carry

        lax.fori_loop(q * part, (q + 1) * part, add, 0, unroll=4)

    def total_of(r):
        return sum_ref[0, r] + sum_ref[1, r]

    corners = jnp.zeros((up_ref.shape[0] - cols, lanes), F32)
    corner_row = lax.broadcasted_iota(jnp.int32, corners.shape, 0)
    for ref, g in ((up_ref, 0), (down_ref, pairs - 1)):
        ref[0:cols, :] = jnp.concatenate([total_of(2 * g), total_of(2 * g + 1)], axis=0).T.astype(BF16)
        rest = corners
        for n in range(4):
            rest = jnp.where(corner_row == n, side_ref[n, g : g + 1, :], rest)
        ref[cols:, :] = rest.astype(BF16)

    def finish(r, carry):
        field_ref[r] = total_of(r).astype(BF16)
        return carry

    lax.fori_loop(0, hblocks, finish, 0, unroll=4)


def sum_field(got, hblocks):
    devices, depth, cols = got.shape
    chans = (depth - META) // CAP
    pairs = hblocks // 2
    message = jax.ShapeDtypeStruct((cols + 16, 2 * chans), BF16)
    return pl.pallas_call(
        sum_kernel,
        out_shape=(
            jax.ShapeDtypeStruct((hblocks, chans, cols), BF16),
            message,
            message,
            jax.ShapeDtypeStruct((4, pairs, 2 * chans), F32),
            jax.ShapeDtypeStruct((8, devices), jnp.int32),
        ),
        in_specs=[hbm()],
        out_specs=(vmem(),) * 5,
        scratch_shapes=[
            pltpu.VMEM((devices, CAP * chans, cols), BF16),
            pltpu.VMEM((devices, META, cols), BF16),
            pltpu.VMEM((devices * META, cols), F32),
            pltpu.VMEM((CAP, hblocks + 1, chans, cols), F32),
            pltpu.SMEM((8, devices), jnp.int32),
            pltpu.SemaphoreType.DMA,
            pltpu.SemaphoreType.DMA((8,)),
            pltpu.SemaphoreType.DMA,
        ],
        compiler_params=params(),
    )(got)


def gelu(x):
    return 0.5 * x * (1.0 + jnp.tanh(0.7978845608028654 * (x + 0.044715 * (x * x * x))))


def taps(x, weights_ref, d):
    lanes = x.shape[1] // 2
    return jnp.dot(x, weights_ref[:, d * lanes : (d + 1) * lanes], preferred_element_type=F32)


def row_pair_conv(upper, lower, weights_ref, bias, before, after):
    cols, lanes = upper.shape
    rows = jnp.concatenate([upper, lower], axis=1)
    product = jnp.dot(rows, weights_ref[...], preferred_element_type=F32)
    column = lax.broadcasted_iota(jnp.int32, (cols, lanes), 0)
    ahead = pltpu.roll(product[:, 0:lanes], 1, axis=0)
    behind = pltpu.roll(product[:, 2 * lanes :], cols - 1, axis=0)
    ahead = jnp.where(column == 0, before, ahead)
    behind = jnp.where(column == cols - 1, after, behind)
    return product[:, lanes : 2 * lanes] + ahead + behind + bias


def round_to_bf16(x):
    return x.astype(BF16).astype(F32)


def inner_kernel(field_ref, side_ref, k1_ref, b1_ref, turned_ref, hid_ref, halo_ref):
    hblocks, chans, cols = field_ref.shape
    pairs = hblocks // 2

    def turn(g, carry):
        turned_ref[g] = field_ref[pl.ds(2 * g, 2)].reshape(2 * chans, cols).T
        return carry

    lax.fori_loop(0, pairs, turn, 0, unroll=4)
    b1 = b1_ref[...]
    for n, (k, d) in enumerate(((1, 0), (2, 2))):
        both = jnp.concatenate([side_ref[k, 0 : pairs - 1, :], side_ref[k, 1:pairs, :]], axis=1)
        halo_ref[n, 1:pairs, :] = taps(both.astype(BF16), k1_ref, d)

    def first(g, carry):
        out = row_pair_conv(
            turned_ref[g - 1],
            turned_ref[g],
            k1_ref,
            b1,
            halo_ref[0, pl.ds(g, 1), :],
            halo_ref[1, pl.ds(g, 1), :],
        )
        hid_ref[g] = gelu(out).astype(BF16)
        return carry

    lax.fori_loop(1, pairs, first, 0, unroll=4)


def inner_hidden(field, sides, k1, b1):
    hblocks, chans, cols = field.shape
    pairs = hblocks // 2
    shape = jax.ShapeDtypeStruct((pairs, cols, 2 * chans), BF16)
    return pl.pallas_call(
        inner_kernel,
        out_shape=(shape, shape),
        in_specs=[vmem()] * 4,
        out_specs=(vmem(), vmem()),
        scratch_shapes=[pltpu.VMEM((2, pairs + 8, 2 * chans), F32)],
        compiler_params=params(),
        cost_estimate=pl.CostEstimate(
            flops=2 * 8192 * 9 * 64 * 64, bytes_accessed=4 << 20, transcendentals=1 << 19
        ),
    )(field, sides, k1, b1)


def outer_kernel(
    pos_ref,
    place_ref,
    field_ref,
    hid_ref,
    sides_ref,
    above_ref,
    below_ref,
    k1_ref,
    b1_ref,
    k2_ref,
    b2_ref,
    send_ref,
    side_ref,
    halo_ref,
    state_ref,
    stage_ref,
    out_sem,
):
    pairs, cols, lanes = field_ref.shape
    chans = lanes // 2
    devices = pos_ref.shape[1]
    groups = pairs + 1
    above = above_ref[cols:, :].astype(F32)
    below = below_ref[cols:, :].astype(F32)
    for n, k in enumerate((0, 1, 4, 5)):
        side_ref[k, 0:1, :] = above[n : n + 1, :]
        side_ref[k, 1 : pairs + 1, :] = sides_ref[n]
        side_ref[k, pairs + 1 : pairs + 2, :] = below[n : n + 1, :]

    def ends(block):
        return (
            block[0:16, :].astype(F32)[0:1, :],
            block[cols - 16 : cols, :].astype(F32)[15:16, :],
        )

    for k, (high, low) in enumerate(zip(ends(above_ref[0:cols, :]), ends(below_ref[0:cols, :]))):
        side_ref[2 + k, 0:1, :] = high
        side_ref[2 + k, pairs + 1 : pairs + 2, :] = low

    def inner_side(g, carry):
        for k, end in enumerate(ends(field_ref[g])):
            side_ref[2 + k, pl.ds(g + 1, 1), :] = end
        return carry

    lax.fori_loop(0, pairs, inner_side, 0, unroll=4)

    def paired(k):
        return jnp.concatenate(
            [side_ref[k, 0:groups, :], side_ref[k, 1 : groups + 1, :]], axis=1
        ).astype(BF16)

    b1 = b1_ref[...]
    b2 = b2_ref[...]
    c = [paired(k) for k in range(6)]
    left = taps(c[1], k1_ref, 0)
    right = taps(c[4], k1_ref, 2)
    before = taps(c[0], k1_ref, 0) + taps(c[1], k1_ref, 1) + taps(c[2], k1_ref, 2) + b1
    after = taps(c[3], k1_ref, 0) + taps(c[4], k1_ref, 1) + taps(c[5], k1_ref, 2) + b1
    before = jnp.where(place_ref[0] > 0, gelu(before), 0.0)
    after = jnp.where(place_ref[1] > 0, gelu(after), 0.0)
    for n, (column, d) in enumerate(((before, 0), (after, 2))):
        side_ref[n, 0:groups, :] = column
        both = jnp.concatenate([side_ref[n, 0:pairs, :], side_ref[n, 1 : pairs + 1, :]], axis=1)
        halo_ref[n, 0:pairs, :] = taps(both.astype(BF16), k2_ref, d)

    def hidden(upper, lower, g):
        out = row_pair_conv(upper, lower, k1_ref, b1, left[g : g + 1, :], right[g : g + 1, :])
        return gelu(out).astype(BF16)

    def second(g, upper, lower):
        out = row_pair_conv(
            upper, lower, k2_ref, b2, halo_ref[0, pl.ds(g, 1), :], halo_ref[1, pl.ds(g, 1), :]
        )
        state = out + field_ref[g].astype(F32)
        state_ref[pl.ds(2 * g, 2)] = state.T.astype(BF16).reshape(2, chans, cols)

    second(0, hidden(above_ref[0:cols, :], field_ref[0], 0), hid_ref[1])
    second(pairs - 1, hid_ref[pairs - 1], hidden(field_ref[pairs - 1], below_ref[0:cols, :], pairs))

    def inner(g, carry):
        second(g, hid_ref[g], hid_ref[g + 1])
        return carry

    lax.fori_loop(1, pairs - 1, inner, 0, unroll=5)
    parts = out_sem.shape[0]
    part = devices // parts
    copies = []
    for q in range(parts):

        def pick(d, carry):
            for rank in range(CAP):
                pos = jnp.maximum(pos_ref[rank, d], 0)
                stage_ref[d, rank * chans : (rank + 1) * chans, :] = state_ref[pos]
            return carry

        lax.fori_loop(q * part, (q + 1) * part, pick, 0, unroll=4)
        piece = pl.ds(q * part, part)
        copies.append(pltpu.make_async_copy(stage_ref.at[piece], send_ref.at[piece], out_sem.at[q]))
        copies[-1].start()
    for copy in copies:
        copy.wait()


def outer_state(positions, place, field, hidden, sides, above, below, k1, b1, k2, b2):
    pairs, cols, lanes = field.shape
    chans = lanes // 2
    devices = positions.shape[1]
    return pl.pallas_call(
        outer_kernel,
        out_shape=jax.ShapeDtypeStruct((devices, CAP * chans, cols), BF16),
        in_specs=[smem(), smem()] + [vmem()] * 9,
        out_specs=hbm(),
        scratch_shapes=[
            pltpu.VMEM((6, pairs + 8, lanes), F32),
            pltpu.VMEM((2, pairs + 8, lanes), F32),
            pltpu.VMEM((2 * pairs, chans, cols), BF16),
            pltpu.VMEM((devices, CAP * chans, cols), BF16),
            pltpu.SemaphoreType.DMA((8,)),
        ],
        compiler_params=params(),
    )(positions, place, field, hidden, sides, above, below, k1, b1, k2, b2)


def backward_kernel(slot_ref, code_ref, got_hbm, table_ref, out_ref, got_ref, rows_ref, got_sem):
    blocks, width = out_ref.shape
    seg = table_ref.shape[1]
    chans = width // seg
    parts = got_sem.shape[0]
    part = blocks // parts

    def fetch(q):
        def one(b, carry):
            for t in range(2):
                slot = slot_ref[b, t]
                at = pl.multiple_of(lax.rem(slot, CAP) * chans, chans)
                pltpu.make_async_copy(
                    got_hbm.at[lax.div(slot, CAP), pl.ds(at, chans), :],
                    got_ref.at[q, 2 * (b - q * part) + t],
                    got_sem.at[q],
                ).start()
            return carry

        lax.fori_loop(q * part, (q + 1) * part, one, 0, unroll=4)

    def arrived(q):
        pltpu.make_async_copy(
            got_hbm.at[pl.ds(0, 2 * part), pl.ds(0, chans), :], got_ref.at[q], got_sem.at[q]
        ).wait()

    for q in range(parts):
        fetch(q)
    for q in range(parts):
        arrived(q)

        def one_block(n, carry):
            b = q * part + n
            state = jnp.concatenate([got_ref[q, 2 * n], got_ref[q, 2 * n + 1]], axis=1)
            weights = jnp.concatenate(
                [table_ref[code_back(code_ref[b, t])] for t in range(2)], axis=1
            )
            rows_ref[pl.ds(b, chans, stride=blocks), :] = lax.dot_general(
                state, weights, NT, preferred_element_type=F32
            )
            return carry

        lax.fori_loop(0, part, one_block, 0, unroll=16)
    for c in range(chans):
        out_ref[:, c * seg : (c + 1) * seg] = rows_ref[c * blocks : (c + 1) * blocks, :].astype(BF16)


def backward_remap(slots, codes, got, back_table):
    blocks = slots.shape[0]
    chans = got.shape[1] // CAP
    seg = got.shape[2]
    parts = 4
    return pl.pallas_call(
        backward_kernel,
        out_shape=jax.ShapeDtypeStruct((blocks, chans * seg), BF16),
        in_specs=[smem(), smem(), hbm(), vmem()],
        out_specs=vmem(),
        scratch_shapes=[
            pltpu.VMEM((parts, 2 * blocks // parts, chans, seg), BF16),
            pltpu.VMEM((chans * blocks, seg), F32),
            pltpu.SemaphoreType.DMA((parts,)),
        ],
        compiler_params=params(),
    )(slots, codes, got, back_table)


def row_pair_weights(kernel):
    none = jnp.zeros((1,) + kernel.shape[1:], kernel.dtype)
    upper = jnp.concatenate([kernel, none], axis=0)
    lower = jnp.concatenate([none, kernel], axis=0)
    both = jnp.stack([upper, lower], axis=3)
    both = both.transpose(0, 2, 1, 3, 4)
    chans = kernel.shape[2]
    return both.reshape(4 * chans, 3 * 2 * kernel.shape[3])


def exchange(buffer):
    return lax.all_to_all(buffer, AXES, split_axis=0, concat_axis=0, tiled=True)


def local(
    ll_blocks,
    dest_dev,
    dest_pos,
    fwd_id,
    back_id,
    fwd_table,
    back_table,
    kernel_one,
    bias_one,
    kernel_two,
    bias_two,
):
    n_fx = lax.axis_size("fx")
    n_fy = lax.axis_size("fy")
    hblocks = 64
    codes = code_of(dest_dev, dest_pos, fwd_id, back_id)
    send, slots = forward_remap(codes, ll_blocks, fwd_table, n_fx * n_fy, n_fy)
    field, up, down, sides, positions = sum_field(exchange(send), hblocks)
    above = lax.ppermute(down, "fx", [(i, (i + 1) % n_fx) for i in range(n_fx)])
    below = lax.ppermute(up, "fx", [((i + 1) % n_fx, i) for i in range(n_fx)])
    k1 = row_pair_weights(kernel_one)
    b1 = jnp.tile(bias_one, 2)[None]
    turned, hidden = inner_hidden(field, sides, k1, b1)
    j = lax.axis_index("fy")
    place = jnp.stack([(j > 0).astype(jnp.int32), (j < n_fy - 1).astype(jnp.int32)])
    k2 = row_pair_weights(kernel_two)
    b2 = jnp.tile(bias_two, 2)[None]
    send_back = outer_state(
        positions, place, turned, hidden, sides, above, below, k1, b1, k2, b2
    )
    return backward_remap(slots, codes, exchange(send_back), back_table)


def solution(mesh):
    blocked = P(AXES, None)
    in_specs = (blocked,) * 5 + (P(),) * 6
    return jax.shard_map(
        local, mesh=mesh, in_specs=in_specs, out_specs=P(AXES, None), check_vma=False
    )
```

time: 187 us -> 161 us (0.86)
  Pallas kernels: 35.8 us -> 28.6 us
  waiting for transfers between devices: 59.9 us -> 54 us
  blocking collectives: 65.4 us -> 59.9 us
  local copies, waits for them, and re-layouts: 8.45 us -> 4.58 us
  starting transfers between devices: 15.4 us -> 12.6 us
    pallas_call x3 -> x4, Pallas kernels: 28.3 us -> 22.4 us  [the longest x1 7.79 us: forward_remap(): pl.pallas_call(functools.partial(forward_kernel, n_fy), out_shape=(jax.Sh...]
    all_to_all x1, blocking collectives: 65.4 us -> 59.9 us  [exchange(): return lax.all_to_all(buffer, AXES, split_axis=0, concat_axis=0, tiled=True)]
    ppermute x4 -> x2, waiting for transfers between devices: 4.33 us -> 0.01 us  [the longest x1 0.01 us: local(): below = lax.ppermute(up, 'fx', [((i + 1) % n_fx, i) for i in range(n_fx)])]
    ppermute x4 -> x2, starting transfers between devices: 4.55 us -> 1.75 us  [the longest x1 1.73 us: local(): below = lax.ppermute(up, 'fx', [((i + 1) % n_fx, i) for i in range(n_fx)])]
    slice x3 -> x0, local copies, waits for them, and re-layouts: 2.68 us -> none  [the longest x1 2.67 us: local(): positions = got[:, got.shape[1] - META::META // 2, 0].astype(jnp.int32)]
  transfers between devices with their start and end apart: 5 -> 3, of which waited for: 3 -> 1; matrix products, arithmetic and copies ran while one was open for 1% -> 1% of each run, Pallas kernels for 0% -> 2%
where the time goes in v1:
time: 161 us
  blocking collectives  59.9 us (37%)
  waiting for transfers between devices  54 us (34%)
  Pallas kernels  28.6 us (18%)
  starting transfers between devices  12.6 us (8%)
  local copies, waits for them, and re-layouts  4.58 us (3%)
    all_to_all x1, blocking collectives, exchange(): return lax.all_to_all(buffer, AXES, split_axis=0, concat_axis=0, tiled=True)  59.9 us
    all_to_all x1, waiting for transfers between devices, exchange(): return lax.all_to_all(buffer, AXES, split_axis=0, concat_axis=0, tiled=True)  54 us
    all_to_all x1, starting transfers between devices, exchange(): return lax.all_to_all(buffer, AXES, split_axis=0, concat_axis=0, tiled=True)  10.9 us
    pallas_call x1, Pallas kernels, forward_remap(): pl.pallas_call(functools.partial(forward_kernel, n_fy), out_shape=(jax.Sh...  7.79 us
    pallas_call x1, Pallas kernels, outer_state(): pl.pallas_call(outer_kernel, out_shape=jax.ShapeDtypeStruct((devices, CAP...  6.24 us
    pallas_call x1, Pallas kernels, backward_remap(): pl.pallas_call(backward_kernel, out_shape=jax.ShapeDtypeStruct((blocks, c...  6.2 us
    pallas_call x1, Pallas kernels, sum_field(): pl.pallas_call(sum_kernel, out_shape=(jax.ShapeDtypeStruct((hblocks, chan...  4.61 us
    pallas_call x1, Pallas kernels, inner_hidden(): pl.pallas_call(inner_kernel, out_shape=(shape, shape), in_specs=[vmem()]...  3.73 us
  transfers between devices with their start and end apart: 3, of which 1 were waited for; matrix products, arithmetic and copies ran while one was open for 1% of the time, Pallas kernels for 2%

profile of v1, /device:TPU:6, one launch (start us, length us, event | category | flops | bytes accessed | tf_op | source)
XLA Modules:
  0.0 160.9 jit_solution(10167133413843521182)
XLA Ops:
  0.0 0.7 multiply_add_fusion
  0.7 0.1 copy.21.code_ref
  0.8 0.0 copy-start.1
  0.8 1.6 copy-done.1
  2.4 0.0 copy-start.2
  2.4 1.2 copy-done.2
  3.7 7.8 %shard_map.109 = (bf16[128,136,128]{2,1,0:T(8,128)(2,1)}, s32[64,2]{1,0:T(8,128)S(1)}) custom-call(s32[64,2]{1,0:T(8,128)S(1)} %copy.21.code_ref, bf16[64,8192]{1,0:T(8,128)(2,1)S(1)} %copy-done.2, bf16[64,128,128]{2,1,0:T(8,128)(2,1)S(1)} %copy-done.1), custom_call_target="tpu_custom_call" | custom-call | tf_op jit(solution)/shard_map/pallas_call | solution.py:171
  11.4 0.0 copy-start.3
  11.5 0.0 copy-start.5
  11.5 0.0 copy-start.4
  11.5 10.9 %all-to-all-start = ((bf16[128,136,128]{2,1,0:T(8,128)(2,1)}), bf16[128,136,128]{2,1,0:T(8,128)(2,1)}, u32[]{:S(2)}, u32[]{:S(2)}) async-start(bf16[128,136,128]{2,1,0:T(8,128)(2,1)} %get-tuple-element.15), calls=%async_computation | async-start | bytes 8912896 | tf_op jit(solution)/shard_map/all_to_all | solution.py:609
  22.4 0.0 copy-start.6
  22.4 0.0 copy-done.3
  22.4 0.1 pad_bitcast_fusion.3
  22.5 0.1 maximum_bitcast_fusion
  22.6 0.4 copy.22
  23.0 0.3 reshape.8.k1_ref
  23.3 0.0 copy-done.5
  23.3 0.1 broadcast_in_dim_tile.6.b1_ref
  23.4 0.0 copy-done.4
  23.4 0.1 pad_bitcast_fusion.1
  23.4 0.1 maximum_bitcast_fusion.1
  23.5 0.4 copy.23
  23.9 0.3 reshape.9.k2_ref
  24.2 0.0 copy-done.6
  24.2 0.1 broadcast_in_dim_tile.7.b2_ref
  24.3 0.1 add_convert_fusion.place_ref
  24.4 54.0 %all-to-all-done.got_hbm = bf16[128,136,128]{2,1,0:T(8,128)(2,1)} async-done(((bf16[128,136,128]{2,1,0:T(8,128)(2,1)}), bf16[128,136,128]{2,1,0:T(8,128)(2,1)}, u32[]{:S(2)}, u32[]{:S(2)}) %all-to-all-start) | async-done | bytes 4456480 | tf_op jit(solution)/shard_map/all_to_all | solution.py:609
  78.4 4.6 %shard_map.110 = (bf16[64,64,128]{2,1,0:T(8,128)(2,1)S(1)}, bf16[144,128]{1,0:T(8,128)(2,1)S(1)}, bf16[144,128]{1,0:T(8,128)(2,1)S(1)}, f32[4,32,128]{2,1,0:T(8,128)S(1)}, s32[8,128]{1,0:T(8,128)S(1)}) custom-call(bf16[128,136,128]{2,1,0:T(8,128)(2,1)} %all-to-all-done.got_hbm), custom_call_target="tpu_custom_call" | custom-call | tf_op jit(solution)/shard_map/pallas_call | solution.py:312
  83.0 0.0 collective-permute-start
  83.0 1.7 %collective-permute-start.1 = (bf16[144,128]{1,0:T(8,128)(2,1)S(1)}, bf16[144,128]{1,0:T(8,128)(2,1)S(1)}, u32[]{:S(2)}, u32[]{:S(2)}) collective-permute-start(bf16[144,128]{1,0:T(8,128)(2,1)S(1)} %get-tuple-element.22), channel_id=1, source_target_pairs={{16,0},{32,16},{48,32},{64,48},{80,64},{96,80},{112,96},{0,112},{1... | collective-permute-start | bytes 110600 | tf_op jit(solution)/shard_map/ppermute | solution.py:632
  84.7 3.7 %shard_map.111 = (bf16[32,128,128]{2,1,0:T(8,128)(2,1)S(1)}, bf16[32,128,128]{2,1,0:T(8,128)(2,1)S(1)}) custom-call(bf16[64,64,128]{2,1,0:T(8,128)(2,1)S(1)} %get-tuple-element.17.field_ref, f32[4,32,128]{2,1,0:T(8,128)S(1)} %get-tuple-element.18.side_ref.sides_ref, bf16[256,384]{1,0:T(8,128)(2,1)S(1)} %reshape.8.k1_ref, ...), custom_call_target="tpu_custom_call" | custom-call | flops 603979776 | bytes 4194304 | tf_op jit(solution)/shard_map/pallas_call | solution.py:395
  88.5 0.0 collective-permute-done.above_ref
  88.5 0.0 collective-permute-done.1.below_ref
  88.5 6.2 %shard_map.112 = bf16[128,128,128]{2,1,0:T(8,128)(2,1)} custom-call(s32[8,128]{1,0:T(8,128)S(1)} %get-tuple-element.16.pos_ref, s32[2]{0:T(128)S(1)} %add_convert_fusion.place_ref, bf16[32,128,128]{2,1,0:T(8,128)(2,1)S(1)} %get-tuple-element.19.field_ref, bf16[32,128,128]{2,1,0:T(8,128)(2,1)S(1)} %get-tuple-element.20.hid_ref, ...), custom_call_target="tpu_custom_call" | custom-call | tf_op jit(solution)/shard_map/pallas_call | solution.py:516
  94.8 0.0 copy-start
  94.8 59.9 %all_to_all.10.got_hbm = bf16[128,128,128]{2,1,0:T(8,128)(2,1)} all-to-all(bf16[128,128,128]{2,1,0:T(8,128)(2,1)} %shard_map.112), channel_id=1, replica_groups=mesh['fx'=8,'fy'=16] {'fx','fy'}, dimensions={0} | all-to-all | bytes 8388608 | tf_op jit(solution)/shard_map/all_to_all | solution.py:609
  154.7 0.0 copy-done
  154.7 6.2 %shard_map.113 = bf16[64,8192]{1,0:T(8,128)(2,1)} custom-call(s32[64,2]{1,0:T(8,128)S(1)} %get-tuple-element.14.slot_ref, s32[64,2]{1,0:T(8,128)S(1)} %copy.21.code_ref, bf16[128,128,128]{2,1,0:T(8,128)(2,1)} %all_to_all.10.got_hbm, bf16[64,128,128]{2,1,0:T(8,128)(2,1)S(1)} %copy-done), custom_call_target="tpu_custom_call" | custom-call | tf_op jit(solution)/shard_map/pallas_call | solution.py:584
  (2 shorter events, 0.0 us)
Async XLA Ops:
  0.8 1.6 copy-start.1
  2.4 1.2 copy-start.2
  11.4 10.9 %copy-start.3 = (bf16[3,3,64,64]{3,2,1,0:T(8,128)(2,1)S(1)}, bf16[3,3,64,64]{3,2,1,0:T(8,128)(2,1)}, u32[]{:S(2)}) copy-start(bf16[3,3,64,64]{3,2,1,0:T(8,128)(2,1)} %param.18) | copy-start | bytes 221188
  11.5 11.8 %copy-start.5 = (f32[64]{0:T(128)S(1)}, f32[64]{0:T(128)}, u32[]{:S(2)}) copy-start(f32[64]{0:T(128)} %param.19) | copy-start | bytes 772
  11.5 11.9 %copy-start.4 = (bf16[3,3,64,64]{3,2,1,0:T(8,128)(2,1)S(1)}, bf16[3,3,64,64]{3,2,1,0:T(8,128)(2,1)}, u32[]{:S(2)}) copy-start(bf16[3,3,64,64]{3,2,1,0:T(8,128)(2,1)} %param.20) | copy-start | bytes 221188
  11.5 66.9 %all-to-all-start = ((bf16[128,136,128]{2,1,0:T(8,128)(2,1)}), bf16[128,136,128]{2,1,0:T(8,128)(2,1)}, u32[]{:S(2)}, u32[]{:S(2)}) async-start(bf16[128,136,128]{2,1,0:T(8,128)(2,1)} %get-tuple-element.15), calls=%async_computation | async-start | bytes 8912896 | tf_op jit(solution)/shard_map/all_to_all | solution.py:609
  22.4 1.8 %copy-start.6 = (f32[64]{0:T(128)S(1)}, f32[64]{0:T(128)}, u32[]{:S(2)}) copy-start(f32[64]{0:T(128)} %param.21) | copy-start | bytes 772
  83.0 5.5 %collective-permute-start = (bf16[144,128]{1,0:T(8,128)(2,1)S(1)}, bf16[144,128]{1,0:T(8,128)(2,1)S(1)}, u32[]{:S(2)}, u32[]{:S(2)}) collective-permute-start(bf16[144,128]{1,0:T(8,128)(2,1)S(1)} %get-tuple-element.21), channel_id=1, source_target_pairs={{0,16},{16,32},{32,48},{48,64},{64,80},{80,96},{96,112},{112,0},{1... | collective-permute-start | bytes 110600 | tf_op jit(solution)/shard_map/ppermute | solution.py:631
  83.0 5.5 %collective-permute-start.1 = (bf16[144,128]{1,0:T(8,128)(2,1)S(1)}, bf16[144,128]{1,0:T(8,128)(2,1)S(1)}, u32[]{:S(2)}, u32[]{:S(2)}) collective-permute-start(bf16[144,128]{1,0:T(8,128)(2,1)S(1)} %get-tuple-element.22), channel_id=1, source_target_pairs={{16,0},{32,16},{48,32},{64,48},{80,64},{96,80},{112,96},{0,112},{1... | collective-permute-start | bytes 110600 | tf_op jit(solution)/shard_map/ppermute | solution.py:632
  94.8 59.9 %copy-start = (bf16[64,128,128]{2,1,0:T(8,128)(2,1)S(1)}, bf16[64,128,128]{2,1,0:T(8,128)(2,1)}, u32[]{:S(2)}) copy-start(bf16[64,128,128]{2,1,0:T(8,128)(2,1)} %table_ref.1) | copy-start | bytes 6291460

commit v2 on v1

--- a/solution.py
+++ b/solution.py
@@ -12,28 +12,9 @@
 AXES = ("fx", "fy")
 F32 = jnp.float32
 BF16 = jnp.bfloat16
-VMEM_LIMIT = 48 * 1024 * 1024
+VMEM_LIMIT = 40 * 1024 * 1024
+FULL_VMEM = 60 * 1024 * 1024
 NT = (((1,), (1,)), ((), ()))
-
-
-def code_of(dev, pos, fwd, back):
-    return ((dev * 64 + pos) * 64 + fwd) * 64 + back
-
-
-def code_dev(code):
-    return lax.shift_right_logical(code, 18)
-
-
-def code_pos(code):
-    return lax.shift_right_logical(code, 12) & 63
-
-
-def code_fwd(code):
-    return lax.shift_right_logical(code, 6) & 63
-
-
-def code_back(code):
-    return code & 63
 
 
 def smem():
@@ -48,8 +29,13 @@
     return pl.BlockSpec(memory_space=pl.ANY)
 
 
-def params():
-    return pltpu.CompilerParams(vmem_limit_bytes=VMEM_LIMIT)
+def params(limit=VMEM_LIMIT):
+    return pltpu.CompilerParams(vmem_limit_bytes=limit)
+
+
+def log2(count):
+    assert count & (count - 1) == 0
+    return count.bit_length() - 1
 
 
 def lane_iota(shape):
@@ -58,11 +44,19 @@
 
 def forward_kernel(
     n_fy,
-    code_ref,
+    dev_hbm,
+    pos_hbm,
+    fwd_hbm,
+    back_hbm,
     x_hbm,
     table_hbm,
     send_ref,
-    slot_ref,
+    return_hbm,
+    dev_ref,
+    pos_ref,
+    fwd_ref,
+    back_ref,
+    return_ref,
     x_ref,
     table_ref,
     rows_ref,
@@ -71,15 +65,18 @@
     meta_ref,
     packed_ref,
     count_ref,
+    code_sem,
     x_sem,
     table_sem,
     out_sem,
     meta_sem,
+    return_sem,
 ):
     blocks, width = x_ref.shape
     tables, seg, _ = table_ref.shape
     chans = width // seg
     devices = count_ref.shape[0]
+    assert n_fy == 1 << log2(n_fy)
     parts = x_sem.shape[0]
     wide = width // parts
     pieces = table_sem.shape[0]
@@ -96,7 +93,13 @@
         )
         for q in range(pieces)
     ]
-    for copy in x_copies + table_copies:
+    code_copies = [
+        pltpu.make_async_copy(source, target, code_sem.at[n])
+        for n, (source, target) in enumerate(
+            ((dev_hbm, dev_ref), (pos_hbm, pos_ref), (fwd_hbm, fwd_ref), (back_hbm, back_ref))
+        )
+    ]
+    for copy in code_copies + x_copies + table_copies:
         copy.start()
 
     def clear(d, carry):
@@ -118,22 +121,24 @@
             return carry
 
         lax.fori_loop(q * deep, (q + 1) * deep, edges, 0, unroll=4)
+    for copy in code_copies:
+        copy.wait()
     lane = lane_iota((1, seg))
 
     def one_block(b, carry):
-        codes = [code_ref[b, t] for t in range(2)]
+        tables_of = [fwd_ref[t, b] for t in range(2)]
         x = rows_ref[pl.ds(b, chans, stride=blocks), :].astype(BF16)
-        weights = jnp.concatenate([table_ref[code_fwd(code)] for code in codes], axis=0)
+        weights = jnp.concatenate([table_ref[n] for n in tables_of], axis=0)
         product = lax.dot_general(x, weights, NT, preferred_element_type=F32)
-        tips = jnp.concatenate([edge_ref[code_fwd(code)] for code in codes], axis=0).astype(BF16)
+        tips = jnp.concatenate([edge_ref[n] for n in tables_of], axis=0).astype(BF16)
         ends = lax.dot_general(tips, x, NT, preferred_element_type=F32)
         ends = jnp.concatenate([ends, ends], axis=1)
-        for t, code in enumerate(codes):
-            dev = code_dev(code)
-            pos = (code_pos(code) + 1).astype(F32)
+        for t in range(2):
+            dev = dev_ref[t, b]
+            pos = (pos_ref[t, b] + 1).astype(F32)
             rank = count_ref[dev]
             count_ref[dev] = rank + 1
-            slot_ref[b, t] = dev * CAP + rank
+            return_ref[t, b] = ((dev * CAP + rank) << log2(tables)) + back_ref[t, b]
             route = 2 * b + t
             stage_ref[route] = product[:, t * seg : (t + 1) * seg].astype(BF16)
             at = pl.multiple_of(rank * chans, chans)
@@ -141,7 +146,7 @@
                 stage_ref.at[route], send_ref.at[dev, pl.ds(at, chans), :], out_sem
             ).start()
             meta_ref[dev, pl.ds(4 + rank, 1), :] = jnp.full((1, seg), pos, F32)
-            col = lax.rem(dev, n_fy)
+            col = dev & (n_fy - 1)
             mine = (lane >= chans) == (rank == 1)
             for side in range(2):
                 inside = (col < n_fy - 1) if side == 0 else (col > 0)
@@ -154,17 +159,20 @@
                 meta_ref[near, 6 + side : 7 + side, :] = jnp.where(mine, pos, old)
         return carry
 
-    lax.fori_loop(0, blocks, one_block, 0, unroll=8)
+    lax.fori_loop(0, blocks, one_block, 0, unroll=True)
     packed_ref[...] = meta_ref[0:devices].astype(BF16)
     meta_copy = pltpu.make_async_copy(
         packed_ref, send_ref.at[:, pl.ds(CAP * chans, META), :], meta_sem
     )
     meta_copy.start()
+    return_copy = pltpu.make_async_copy(return_ref, return_hbm, return_sem)
+    return_copy.start()
     pltpu.make_async_copy(stage_ref, send_ref.at[:, pl.ds(0, chans), :], out_sem).wait()
     meta_copy.wait()
-
-
-def forward_remap(codes, ll_blocks, fwd_table, devices, n_fy):
+    return_copy.wait()
+
+
+def forward_remap(dest_dev, dest_pos, fwd_id, back_id, ll_blocks, fwd_table, devices, n_fy):
     blocks, width = ll_blocks.shape
     tables, seg, _ = fwd_table.shape
     chans = width // seg
@@ -172,11 +180,16 @@
         functools.partial(forward_kernel, n_fy),
         out_shape=(
             jax.ShapeDtypeStruct((devices, CAP * chans + META, seg), BF16),
-            jax.ShapeDtypeStruct((blocks, 2), jnp.int32),
+            jax.ShapeDtypeStruct((2, blocks), jnp.int32),
         ),
-        in_specs=[smem(), hbm(), hbm()],
-        out_specs=(hbm(), smem()),
+        in_specs=[hbm()] * 6,
+        out_specs=(hbm(), hbm()),
         scratch_shapes=[
+            pltpu.SMEM((2, blocks), jnp.int32),
+            pltpu.SMEM((2, blocks), jnp.int32),
+            pltpu.SMEM((2, blocks), jnp.int32),
+            pltpu.SMEM((2, blocks), jnp.int32),
+            pltpu.SMEM((2, blocks), jnp.int32),
             pltpu.VMEM((blocks, width), BF16),
             pltpu.VMEM((tables, seg, seg), BF16),
             pltpu.VMEM((chans * blocks, seg), F32),
@@ -186,12 +199,14 @@
             pltpu.VMEM((devices, META, seg), BF16),
             pltpu.SMEM((devices,), jnp.int32),
             pltpu.SemaphoreType.DMA((4,)),
+            pltpu.SemaphoreType.DMA((4,)),
             pltpu.SemaphoreType.DMA((8,)),
             pltpu.SemaphoreType.DMA,
             pltpu.SemaphoreType.DMA,
+            pltpu.SemaphoreType.DMA,
         ],
-        compiler_params=params(),
-    )(codes, ll_blocks, fwd_table)
+        compiler_params=params(FULL_VMEM),
+    )(dest_dev.T, dest_pos.T, fwd_id.T, back_id.T, ll_blocks, fwd_table)
 
 
 def sum_kernel(
@@ -385,7 +400,7 @@
         hid_ref[g] = gelu(out).astype(BF16)
         return carry
 
-    lax.fori_loop(1, pairs, first, 0, unroll=4)
+    lax.fori_loop(1, pairs, first, 0, unroll=True)
 
 
 def inner_hidden(field, sides, k1, b1):
@@ -406,7 +421,7 @@
 
 
 def outer_kernel(
-    pos_ref,
+    pos_hbm,
     place_ref,
     field_ref,
     hid_ref,
@@ -422,8 +437,12 @@
     halo_ref,
     state_ref,
     stage_ref,
+    pos_ref,
     out_sem,
+    pos_sem,
 ):
+    pos_copy = pltpu.make_async_copy(pos_hbm, pos_ref, pos_sem)
+    pos_copy.start()
     pairs, cols, lanes = field_ref.shape
     chans = lanes // 2
     devices = pos_ref.shape[1]
@@ -464,8 +483,8 @@
     right = taps(c[4], k1_ref, 2)
     before = taps(c[0], k1_ref, 0) + taps(c[1], k1_ref, 1) + taps(c[2], k1_ref, 2) + b1
     after = taps(c[3], k1_ref, 0) + taps(c[4], k1_ref, 1) + taps(c[5], k1_ref, 2) + b1
-    before = jnp.where(place_ref[0] > 0, gelu(before), 0.0)
-    after = jnp.where(place_ref[1] > 0, gelu(after), 0.0)
+    before = jnp.where(place_ref[0:1, :] > 0, gelu(before), 0.0)
+    after = jnp.where(place_ref[1:2, :] > 0, gelu(after), 0.0)
     for n, (column, d) in enumerate(((before, 0), (after, 2))):
         side_ref[n, 0:groups, :] = column
         both = jnp.concatenate([side_ref[n, 0:pairs, :], side_ref[n, 1 : pairs + 1, :]], axis=1)
@@ -489,10 +508,11 @@
         second(g, hid_ref[g], hid_ref[g + 1])
         return carry
 
-    lax.fori_loop(1, pairs - 1, inner, 0, unroll=5)
+    lax.fori_loop(1, pairs - 1, inner, 0, unroll=True)
     parts = out_sem.shape[0]
     part = devices // parts
     copies = []
+    pos_copy.wait()
     for q in range(parts):
 
         def pick(d, carry):
@@ -516,83 +536,109 @@
     return pl.pallas_call(
         outer_kernel,
         out_shape=jax.ShapeDtypeStruct((devices, CAP * chans, cols), BF16),
-        in_specs=[smem(), smem()] + [vmem()] * 9,
+        in_specs=[vmem()] * 11,
         out_specs=hbm(),
         scratch_shapes=[
             pltpu.VMEM((6, pairs + 8, lanes), F32),
             pltpu.VMEM((2, pairs + 8, lanes), F32),
             pltpu.VMEM((2 * pairs, chans, cols), BF16),
             pltpu.VMEM((devices, CAP * chans, cols), BF16),
+            pltpu.SMEM(positions.shape, jnp.int32),
             pltpu.SemaphoreType.DMA((8,)),
+            pltpu.SemaphoreType.DMA,
         ],
         compiler_params=params(),
     )(positions, place, field, hidden, sides, above, below, k1, b1, k2, b2)
 
 
-def backward_kernel(slot_ref, code_ref, got_hbm, table_ref, out_ref, got_ref, rows_ref, got_sem):
-    blocks, width = out_ref.shape
-    seg = table_ref.shape[1]
+def backward_kernel(
+    return_hbm,
+    got_hbm,
+    table_ref,
+    out_hbm,
+    return_ref,
+    got_ref,
+    rows_ref,
+    out_ref,
+    return_sem,
+    got_sem,
+    out_sem,
+):
+    blocks, width = out_hbm.shape
+    tables, seg, _ = table_ref.shape
     chans = width // seg
-    parts = got_sem.shape[0]
+    devices = got_ref.shape[0]
+    loads = got_sem.shape[0]
+    load = devices // loads
+    parts = out_sem.shape[0]
     part = blocks // parts
-
-    def fetch(q):
-        def one(b, carry):
+    copies = [pltpu.make_async_copy(return_hbm, return_ref, return_sem)]
+    for q in range(loads):
+        piece = pl.ds(q * load, load)
+        copies.append(
+            pltpu.make_async_copy(got_hbm.at[piece], got_ref.at[piece], got_sem.at[q])
+        )
+    for copy in copies:
+        copy.start()
+    for copy in copies:
+        copy.wait()
+
+    out_copies = []
+
+    def finish(q):
+        piece = pl.ds(q * part, part)
+        for c in range(chans):
+            out_ref[piece, c * seg : (c + 1) * seg] = rows_ref[
+                q, c * part : (c + 1) * part, :
+            ].astype(BF16)
+        out_copies.append(
+            pltpu.make_async_copy(out_ref.at[piece], out_hbm.at[piece], out_sem.at[q])
+        )
+        out_copies[-1].start()
+
+    for q in range(parts):
+        if q > 0:
+            finish(q - 1)
+        for n in range(part):
+            states, weights = [], []
             for t in range(2):
-                slot = slot_ref[b, t]
-                at = pl.multiple_of(lax.rem(slot, CAP) * chans, chans)
-                pltpu.make_async_copy(
-                    got_hbm.at[lax.div(slot, CAP), pl.ds(at, chans), :],
-                    got_ref.at[q, 2 * (b - q * part) + t],
-                    got_sem.at[q],
-                ).start()
-            return carry
-
-        lax.fori_loop(q * part, (q + 1) * part, one, 0, unroll=4)
-
-    def arrived(q):
-        pltpu.make_async_copy(
-            got_hbm.at[pl.ds(0, 2 * part), pl.ds(0, chans), :], got_ref.at[q], got_sem.at[q]
-        ).wait()
-
-    for q in range(parts):
-        fetch(q)
-    for q in range(parts):
-        arrived(q)
-
-        def one_block(n, carry):
-            b = q * part + n
-            state = jnp.concatenate([got_ref[q, 2 * n], got_ref[q, 2 * n + 1]], axis=1)
-            weights = jnp.concatenate(
-                [table_ref[code_back(code_ref[b, t])] for t in range(2)], axis=1
+                code = return_ref[t, q * part + n]
+                slot = code >> log2(tables)
+                at = pl.multiple_of((slot & 1) * chans, chans)
+                states.append(got_ref[slot >> 1, pl.ds(at, chans), :])
+                weights.append(table_ref[code & (tables - 1)])
+            rows_ref[q, pl.ds(n, chans, stride=part), :] = lax.dot_general(
+                jnp.concatenate(states, axis=1),
+                jnp.concatenate(weights, axis=1),
+                NT,
+                preferred_element_type=F32,
             )
-            rows_ref[pl.ds(b, chans, stride=blocks), :] = lax.dot_general(
-                state, weights, NT, preferred_element_type=F32
-            )
-            return carry
-
-        lax.fori_loop(0, part, one_block, 0, unroll=16)
-    for c in range(chans):
-        out_ref[:, c * seg : (c + 1) * seg] = rows_ref[c * blocks : (c + 1) * blocks, :].astype(BF16)
-
-
-def backward_remap(slots, codes, got, back_table):
-    blocks = slots.shape[0]
+    finish(parts - 1)
+    for copy in out_copies:
+        copy.wait()
+
+
+def backward_remap(returns, got, back_table):
+    blocks = returns.shape[1]
     chans = got.shape[1] // CAP
     seg = got.shape[2]
     parts = 4
     return pl.pallas_call(
         backward_kernel,
         out_shape=jax.ShapeDtypeStruct((blocks, chans * seg), BF16),
-        in_specs=[smem(), smem(), hbm(), vmem()],
-        out_specs=vmem(),
+        in_specs=[hbm(), hbm(), vmem()],
+        out_specs=hbm(),
         scratch_shapes=[
-            pltpu.VMEM((parts, 2 * blocks // parts, chans, seg), BF16),
-            pltpu.VMEM((chans * blocks, seg), F32),
+            pltpu.SMEM(returns.shape, jnp.int32),
+            pltpu.VMEM(got.shape, BF16),
+            pltpu.VMEM((parts, chans * blocks // parts, seg), F32),
+            pltpu.VMEM((blocks, chans * seg), BF16),
+            pltpu.SemaphoreType.DMA,
+            pltpu.SemaphoreType.DMA((8,)),
             pltpu.SemaphoreType.DMA((parts,)),
         ],
         compiler_params=params(),
-    )(slots, codes, got, back_table)
+    )(returns, got, back_table)
 
 
 def row_pair_weights(kernel):
@@ -625,8 +671,9 @@
     n_fx = lax.axis_size("fx")
     n_fy = lax.axis_size("fy")
     hblocks = 64
-    codes = code_of(dest_dev, dest_pos, fwd_id, back_id)
-    send, slots = forward_remap(codes, ll_blocks, fwd_table, n_fx * n_fy, n_fy)
+    send, returns = forward_remap(
+        dest_dev, dest_pos, fwd_id, back_id, ll_blocks, fwd_table, n_fx * n_fy, n_fy
+    )
     field, up, down, sides, positions = sum_field(exchange(send), hblocks)
     above = lax.ppermute(down, "fx", [(i, (i + 1) % n_fx) for i in range(n_fx)])
     below = lax.ppermute(up, "fx", [((i + 1) % n_fx, i) for i in range(n_fx)])
@@ -634,13 +681,14 @@
     b1 = jnp.tile(bias_one, 2)[None]
     turned, hidden = inner_hidden(field, sides, k1, b1)
     j = lax.axis_index("fy")
-    place = jnp.stack([(j > 0).astype(jnp.int32), (j < n_fy - 1).astype(jnp.int32)])
+    place = jnp.stack([j > 0, j < n_fy - 1]).astype(jnp.int32)[:, None]
+    place = jnp.broadcast_to(place, (2, 128))
     k2 = row_pair_weights(kernel_two)
     b2 = jnp.tile(bias_two, 2)[None]
     send_back = outer_state(
         positions, place, turned, hidden, sides, above, below, k1, b1, k2, b2
     )
-    return backward_remap(slots, codes, exchange(send_back), back_table)
+    return backward_remap(returns, exchange(send_back), back_table)
 
 
 def solution(mesh):

time: 161 us -> 149 us (0.925)
  Pallas kernels: 28.6 us -> 18.7 us
  local copies, waits for them, and re-layouts: 4.58 us -> 1.74 us
    pallas_call x1, Pallas kernels: 6.24 us -> 3.14 us  [outer_state(): pl.pallas_call(outer_kernel, out_shape=jax.ShapeDtypeStruct((devices, CAP...]
    pallas_call x1, Pallas kernels: 6.2 us -> 3.12 us  [backward_remap(): pl.pallas_call(backward_kernel, out_shape=jax.ShapeDtypeStruct((blocks, c...]
    unnamed x14 -> x12, local copies, waits for them, and re-layouts: 2.85 us -> 0.04 us
    pallas_call x1, Pallas kernels: 7.79 us -> 5.62 us  [forward_remap(): pl.pallas_call(functools.partial(forward_kernel, n_fy), out_shape=(jax.Sh...]
where the time goes in v2:
time: 149 us
  blocking collectives  61.2 us (41%)
  waiting for transfers between devices  54 us (36%)
  Pallas kernels  18.7 us (13%)
  starting transfers between devices  12.6 us (8%)
  local copies, waits for them, and re-layouts  1.74 us (1%)
    all_to_all x1, blocking collectives, exchange(): return lax.all_to_all(buffer, AXES, split_axis=0, concat_axis=0, tiled=True)  61.2 us
    all_to_all x1, waiting for transfers between devices, exchange(): return lax.all_to_all(buffer, AXES, split_axis=0, concat_axis=0, tiled=True)  54 us
    all_to_all x1, starting transfers between devices, exchange(): return lax.all_to_all(buffer, AXES, split_axis=0, concat_axis=0, tiled=True)  10.9 us
    pallas_call x1, Pallas kernels, forward_remap(): pl.pallas_call(functools.partial(forward_kernel, n_fy), out_shape=(jax.Sh...  5.62 us
    pallas_call x1, Pallas kernels, sum_field(): pl.pallas_call(sum_kernel, out_shape=(jax.ShapeDtypeStruct((hblocks, chan...  4.61 us
    pallas_call x1, Pallas kernels, outer_state(): pl.pallas_call(outer_kernel, out_shape=jax.ShapeDtypeStruct((devices, CAP...  3.14 us
    pallas_call x1, Pallas kernels, backward_remap(): pl.pallas_call(backward_kernel, out_shape=jax.ShapeDtypeStruct((blocks, c...  3.12 us
  transfers between devices with their start and end apart: 3, of which 1 were waited for; matrix products, arithmetic and copies ran while one was open for 1% of the time, Pallas kernels for 2%

profile of v2, /device:TPU:6, one launch (start us, length us, event | category | flops | bytes accessed | tf_op | source)
XLA Modules:
  0.0 148.7 jit_solution(288511554053174376)
XLA Ops:
  0.0 5.6 %shard_map.109 = (bf16[128,136,128]{2,1,0:T(8,128)(2,1)}, s32[2,64]{1,0:T(2,128)}) custom-call(s32[2,64]{1,0:T(2,128)} %bitcast.18, s32[2,64]{1,0:T(2,128)} %bitcast.19, s32[2,64]{1,0:T(2,128)} %bitcast.20, s32[2,64]{1,0:T(2,128)} %bitcast.21, bf16[64,8192]{1,0:T(8,128)(2,1)} %x_hbm.1, bf16[64,128,128]{2,1,0:T(8,128)(2,1)} %table_hbm.1), custom_call_target="tpu_custom_call" | custom-call | tf_op jit(solution)/shard_map/pallas_call | solution.py:179
  5.6 0.0 copy-start.2
  5.6 0.0 copy-start.4
  5.7 0.0 copy-start.3
  5.7 10.9 %all-to-all-start = ((bf16[128,136,128]{2,1,0:T(8,128)(2,1)}), bf16[128,136,128]{2,1,0:T(8,128)(2,1)}, u32[]{:S(2)}, u32[]{:S(2)}) async-start(bf16[128,136,128]{2,1,0:T(8,128)(2,1)} %get-tuple-element.15), calls=%async_computation | async-start | bytes 8912896 | tf_op jit(solution)/shard_map/all_to_all | solution.py:655
  16.6 0.0 copy-start.5
  16.6 0.0 copy-done.2
  16.6 0.1 pad_bitcast_fusion.3
  16.7 0.1 maximum_bitcast_fusion
  16.8 0.4 copy.12
  17.2 0.3 reshape.25.k1_ref
  17.4 0.0 copy-done.4
  17.5 0.1 broadcast_in_dim_tile.6.b1_ref
  17.5 0.0 copy-done.3
  17.5 0.1 pad_bitcast_fusion.1
  17.6 0.1 maximum_bitcast_fusion.1
  17.7 0.4 copy.13
  18.1 0.3 reshape.26.k2_ref
  18.4 0.0 copy-done.5
  18.4 0.1 broadcast_in_dim_tile.7.b2_ref
  18.5 0.1 add_convert_fusion
  18.6 54.0 %all-to-all-done.got_hbm = bf16[128,136,128]{2,1,0:T(8,128)(2,1)} async-done(((bf16[128,136,128]{2,1,0:T(8,128)(2,1)}), bf16[128,136,128]{2,1,0:T(8,128)(2,1)}, u32[]{:S(2)}, u32[]{:S(2)}) %all-to-all-start) | async-done | bytes 4456480 | tf_op jit(solution)/shard_map/all_to_all | solution.py:655
  72.6 4.6 %shard_map.110 = (bf16[64,64,128]{2,1,0:T(8,128)(2,1)S(1)}, bf16[144,128]{1,0:T(8,128)(2,1)S(1)}, bf16[144,128]{1,0:T(8,128)(2,1)S(1)}, f32[4,32,128]{2,1,0:T(8,128)S(1)}, s32[8,128]{1,0:T(8,128)S(1)}) custom-call(bf16[128,136,128]{2,1,0:T(8,128)(2,1)} %all-to-all-done.got_hbm), custom_call_target="tpu_custom_call" | custom-call | tf_op jit(solution)/shard_map/pallas_call | solution.py:327
  77.2 0.0 collective-permute-start
  77.2 1.7 %collective-permute-start.1 = (bf16[144,128]{1,0:T(8,128)(2,1)S(1)}, bf16[144,128]{1,0:T(8,128)(2,1)S(1)}, u32[]{:S(2)}, u32[]{:S(2)}) collective-permute-start(bf16[144,128]{1,0:T(8,128)(2,1)S(1)} %get-tuple-element.22), channel_id=1, source_target_pairs={{16,0},{32,16},{48,32},{64,48},{80,64},{96,80},{112,96},{0,112},{1... | collective-permute-start | bytes 110600 | tf_op jit(solution)/shard_map/ppermute | solution.py:679
  78.9 2.2 %shard_map.111 = (bf16[32,128,128]{2,1,0:T(8,128)(2,1)S(1)}, bf16[32,128,128]{2,1,0:T(8,128)(2,1)S(1)}) custom-call(bf16[64,64,128]{2,1,0:T(8,128)(2,1)S(1)} %get-tuple-element.17.field_ref, f32[4,32,128]{2,1,0:T(8,128)S(1)} %get-tuple-element.18.side_ref.sides_ref, bf16[256,384]{1,0:T(8,128)(2,1)S(1)} %reshape.25.k1_ref, ...), custom_call_target="tpu_custom_call" | custom-call | flops 603979776 | bytes 4194304 | tf_op jit(solution)/shard_map/pallas_call | solution.py:410
  81.2 0.0 collective-permute-done.above_ref
  81.2 0.0 collective-permute-done.1.below_ref
  81.2 0.1 broadcast_in_dim.2.place_ref
  81.3 3.1 %shard_map.112 = bf16[128,128,128]{2,1,0:T(8,128)(2,1)S(1)} custom-call(s32[8,128]{1,0:T(8,128)S(1)} %get-tuple-element.16.pos_hbm, s32[2,128]{1,0:T(2,128)S(1)} %broadcast_in_dim.2.place_ref, bf16[32,128,128]{2,1,0:T(8,128)(2,1)S(1)} %get-tuple-element.19.field_ref, bf16[32,128,128]{2,1,0:T(8,128)(2,1)S(1)} %get-tuple-element.20.hid_ref, ...), custom_call_target="tpu_custom_call" | custom-call | tf_op jit(solution)/shard_map/pallas_call | solution.py:536
  84.4 0.0 copy-start
  84.4 0.0 copy-start.1
  84.4 61.2 %all_to_all.10.got_hbm = bf16[128,128,128]{2,1,0:T(8,128)(2,1)S(1)} all-to-all(bf16[128,128,128]{2,1,0:T(8,128)(2,1)S(1)} %shard_map.112), channel_id=1, replica_groups=mesh['fx'=8,'fy'=16] {'fx','fy'}, dimensions={0} | all-to-all | bytes 8388608 | tf_op jit(solution)/shard_map/all_to_all | solution.py:655
  145.6 0.0 copy-done
  145.6 0.0 copy-done.1
  145.6 3.1 %shard_map.113 = bf16[64,8192]{1,0:T(8,128)(2,1)} custom-call(s32[2,64]{1,0:T(2,128)S(1)} %copy-done.1, bf16[128,128,128]{2,1,0:T(8,128)(2,1)S(1)} %all_to_all.10.got_hbm, bf16[64,128,128]{2,1,0:T(8,128)(2,1)S(1)} %copy-done), custom_call_target="tpu_custom_call" | custom-call | tf_op jit(solution)/shard_map/pallas_call | solution.py:626
  (2 shorter events, 0.0 us)
Async XLA Ops:
  5.6 11.0 %copy-start.2 = (bf16[3,3,64,64]{3,2,1,0:T(8,128)(2,1)S(1)}, bf16[3,3,64,64]{3,2,1,0:T(8,128)(2,1)}, u32[]{:S(2)}) copy-start(bf16[3,3,64,64]{3,2,1,0:T(8,128)(2,1)} %param.18) | copy-start | bytes 221188
  5.6 11.8 %copy-start.4 = (f32[64]{0:T(128)S(1)}, f32[64]{0:T(128)}, u32[]{:S(2)}) copy-start(f32[64]{0:T(128)} %param.19) | copy-start | bytes 772
  5.7 11.9 %copy-start.3 = (bf16[3,3,64,64]{3,2,1,0:T(8,128)(2,1)S(1)}, bf16[3,3,64,64]{3,2,1,0:T(8,128)(2,1)}, u32[]{:S(2)}) copy-start(bf16[3,3,64,64]{3,2,1,0:T(8,128)(2,1)} %param.20) | copy-start | bytes 221188
  5.7 66.9 %all-to-all-start = ((bf16[128,136,128]{2,1,0:T(8,128)(2,1)}), bf16[128,136,128]{2,1,0:T(8,128)(2,1)}, u32[]{:S(2)}, u32[]{:S(2)}) async-start(bf16[128,136,128]{2,1,0:T(8,128)(2,1)} %get-tuple-element.15), calls=%async_computation | async-start | bytes 8912896 | tf_op jit(solution)/shard_map/all_to_all | solution.py:655
  16.6 1.8 %copy-start.5 = (f32[64]{0:T(128)S(1)}, f32[64]{0:T(128)}, u32[]{:S(2)}) copy-start(f32[64]{0:T(128)} %param.21) | copy-start | bytes 772
  77.2 4.0 %collective-permute-start = (bf16[144,128]{1,0:T(8,128)(2,1)S(1)}, bf16[144,128]{1,0:T(8,128)(2,1)S(1)}, u32[]{:S(2)}, u32[]{:S(2)}) collective-permute-start(bf16[144,128]{1,0:T(8,128)(2,1)S(1)} %get-tuple-element.21), channel_id=1, source_target_pairs={{0,16},{16,32},{32,48},{48,64},{64,80},{80,96},{96,112},{112,0},{1... | collective-permute-start | bytes 110600 | tf_op jit(solution)/shard_map/ppermute | solution.py:678
  77.2 4.0 %collective-permute-start.1 = (bf16[144,128]{1,0:T(8,128)(2,1)S(1)}, bf16[144,128]{1,0:T(8,128)(2,1)S(1)}, u32[]{:S(2)}, u32[]{:S(2)}) collective-permute-start(bf16[144,128]{1,0:T(8,128)(2,1)S(1)} %get-tuple-element.22), channel_id=1, source_target_pairs={{16,0},{32,16},{48,32},{64,48},{80,64},{96,80},{112,96},{0,112},{1... | collective-permute-start | bytes 110600 | tf_op jit(solution)/shard_map/ppermute | solution.py:679
  84.4 61.2 %copy-start = (bf16[64,128,128]{2,1,0:T(8,128)(2,1)S(1)}, bf16[64,128,128]{2,1,0:T(8,128)(2,1)}, u32[]{:S(2)}) copy-start(bf16[64,128,128]{2,1,0:T(8,128)(2,1)} %table_ref.1) | copy-start | bytes 6291460
  84.4 61.2 %copy-start.1 = (s32[2,64]{1,0:T(2,128)S(1)}, s32[2,64]{1,0:T(2,128)}, u32[]{:S(2)}) copy-start(s32[2,64]{1,0:T(2,128)} %get-tuple-element.14.return_hbm) | copy-start | bytes 1540

commit v3 on v2

--- a/solution.py
+++ b/solution.py
@@ -13,7 +13,6 @@
 F32 = jnp.float32
 BF16 = jnp.bfloat16
 VMEM_LIMIT = 40 * 1024 * 1024
-FULL_VMEM = 60 * 1024 * 1024
 NT = (((1,), (1,)), ((), ()))
 
 
@@ -29,8 +28,12 @@
     return pl.BlockSpec(memory_space=pl.ANY)
 
 
-def params(limit=VMEM_LIMIT):
-    return pltpu.CompilerParams(vmem_limit_bytes=limit)
+def params():
+    return pltpu.CompilerParams(vmem_limit_bytes=VMEM_LIMIT)
+
+
+def in_hbm(x):
+    return pltpu.with_memory_space_constraint(x, pltpu.HBM)
 
 
 def log2(count):
@@ -40,6 +43,18 @@
 
 def lane_iota(shape):
     return lax.broadcasted_iota(jnp.int32, shape, len(shape) - 1)
+
+
+def row_pair_weights(taps_ref, weights_ref):
+    _, columns, chans, _ = taps_ref.shape
+    none = jnp.zeros((chans, chans), BF16)
+    for q in range(4):
+        for d in range(columns):
+            upper = taps_ref[q, d] if q < 3 else none
+            lower = taps_ref[q - 1, d] if q > 0 else none
+            weights_ref[q * chans : (q + 1) * chans, 2 * d * chans : 2 * (d + 1) * chans] = (
+                jnp.concatenate([upper, lower], axis=1)
+            )
 
 
 def forward_kernel(
@@ -50,8 +65,12 @@
     back_hbm,
     x_hbm,
     table_hbm,
+    k1_hbm,
+    k2_hbm,
     send_ref,
     return_hbm,
+    w1_ref,
+    w2_ref,
     dev_ref,
     pos_ref,
     fwd_ref,
@@ -59,17 +78,15 @@
     return_ref,
     x_ref,
     table_ref,
+    taps_ref,
     rows_ref,
     edge_ref,
-    stage_ref,
     meta_ref,
-    packed_ref,
     count_ref,
     code_sem,
     x_sem,
     table_sem,
-    out_sem,
-    meta_sem,
+    taps_sem,
     return_sem,
 ):
     blocks, width = x_ref.shape
@@ -99,7 +116,11 @@
             ((dev_hbm, dev_ref), (pos_hbm, pos_ref), (fwd_hbm, fwd_ref), (back_hbm, back_ref))
         )
     ]
-    for copy in code_copies + x_copies + table_copies:
+    taps_copies = [
+        pltpu.make_async_copy(source, taps_ref.at[n], taps_sem.at[n])
+        for n, source in enumerate((k1_hbm, k2_hbm))
+    ]
+    for copy in code_copies + x_copies + taps_copies + table_copies:
         copy.start()
 
     def clear(d, carry):
@@ -112,6 +133,9 @@
         copy.wait()
         for c in range(q * wide // seg, (q + 1) * wide // seg):
             rows_ref[c * blocks : (c + 1) * blocks, :] = x_ref[:, c * seg : (c + 1) * seg].astype(F32)
+    for n, (copy, weights_ref) in enumerate(zip(taps_copies, (w1_ref, w2_ref))):
+        copy.wait()
+        row_pair_weights(taps_ref.at[n], weights_ref)
     for q, copy in enumerate(table_copies):
         copy.wait()
 
@@ -139,12 +163,8 @@
             rank = count_ref[dev]
             count_ref[dev] = rank + 1
             return_ref[t, b] = ((dev * CAP + rank) << log2(tables)) + back_ref[t, b]
-            route = 2 * b + t
-            stage_ref[route] = product[:, t * seg : (t + 1) * seg].astype(BF16)
             at = pl.multiple_of(rank * chans, chans)
-            pltpu.make_async_copy(
-                stage_ref.at[route], send_ref.at[dev, pl.ds(at, chans), :], out_sem
-            ).start()
+            send_ref[dev, pl.ds(at, chans), :] = product[:, t * seg : (t + 1) * seg].astype(BF16)
             meta_ref[dev, pl.ds(4 + rank, 1), :] = jnp.full((1, seg), pos, F32)
             col = dev & (n_fy - 1)
             mine = (lane >= chans) == (rank == 1)
@@ -160,19 +180,15 @@
         return carry
 
     lax.fori_loop(0, blocks, one_block, 0, unroll=True)
-    packed_ref[...] = meta_ref[0:devices].astype(BF16)
-    meta_copy = pltpu.make_async_copy(
-        packed_ref, send_ref.at[:, pl.ds(CAP * chans, META), :], meta_sem
-    )
-    meta_copy.start()
+    send_ref[:, CAP * chans :, :] = meta_ref[0:devices].astype(BF16)
     return_copy = pltpu.make_async_copy(return_ref, return_hbm, return_sem)
     return_copy.start()
-    pltpu.make_async_copy(stage_ref, send_ref.at[:, pl.ds(0, chans), :], out_sem).wait()
-    meta_copy.wait()
     return_copy.wait()
 
 
-def forward_remap(dest_dev, dest_pos, fwd_id, back_id, ll_blocks, fwd_table, devices, n_fy):
+def forward_remap(
+    dest_dev, dest_pos, fwd_id, back_id, ll_blocks, fwd_table, k1, k2, devices, n_fy
+):
     blocks, width = ll_blocks.shape
     tables, seg, _ = fwd_table.shape
     chans = width // seg
@@ -181,9 +197,11 @@
         out_shape=(
             jax.ShapeDtypeStruct((devices, CAP * chans + META, seg), BF16),
             jax.ShapeDtypeStruct((2, blocks), jnp.int32),
+            jax.ShapeDtypeStruct((4 * chans, 6 * chans), BF16),
+            jax.ShapeDtypeStruct((4 * chans, 6 * chans), BF16),
         ),
-        in_specs=[hbm()] * 6,
-        out_specs=(hbm(), hbm()),
+        in_specs=[hbm()] * 8,
+        out_specs=(vmem(), hbm(), vmem(), vmem()),
         scratch_shapes=[
             pltpu.SMEM((2, blocks), jnp.int32),
             pltpu.SMEM((2, blocks), jnp.int32),
@@ -192,68 +210,41 @@
             pltpu.SMEM((2, blocks), jnp.int32),
             pltpu.VMEM((blocks, width), BF16),
             pltpu.VMEM((tables, seg, seg), BF16),
+            pltpu.VMEM((2,) + k1.shape, BF16),
             pltpu.VMEM((chans * blocks, seg), F32),
             pltpu.VMEM((tables, 4, seg), F32),
-            pltpu.VMEM((2 * blocks, chans, seg), BF16),
             pltpu.VMEM((devices + 1, META, seg), F32),
-            pltpu.VMEM((devices, META, seg), BF16),
             pltpu.SMEM((devices,), jnp.int32),
             pltpu.SemaphoreType.DMA((4,)),
             pltpu.SemaphoreType.DMA((4,)),
             pltpu.SemaphoreType.DMA((8,)),
-            pltpu.SemaphoreType.DMA,
-            pltpu.SemaphoreType.DMA,
+            pltpu.SemaphoreType.DMA((2,)),
             pltpu.SemaphoreType.DMA,
         ],
-        compiler_params=params(FULL_VMEM),
-    )(dest_dev.T, dest_pos.T, fwd_id.T, back_id.T, ll_blocks, fwd_table)
+        compiler_params=params(),
+    )(
+        *(in_hbm(route.T) for route in (dest_dev, dest_pos, fwd_id, back_id)),
+        *(in_hbm(x) for x in (ll_blocks, fwd_table, k1, k2)),
+    )
 
 
 def sum_kernel(
-    got_hbm,
+    got_ref,
     field_ref,
     up_ref,
     down_ref,
     side_ref,
     pos_ref,
-    got_ref,
-    meta_ref,
     rows_ref,
     sum_ref,
     spot_ref,
-    meta_sem,
-    got_sem,
     spot_sem,
 ):
     devices, _, cols = got_ref.shape
     hblocks, chans, _ = field_ref.shape
     pairs = hblocks // 2
     lanes = 2 * chans
-    parts = got_sem.shape[0]
-    part = devices // parts
-    meta_copy = pltpu.make_async_copy(
-        got_hbm.at[:, pl.ds(CAP * chans, META), :], meta_ref, meta_sem
-    )
-    meta_copy.start()
-    copies = [
-        pltpu.make_async_copy(
-            got_hbm.at[pl.ds(q * part, part), pl.ds(0, CAP * chans), :],
-            got_ref.at[pl.ds(q * part, part)],
-            got_sem.at[q],
-        )
-        for q in range(parts)
-    ]
-    for copy in copies:
-        copy.start()
-
-    def clear(r, carry):
-        for rank in range(CAP):
-            sum_ref[rank, r] = jnp.zeros((chans, cols), F32)
-        return carry
-
-    lax.fori_loop(0, hblocks, clear, 0, unroll=4)
-    meta_copy.wait()
-    rows_ref[...] = meta_ref[...].reshape(devices * META, lanes).astype(F32)
+    rows_ref[...] = got_ref[:, CAP * chans :, :].reshape(devices * META, lanes).astype(F32)
 
     def meta_row(n):
         return rows_ref[pl.ds(n, devices, stride=META), :]
@@ -270,6 +261,13 @@
     pos_ref[...] = spots
     spot_copy = pltpu.make_async_copy(pos_ref, spot_ref, spot_sem)
     spot_copy.start()
+
+    def clear(r, carry):
+        for rank in range(CAP):
+            sum_ref[rank, r] = jnp.zeros((chans, cols), F32)
+        return carry
+
+    lax.fori_loop(0, hblocks, clear, 0, unroll=4)
     block = lax.broadcasted_iota(jnp.int32, (pairs, devices), 0)
     low = lane_iota((pairs, lanes)) < chans
     for side in range(2):
@@ -287,18 +285,16 @@
         side_ref[2 * side] = jnp.where(low, even, pltpu.roll(odd, chans, axis=1))
         side_ref[2 * side + 1] = jnp.where(low, pltpu.roll(even, chans, axis=1), odd)
     spot_copy.wait()
-    for q, copy in enumerate(copies):
-        copy.wait()
-
-        def add(d, carry):
-            for rank in range(CAP):
-                pos = spot_ref[rank, d]
-                row = jnp.where(pos < 0, hblocks, pos)
-                block = got_ref[d, rank * chans : (rank + 1) * chans, :]
-                sum_ref[rank, row] = sum_ref[rank, row] + block.astype(F32)
-            return carry
-
-        lax.fori_loop(q * part, (q + 1) * part, add, 0, unroll=4)
+
+    def add(d, carry):
+        for rank in range(CAP):
+            pos = spot_ref[rank, d]
+            row = jnp.where(pos < 0, hblocks, pos)
+            block = got_ref[d, rank * chans : (rank + 1) * chans, :]
+            sum_ref[rank, row] = sum_ref[rank, row] + block.astype(F32)
+        return carry
+
+    lax.fori_loop(0, devices, add, 0, unroll=16)
 
     def total_of(r):
         return sum_ref[0, r] + sum_ref[1, r]
@@ -333,16 +329,12 @@
             jax.ShapeDtypeStruct((4, pairs, 2 * chans), F32),
             jax.ShapeDtypeStruct((8, devices), jnp.int32),
         ),
-        in_specs=[hbm()],
+        in_specs=[vmem()],
         out_specs=(vmem(),) * 5,
         scratch_shapes=[
-            pltpu.VMEM((devices, CAP * chans, cols), BF16),
-            pltpu.VMEM((devices, META, cols), BF16),
             pltpu.VMEM((devices * META, cols), F32),
             pltpu.VMEM((CAP, hblocks + 1, chans, cols), F32),
             pltpu.SMEM((8, devices), jnp.int32),
-            pltpu.SemaphoreType.DMA,
-            pltpu.SemaphoreType.DMA((8,)),
             pltpu.SemaphoreType.DMA,
         ],
         compiler_params=params(),
@@ -370,8 +362,8 @@
     return product[:, lanes : 2 * lanes] + ahead + behind + bias
 
 
-def round_to_bf16(x):
-    return x.astype(BF16).astype(F32)
+def twice(bias_ref):
+    return jnp.concatenate([bias_ref[...], bias_ref[...]], axis=1)
 
 
 def inner_kernel(field_ref, side_ref, k1_ref, b1_ref, turned_ref, hid_ref, halo_ref):
@@ -383,7 +375,7 @@
         return carry
 
     lax.fori_loop(0, pairs, turn, 0, unroll=4)
-    b1 = b1_ref[...]
+    b1 = twice(b1_ref)
     for n, (k, d) in enumerate(((1, 0), (2, 2))):
         both = jnp.concatenate([side_ref[k, 0 : pairs - 1, :], side_ref[k, 1:pairs, :]], axis=1)
         halo_ref[n, 1:pairs, :] = taps(both.astype(BF16), k1_ref, d)
@@ -436,9 +428,7 @@
     side_ref,
     halo_ref,
     state_ref,
-    stage_ref,
     pos_ref,
-    out_sem,
     pos_sem,
 ):
     pos_copy = pltpu.make_async_copy(pos_hbm, pos_ref, pos_sem)
@@ -476,8 +466,8 @@
             [side_ref[k, 0:groups, :], side_ref[k, 1 : groups + 1, :]], axis=1
         ).astype(BF16)
 
-    b1 = b1_ref[...]
-    b2 = b2_ref[...]
+    b1 = twice(b1_ref)
+    b2 = twice(b2_ref)
     c = [paired(k) for k in range(6)]
     left = taps(c[1], k1_ref, 0)
     right = taps(c[4], k1_ref, 2)
@@ -509,24 +499,15 @@
         return carry
 
     lax.fori_loop(1, pairs - 1, inner, 0, unroll=True)
-    parts = out_sem.shape[0]
-    part = devices // parts
-    copies = []
     pos_copy.wait()
-    for q in range(parts):
-
-        def pick(d, carry):
-            for rank in range(CAP):
-                pos = jnp.maximum(pos_ref[rank, d], 0)
-                stage_ref[d, rank * chans : (rank + 1) * chans, :] = state_ref[pos]
-            return carry
-
-        lax.fori_loop(q * part, (q + 1) * part, pick, 0, unroll=4)
-        piece = pl.ds(q * part, part)
-        copies.append(pltpu.make_async_copy(stage_ref.at[piece], send_ref.at[piece], out_sem.at[q]))
-        copies[-1].start()
-    for copy in copies:
-        copy.wait()
+
+    def pick(d, carry):
+        for rank in range(CAP):
+            pos = jnp.maximum(pos_ref[rank, d], 0)
+            send_ref[d, rank * chans : (rank + 1) * chans, :] = state_ref[pos]
+        return carry
+
+    lax.fori_loop(0, devices, pick, 0, unroll=16)
 
 
 def outer_state(positions, place, field, hidden, sides, above, below, k1, b1, k2, b2):
@@ -537,14 +518,12 @@
         outer_kernel,
         out_shape=jax.ShapeDtypeStruct((devices, CAP * chans, cols), BF16),
         in_specs=[vmem()] * 11,
-        out_specs=hbm(),
+        out_specs=vmem(),
         scratch_shapes=[
             pltpu.VMEM((6, pairs + 8, lanes), F32),
             pltpu.VMEM((2, pairs + 8, lanes), F32),
             pltpu.VMEM((2 * pairs, chans, cols), BF16),
-            pltpu.VMEM((devices, CAP * chans, cols), BF16),
             pltpu.SMEM(positions.shape, jnp.int32),
-            pltpu.SemaphoreType.DMA((8,)),
             pltpu.SemaphoreType.DMA,
         ],
         compiler_params=params(),
@@ -553,36 +532,23 @@
 
 def backward_kernel(
     return_hbm,
-    got_hbm,
+    got_ref,
     table_ref,
     out_hbm,
     return_ref,
-    got_ref,
     rows_ref,
     out_ref,
     return_sem,
-    got_sem,
     out_sem,
 ):
     blocks, width = out_hbm.shape
     tables, seg, _ = table_ref.shape
     chans = width // seg
-    devices = got_ref.shape[0]
-    loads = got_sem.shape[0]
-    load = devices // loads
     parts = out_sem.shape[0]
     part = blocks // parts
-    copies = [pltpu.make_async_copy(return_hbm, return_ref, return_sem)]
-    for q in range(loads):
-        piece = pl.ds(q * load, load)
-        copies.append(
-            pltpu.make_async_copy(got_hbm.at[piece], got_ref.at[piece], got_sem.at[q])
-        )
-    for copy in copies:
-        copy.start()
-    for copy in copies:
-        copy.wait()
-
+    return_copy = pltpu.make_async_copy(return_hbm, return_ref, return_sem)
+    return_copy.start()
+    return_copy.wait()
     out_copies = []
 
     def finish(q):
@@ -626,29 +592,17 @@
     return pl.pallas_call(
         backward_kernel,
         out_shape=jax.ShapeDtypeStruct((blocks, chans * seg), BF16),
-        in_specs=[hbm(), hbm(), vmem()],
+        in_specs=[hbm(), vmem(), vmem()],
         out_specs=hbm(),
         scratch_shapes=[
             pltpu.SMEM(returns.shape, jnp.int32),
-            pltpu.VMEM(got.shape, BF16),
             pltpu.VMEM((parts, chans * blocks // parts, seg), F32),
             pltpu.VMEM((blocks, chans * seg), BF16),
             pltpu.SemaphoreType.DMA,
-            pltpu.SemaphoreType.DMA((8,)),
             pltpu.SemaphoreType.DMA((parts,)),
         ],
         compiler_params=params(),
     )(returns, got, back_table)
-
-
-def row_pair_weights(kernel):
-    none = jnp.zeros((1,) + kernel.shape[1:], kernel.dtype)
-    upper = jnp.concatenate([kernel, none], axis=0)
-    lower = jnp.concatenate([none, kernel], axis=0)
-    both = jnp.stack([upper, lower], axis=3)
-    both = both.transpose(0, 2, 1, 3, 4)
-    chans = kernel.shape[2]
-    return both.reshape(4 * chans, 3 * 2 * kernel.shape[3])
 
 
 def exchange(buffer):
@@ -671,22 +625,29 @@
     n_fx = lax.axis_size("fx")
     n_fy = lax.axis_size("fy")
     hblocks = 64
-    send, returns = forward_remap(
-        dest_dev, dest_pos, fwd_id, back_id, ll_blocks, fwd_table, n_fx * n_fy, n_fy
+    j = lax.axis_index("fy")
+    place = jnp.stack([j > 0, j < n_fy - 1]).astype(jnp.int32)[:, None]
+    place = jnp.broadcast_to(place, (2, 128))
+    send, returns, w1, w2 = forward_remap(
+        dest_dev,
+        dest_pos,
+        fwd_id,
+        back_id,
+        ll_blocks,
+        fwd_table,
+        kernel_one,
+        kernel_two,
+        n_fx * n_fy,
+        n_fy,
     )
+    send, place = lax.optimization_barrier((send, place))
+    b1, b2 = bias_one[None], bias_two[None]
     field, up, down, sides, positions = sum_field(exchange(send), hblocks)
     above = lax.ppermute(down, "fx", [(i, (i + 1) % n_fx) for i in range(n_fx)])
     below = lax.ppermute(up, "fx", [((i + 1) % n_fx, i) for i in range(n_fx)])
-    k1 = row_pair_weights(kernel_one)
-    b1 = jnp.tile(bias_one, 2)[None]
-    turned, hidden = inner_hidden(field, sides, k1, b1)
-    j = lax.axis_index("fy")
-    place = jnp.stack([j > 0, j < n_fy - 1]).astype(jnp.int32)[:, None]
-    place = jnp.broadcast_to(place, (2, 128))
-    k2 = row_pair_weights(kernel_two)
-    b2 = jnp.tile(bias_two, 2)[None]
+    turned, hidden = inner_hidden(field, sides, w1, b1)
     send_back = outer_state(
-        positions, place, turned, hidden, sides, above, below, k1, b1, k2, b2
+        positions, place, turned, hidden, sides, above, below, w1, b1, w2, b2
     )
     return backward_remap(returns, exchange(send_back), back_table)
 

time: 149 us -> 146 us (0.980)
  blocking collectives: 61.2 us -> 127 us
  waiting for transfers between devices: 54 us -> 0.01 us
  starting transfers between devices: 12.6 us -> 1.75 us
  Pallas kernels: 18.7 us -> 16.7 us
  local copies, waits for them, and re-layouts: 1.74 us -> 0.08 us
    all_to_all x1 -> x2, blocking collectives: 61.2 us -> 127 us  [exchange(): return lax.all_to_all(buffer, AXES, split_axis=0, concat_axis=0, tiled=True)]
    all_to_all x1 -> x0, waiting for transfers between devices: 54 us -> none  [exchange(): return lax.all_to_all(buffer, AXES, split_axis=0, concat_axis=0, tiled=True)]
    all_to_all x1 -> x0, starting transfers between devices: 10.9 us -> none  [exchange(): return lax.all_to_all(buffer, AXES, split_axis=0, concat_axis=0, tiled=True)]
    pallas_call x1, Pallas kernels: 4.61 us -> 2.75 us  [sum_field(): pl.pallas_call(sum_kernel, out_shape=(jax.ShapeDtypeStruct((hblocks, chan...]
  transfers between devices with their start and end apart: 3 -> 2, of which waited for: 1 -> 0; matrix products, arithmetic and copies ran while one was open for 1% -> 0% of each run, Pallas kernels for 2% -> 2%
where the time goes in v3:
time: 146 us; the launch traced here: 145 us
  blocking collectives  127 us (87%)
  Pallas kernels  16.7 us (11%)
  starting transfers between devices  1.75 us (1%)
    all_to_all x2, blocking collectives, exchange(): return lax.all_to_all(buffer, AXES, split_axis=0, concat_axis=0, tiled=True)  127 us
    pallas_call x1, Pallas kernels, forward_remap(): pl.pallas_call(functools.partial(forward_kernel, n_fy), out_shape=(jax.Sh...  5.82 us
    pallas_call x1, Pallas kernels, backward_remap(): pl.pallas_call(backward_kernel, out_shape=jax.ShapeDtypeStruct((blocks, c...  3.1 us
  transfers between devices with their start and end apart: 2, of which 0 were waited for; matrix products, arithmetic and copies ran while one was open for 0% of the time, Pallas kernels for 2%

profile of v3, /device:TPU:6, one launch (start us, length us, event | category | flops | bytes accessed | tf_op | source)
XLA Modules:
  0.0 145.5 jit_solution(13811400578749884749)
XLA Ops:
  0.0 0.1 add_convert_fusion
  0.1 5.8 %shard_map.109 = (bf16[128,136,128]{2,1,0:T(8,128)(2,1)S(1)}, s32[2,64]{1,0:T(2,128)S(1)}, bf16[256,384]{1,0:T(8,128)(2,1)S(1)}, bf16[256,384]{1,0:T(8,128)(2,1)S(1)}) custom-call(s32[2,64]{1,0:T(2,128)} %bitcast.11, s32[2,64]{1,0:T(2,128)} %bitcast.12, s32[2,64]{1,0:T(2,128)} %bitcast.13, s32[2,64]{1,0:T(2,128)} %bitcast.14, bf16[64,8192]{1,0:T(8,128)(2,1)} %x_hbm.1, ...), custom_call_target="tpu_custom_call" | custom-call | tf_op jit(solution)/shard_map/pallas_call | solution.py:195
  5.9 0.1 broadcast_in_dim.12.place_ref
  6.0 66.8 %all_to_all.10.got_ref = bf16[128,136,128]{2,1,0:T(8,128)(2,1)S(1)} all-to-all(bf16[128,136,128]{2,1,0:T(8,128)(2,1)S(1)} %get-tuple-element.20), channel_id=1, replica_groups=mesh['fx'=8,'fy'=16] {'fx','fy'}, dimensions={0} | all-to-all | bytes 8912896 | tf_op jit(solution)/shard_map/all_to_all | solution.py:609
  72.8 0.0 copy-start.1
  72.8 0.0 copy-start.2
  72.8 2.7 %shard_map.110 = (bf16[64,64,128]{2,1,0:T(8,128)(2,1)S(1)}, bf16[144,128]{1,0:T(8,128)(2,1)S(1)}, bf16[144,128]{1,0:T(8,128)(2,1)S(1)}, f32[4,32,128]{2,1,0:T(8,128)S(1)}, s32[8,128]{1,0:T(8,128)S(1)}) custom-call(bf16[128,136,128]{2,1,0:T(8,128)(2,1)S(1)} %all_to_all.10.got_ref), custom_call_target="tpu_custom_call" | custom-call | tf_op jit(solution)/shard_map/pallas_call | solution.py:323
  75.6 0.0 collective-permute-start
  75.6 1.7 %collective-permute-start.1 = (bf16[144,128]{1,0:T(8,128)(2,1)S(1)}, bf16[144,128]{1,0:T(8,128)(2,1)S(1)}, u32[]{:S(2)}, u32[]{:S(2)}) collective-permute-start(bf16[144,128]{1,0:T(8,128)(2,1)S(1)} %get-tuple-element.29), channel_id=1, source_target_pairs={{16,0},{32,16},{48,32},{64,48},{80,64},{96,80},{112,96},{0,112},{1... | collective-permute-start | bytes 110600 | tf_op jit(solution)/shard_map/ppermute | solution.py:647
  77.3 0.0 copy-done.1
  77.3 2.3 %shard_map.111 = (bf16[32,128,128]{2,1,0:T(8,128)(2,1)S(1)}, bf16[32,128,128]{2,1,0:T(8,128)(2,1)S(1)}) custom-call(bf16[64,64,128]{2,1,0:T(8,128)(2,1)S(1)} %get-tuple-element.23.field_ref, f32[4,32,128]{2,1,0:T(8,128)S(1)} %get-tuple-element.24.side_ref.sides_ref, bf16[256,384]{1,0:T(8,128)(2,1)S(1)} %get-tuple-element.25.k1_ref, f32[1,64]{1,0:T(1,128)S(1)} %bitcast.8), custom_call_target="tpu_custom_call" | custom-call | flops 603979776 | bytes 4194304 | tf_op jit(solution)/shard_map/pallas_call | solution.py:402
  79.7 0.0 collective-permute-done.above_ref
  79.7 0.0 collective-permute-done.1.below_ref
  79.7 0.0 copy-done.2
  79.7 2.7 %shard_map.112 = bf16[128,128,128]{2,1,0:T(8,128)(2,1)S(1)} custom-call(s32[8,128]{1,0:T(8,128)S(1)} %get-tuple-element.21.pos_hbm, s32[2,128]{1,0:T(2,128)S(1)} %broadcast_in_dim.12.place_ref, bf16[32,128,128]{2,1,0:T(8,128)(2,1)S(1)} %get-tuple-element.26.field_ref, bf16[32,128,128]{2,1,0:T(8,128)(2,1)S(1)} %get-tuple-element.27.hid_ref, ...), custom_call_target="tpu_custom_call" | custom-call | tf_op jit(solution)/shard_map/pallas_call | solution.py:517
  82.4 0.0 copy-start
  82.4 60.0 %all_to_all.11.got_ref = bf16[128,128,128]{2,1,0:T(8,128)(2,1)S(1)} all-to-all(bf16[128,128,128]{2,1,0:T(8,128)(2,1)S(1)} %shard_map.112), channel_id=1, replica_groups=mesh['fx'=8,'fy'=16] {'fx','fy'}, dimensions={0} | all-to-all | bytes 8388608 | tf_op jit(solution)/shard_map/all_to_all | solution.py:609
  142.4 0.0 copy-done
  142.4 3.1 %shard_map.113 = bf16[64,8192]{1,0:T(8,128)(2,1)} custom-call(s32[2,64]{1,0:T(2,128)S(1)} %get-tuple-element.18.return_hbm, bf16[128,128,128]{2,1,0:T(8,128)(2,1)S(1)} %all_to_all.11.got_ref, bf16[64,128,128]{2,1,0:T(8,128)(2,1)S(1)} %copy-done), custom_call_target="tpu_custom_call" | custom-call | tf_op jit(solution)/shard_map/pallas_call | solution.py:592
Async XLA Ops:
  72.8 4.5 %copy-start.1 = (f32[64]{0:T(128)S(1)}, f32[64]{0:T(128)}, u32[]{:S(2)}) copy-start(f32[64]{0:T(128)} %param.19) | copy-start | bytes 772
  72.8 6.9 %copy-start.2 = (f32[64]{0:T(128)S(1)}, f32[64]{0:T(128)}, u32[]{:S(2)}) copy-start(f32[64]{0:T(128)} %param.21) | copy-start | bytes 772
  75.6 4.1 %collective-permute-start = (bf16[144,128]{1,0:T(8,128)(2,1)S(1)}, bf16[144,128]{1,0:T(8,128)(2,1)S(1)}, u32[]{:S(2)}, u32[]{:S(2)}) collective-permute-start(bf16[144,128]{1,0:T(8,128)(2,1)S(1)} %get-tuple-element.28), channel_id=1, source_target_pairs={{0,16},{16,32},{32,48},{48,64},{64,80},{80,96},{96,112},{112,0},{1... | collective-permute-start | bytes 110600 | tf_op jit(solution)/shard_map/ppermute | solution.py:646
  75.6 4.1 %collective-permute-start.1 = (bf16[144,128]{1,0:T(8,128)(2,1)S(1)}, bf16[144,128]{1,0:T(8,128)(2,1)S(1)}, u32[]{:S(2)}, u32[]{:S(2)}) collective-permute-start(bf16[144,128]{1,0:T(8,128)(2,1)S(1)} %get-tuple-element.29), channel_id=1, source_target_pairs={{16,0},{32,16},{48,32},{64,48},{80,64},{96,80},{112,96},{0,112},{1... | collective-permute-start | bytes 110600 | tf_op jit(solution)/shard_map/ppermute | solution.py:647
  82.4 60.0 %copy-start = (bf16[64,128,128]{2,1,0:T(8,128)(2,1)S(1)}, bf16[64,128,128]{2,1,0:T(8,128)(2,1)}, u32[]{:S(2)}) copy-start(bf16[64,128,128]{2,1,0:T(8,128)(2,1)} %table_ref.1) | copy-start | bytes 6291460

commit v4 on v3

--- a/solution.py
+++ b/solution.py
@@ -8,6 +8,7 @@
 from jax.sharding import PartitionSpec as P
 
 CAP = 2
+PAD = 8
 META = 8
 AXES = ("fx", "fy")
 F32 = jnp.float32
@@ -96,6 +97,7 @@
     assert n_fy == 1 << log2(n_fy)
     parts = x_sem.shape[0]
     wide = width // parts
+    step = rows_ref.shape[0] // chans
     pieces = table_sem.shape[0]
     deep = tables // pieces
     x_copies = [
@@ -129,10 +131,38 @@
 
     lax.fori_loop(0, devices, clear, 0, unroll=8)
     meta_ref[...] = jnp.zeros_like(meta_ref)
+    for copy in code_copies:
+        copy.wait()
+
+    def plan(b, carry):
+        for t in range(2):
+            dev = dev_ref[t, b]
+            rank = count_ref[dev]
+            count_ref[dev] = rank + 1
+            return_ref[t, b] = ((dev * CAP + rank) << log2(tables)) + back_ref[t, b]
+            pos = (pos_ref[t, b] + 1).astype(F32)
+            meta_ref[pl.ds(dev * META + 4 + rank, 1), :] = jnp.full((1, seg), pos, F32)
+        return carry
+
+    lax.fori_loop(0, blocks, plan, 0, unroll=8)
+    return_copy = pltpu.make_async_copy(return_ref, return_hbm, return_sem)
+    return_copy.start()
+    both = jnp.where(
+        lane_iota((devices, seg)) < chans,
+        meta_ref[pl.ds(4, devices, stride=META), :],
+        meta_ref[pl.ds(5, devices, stride=META), :],
+    )
+    col = lax.broadcasted_iota(jnp.int32, both.shape, 0) & (n_fy - 1)
+    meta_ref[pl.ds(6, devices, stride=META), :] = jnp.where(
+        col > 0, pltpu.roll(both, 1, axis=0), 0.0
+    )
+    meta_ref[pl.ds(7, devices, stride=META), :] = jnp.where(
+        col < n_fy - 1, pltpu.roll(both, devices - 1, axis=0), 0.0
+    )
     for q, copy in enumerate(x_copies):
         copy.wait()
         for c in range(q * wide // seg, (q + 1) * wide // seg):
-            rows_ref[c * blocks : (c + 1) * blocks, :] = x_ref[:, c * seg : (c + 1) * seg].astype(F32)
+            rows_ref[c * step : c * step + blocks, :] = x_ref[:, c * seg : (c + 1) * seg].astype(F32)
     for n, (copy, weights_ref) in enumerate(zip(taps_copies, (w1_ref, w2_ref))):
         copy.wait()
         row_pair_weights(taps_ref.at[n], weights_ref)
@@ -145,44 +175,35 @@
             return carry
 
         lax.fori_loop(q * deep, (q + 1) * deep, edges, 0, unroll=4)
-    for copy in code_copies:
-        copy.wait()
     lane = lane_iota((1, seg))
 
     def one_block(b, carry):
         tables_of = [fwd_ref[t, b] for t in range(2)]
-        x = rows_ref[pl.ds(b, chans, stride=blocks), :].astype(BF16)
+        x = rows_ref[pl.ds(b, chans, stride=step), :].astype(BF16)
         weights = jnp.concatenate([table_ref[n] for n in tables_of], axis=0)
         product = lax.dot_general(x, weights, NT, preferred_element_type=F32)
         tips = jnp.concatenate([edge_ref[n] for n in tables_of], axis=0).astype(BF16)
         ends = lax.dot_general(tips, x, NT, preferred_element_type=F32)
         ends = jnp.concatenate([ends, ends], axis=1)
         for t in range(2):
-            dev = dev_ref[t, b]
-            pos = (pos_ref[t, b] + 1).astype(F32)
-            rank = count_ref[dev]
-            count_ref[dev] = rank + 1
-            return_ref[t, b] = ((dev * CAP + rank) << log2(tables)) + back_ref[t, b]
+            slot = return_ref[t, b] >> log2(tables)
+            dev, rank = slot >> 1, slot & 1
             at = pl.multiple_of(rank * chans, chans)
             send_ref[dev, pl.ds(at, chans), :] = product[:, t * seg : (t + 1) * seg].astype(BF16)
-            meta_ref[dev, pl.ds(4 + rank, 1), :] = jnp.full((1, seg), pos, F32)
             col = dev & (n_fy - 1)
-            mine = (lane >= chans) == (rank == 1)
             for side in range(2):
                 inside = (col < n_fy - 1) if side == 0 else (col > 0)
                 near = jnp.where(inside, dev + 1 - 2 * side, devices)
                 first = t * 4 + side * 2
-                meta_ref[near, pl.ds(2 * side + rank, 1), :] = jnp.where(
+                meta_ref[pl.ds(near * META + 2 * side + rank, 1), :] = jnp.where(
                     lane < chans, ends[first : first + 1, :], ends[first + 1 : first + 2, :]
                 )
-                old = meta_ref[near, 6 + side : 7 + side, :]
-                meta_ref[near, 6 + side : 7 + side, :] = jnp.where(mine, pos, old)
         return carry
 
     lax.fori_loop(0, blocks, one_block, 0, unroll=True)
-    send_ref[:, CAP * chans :, :] = meta_ref[0:devices].astype(BF16)
-    return_copy = pltpu.make_async_copy(return_ref, return_hbm, return_sem)
-    return_copy.start()
+    send_ref[:, CAP * chans :, :] = (
+        meta_ref[0 : devices * META, :].astype(BF16).reshape(devices, META, seg)
+    )
     return_copy.wait()
 
 
@@ -211,9 +232,9 @@
             pltpu.VMEM((blocks, width), BF16),
             pltpu.VMEM((tables, seg, seg), BF16),
             pltpu.VMEM((2,) + k1.shape, BF16),
-            pltpu.VMEM((chans * blocks, seg), F32),
+            pltpu.VMEM((chans * (blocks + PAD), seg), F32),
             pltpu.VMEM((tables, 4, seg), F32),
-            pltpu.VMEM((devices + 1, META, seg), F32),
+            pltpu.VMEM(((devices + 1) * META, seg), F32),
             pltpu.SMEM((devices,), jnp.int32),
             pltpu.SemaphoreType.DMA((4,)),
             pltpu.SemaphoreType.DMA((4,)),
@@ -354,11 +375,13 @@
     cols, lanes = upper.shape
     rows = jnp.concatenate([upper, lower], axis=1)
     product = jnp.dot(rows, weights_ref[...], preferred_element_type=F32)
-    column = lax.broadcasted_iota(jnp.int32, (cols, lanes), 0)
     ahead = pltpu.roll(product[:, 0:lanes], 1, axis=0)
     behind = pltpu.roll(product[:, 2 * lanes :], cols - 1, axis=0)
-    ahead = jnp.where(column == 0, before, ahead)
-    behind = jnp.where(column == cols - 1, after, behind)
+    edge = lax.broadcasted_iota(jnp.int32, (8, lanes), 0)
+    first = jnp.where(edge == 0, before, ahead[0:8, :])
+    last = jnp.where(edge == 7, after, behind[cols - 8 :, :])
+    ahead = jnp.concatenate([first, ahead[8:, :]], axis=0)
+    behind = jnp.concatenate([behind[: cols - 8, :], last], axis=0)
     return product[:, lanes : 2 * lanes] + ahead + behind + bias
 
 
@@ -374,7 +397,7 @@
         turned_ref[g] = field_ref[pl.ds(2 * g, 2)].reshape(2 * chans, cols).T
         return carry
 
-    lax.fori_loop(0, pairs, turn, 0, unroll=4)
+    lax.fori_loop(0, pairs, turn, 0, unroll=True)
     b1 = twice(b1_ref)
     for n, (k, d) in enumerate(((1, 0), (2, 2))):
         both = jnp.concatenate([side_ref[k, 0 : pairs - 1, :], side_ref[k, 1:pairs, :]], axis=1)
@@ -549,13 +572,14 @@
     return_copy = pltpu.make_async_copy(return_hbm, return_ref, return_sem)
     return_copy.start()
     return_copy.wait()
+    step = rows_ref.shape[1] // chans
     out_copies = []
 
     def finish(q):
         piece = pl.ds(q * part, part)
         for c in range(chans):
             out_ref[piece, c * seg : (c + 1) * seg] = rows_ref[
-                q, c * part : (c + 1) * part, :
+                q, c * step : c * step + part, :
             ].astype(BF16)
         out_copies.append(
             pltpu.make_async_copy(out_ref.at[piece], out_hbm.at[piece], out_sem.at[q])
@@ -573,7 +597,7 @@
                 at = pl.multiple_of((slot & 1) * chans, chans)
                 states.append(got_ref[slot >> 1, pl.ds(at, chans), :])
                 weights.append(table_ref[code & (tables - 1)])
-            rows_ref[q, pl.ds(n, chans, stride=part), :] = lax.dot_general(
+            rows_ref[q, pl.ds(n, chans, stride=step), :] = lax.dot_general(
                 jnp.concatenate(states, axis=1),
                 jnp.concatenate(weights, axis=1),
                 NT,
@@ -596,7 +620,7 @@
         out_specs=hbm(),
         scratch_shapes=[
             pltpu.SMEM(returns.shape, jnp.int32),
-            pltpu.VMEM((parts, chans * blocks // parts, seg), F32),
+            pltpu.VMEM((parts, chans * (blocks // parts + PAD), seg), F32),
             pltpu.VMEM((blocks, chans * seg), BF16),
             pltpu.SemaphoreType.DMA,
             pltpu.SemaphoreType.DMA((parts,)),

time: 146 us -> 144 us (0.986)
  Pallas kernels: 16.7 us -> 14.7 us
  transfers between devices with their start and end apart: 2 -> 2, of which waited for: 0 -> 0; matrix products, arithmetic and copies ran while one was open for 0% -> 0% of each run, Pallas kernels for 2% -> 1%
where the time goes in v4:
time: 144 us
  blocking collectives  127 us (88%)
  Pallas kernels  14.7 us (10%)
  starting transfers between devices  1.75 us (1%)
    all_to_all x2, blocking collectives, exchange(): return lax.all_to_all(buffer, AXES, split_axis=0, concat_axis=0, tiled=True)  127 us
    pallas_call x1, Pallas kernels, forward_remap(): pl.pallas_call(functools.partial(forward_kernel, n_fy), out_shape=(jax.Sh...  4.45 us
    pallas_call x1, Pallas kernels, backward_remap(): pl.pallas_call(backward_kernel, out_shape=jax.ShapeDtypeStruct((blocks, c...  3.01 us
  transfers between devices with their start and end apart: 2, of which 0 were waited for; matrix products, arithmetic and copies ran while one was open for 0% of the time, Pallas kernels for 1%

profile of v4, /device:TPU:6, one launch (start us, length us, event | category | flops | bytes accessed | tf_op | source)
XLA Modules:
  0.0 144.0 jit_solution(13349842561817747576)
XLA Ops:
  0.0 0.1 add_convert_fusion
  0.1 4.4 %shard_map.109 = (bf16[128,136,128]{2,1,0:T(8,128)(2,1)S(1)}, s32[2,64]{1,0:T(2,128)S(1)}, bf16[256,384]{1,0:T(8,128)(2,1)S(1)}, bf16[256,384]{1,0:T(8,128)(2,1)S(1)}) custom-call(s32[2,64]{1,0:T(2,128)} %bitcast.11, s32[2,64]{1,0:T(2,128)} %bitcast.12, s32[2,64]{1,0:T(2,128)} %bitcast.13, s32[2,64]{1,0:T(2,128)} %bitcast.14, bf16[64,8192]{1,0:T(8,128)(2,1)} %x_hbm.1, ...), custom_call_target="tpu_custom_call" | custom-call | tf_op jit(solution)/shard_map/pallas_call | solution.py:216
  4.5 0.1 broadcast_in_dim.12.place_ref
  4.6 66.8 %all_to_all.10.got_ref = bf16[128,136,128]{2,1,0:T(8,128)(2,1)S(1)} all-to-all(bf16[128,136,128]{2,1,0:T(8,128)(2,1)S(1)} %get-tuple-element.20), channel_id=1, replica_groups=mesh['fx'=8,'fy'=16] {'fx','fy'}, dimensions={0} | all-to-all | bytes 8912896 | tf_op jit(solution)/shard_map/all_to_all | solution.py:633
  71.4 0.0 copy-start.1
  71.4 0.0 copy-start.2
  71.4 2.7 %shard_map.110 = (bf16[64,64,128]{2,1,0:T(8,128)(2,1)S(1)}, bf16[144,128]{1,0:T(8,128)(2,1)S(1)}, bf16[144,128]{1,0:T(8,128)(2,1)S(1)}, f32[4,32,128]{2,1,0:T(8,128)S(1)}, s32[8,128]{1,0:T(8,128)S(1)}) custom-call(bf16[128,136,128]{2,1,0:T(8,128)(2,1)S(1)} %all_to_all.10.got_ref), custom_call_target="tpu_custom_call" | custom-call | tf_op jit(solution)/shard_map/pallas_call | solution.py:344
  74.2 0.0 collective-permute-start
  74.2 1.7 %collective-permute-start.1 = (bf16[144,128]{1,0:T(8,128)(2,1)S(1)}, bf16[144,128]{1,0:T(8,128)(2,1)S(1)}, u32[]{:S(2)}, u32[]{:S(2)}) collective-permute-start(bf16[144,128]{1,0:T(8,128)(2,1)S(1)} %get-tuple-element.29), channel_id=1, source_target_pairs={{16,0},{32,16},{48,32},{64,48},{80,64},{96,80},{112,96},{0,112},{1... | collective-permute-start | bytes 110600 | tf_op jit(solution)/shard_map/ppermute | solution.py:671
  75.9 0.0 copy-done.1
  75.9 1.9 %shard_map.111 = (bf16[32,128,128]{2,1,0:T(8,128)(2,1)S(1)}, bf16[32,128,128]{2,1,0:T(8,128)(2,1)S(1)}) custom-call(bf16[64,64,128]{2,1,0:T(8,128)(2,1)S(1)} %get-tuple-element.23.field_ref, f32[4,32,128]{2,1,0:T(8,128)S(1)} %get-tuple-element.24.side_ref.sides_ref, bf16[256,384]{1,0:T(8,128)(2,1)S(1)} %get-tuple-element.25.k1_ref, f32[1,64]{1,0:T(1,128)S(1)} %bitcast.8), custom_call_target="tpu_custom_call" | custom-call | flops 603979776 | bytes 4194304 | tf_op jit(solution)/shard_map/pallas_call | solution.py:425
  77.8 0.0 collective-permute-done.above_ref
  77.8 0.0 collective-permute-done.1.below_ref
  77.8 0.0 copy-done.2
  77.8 2.6 %shard_map.112 = bf16[128,128,128]{2,1,0:T(8,128)(2,1)S(1)} custom-call(s32[8,128]{1,0:T(8,128)S(1)} %get-tuple-element.21.pos_hbm, s32[2,128]{1,0:T(2,128)S(1)} %broadcast_in_dim.12.place_ref, bf16[32,128,128]{2,1,0:T(8,128)(2,1)S(1)} %get-tuple-element.26.field_ref, bf16[32,128,128]{2,1,0:T(8,128)(2,1)S(1)} %get-tuple-element.27.hid_ref, ...), custom_call_target="tpu_custom_call" | custom-call | tf_op jit(solution)/shard_map/pallas_call | solution.py:540
  80.5 0.0 copy-start
  80.5 60.5 %all_to_all.11.got_ref = bf16[128,128,128]{2,1,0:T(8,128)(2,1)S(1)} all-to-all(bf16[128,128,128]{2,1,0:T(8,128)(2,1)S(1)} %shard_map.112), channel_id=1, replica_groups=mesh['fx'=8,'fy'=16] {'fx','fy'}, dimensions={0} | all-to-all | bytes 8388608 | tf_op jit(solution)/shard_map/all_to_all | solution.py:633
  141.0 0.0 copy-done
  141.0 3.0 %shard_map.113 = bf16[64,8192]{1,0:T(8,128)(2,1)} custom-call(s32[2,64]{1,0:T(2,128)S(1)} %get-tuple-element.18.return_hbm, bf16[128,128,128]{2,1,0:T(8,128)(2,1)S(1)} %all_to_all.11.got_ref, bf16[64,128,128]{2,1,0:T(8,128)(2,1)S(1)} %copy-done), custom_call_target="tpu_custom_call" | custom-call | tf_op jit(solution)/shard_map/pallas_call | solution.py:616
Async XLA Ops:
  71.4 4.5 %copy-start.1 = (f32[64]{0:T(128)S(1)}, f32[64]{0:T(128)}, u32[]{:S(2)}) copy-start(f32[64]{0:T(128)} %param.19) | copy-start | bytes 772
  71.4 6.4 %copy-start.2 = (f32[64]{0:T(128)S(1)}, f32[64]{0:T(128)}, u32[]{:S(2)}) copy-start(f32[64]{0:T(128)} %param.21) | copy-start | bytes 772
  74.2 3.6 %collective-permute-start = (bf16[144,128]{1,0:T(8,128)(2,1)S(1)}, bf16[144,128]{1,0:T(8,128)(2,1)S(1)}, u32[]{:S(2)}, u32[]{:S(2)}) collective-permute-start(bf16[144,128]{1,0:T(8,128)(2,1)S(1)} %get-tuple-element.28), channel_id=1, source_target_pairs={{0,16},{16,32},{32,48},{48,64},{64,80},{80,96},{96,112},{112,0},{1... | collective-permute-start | bytes 110600 | tf_op jit(solution)/shard_map/ppermute | solution.py:670
  74.2 3.6 %collective-permute-start.1 = (bf16[144,128]{1,0:T(8,128)(2,1)S(1)}, bf16[144,128]{1,0:T(8,128)(2,1)S(1)}, u32[]{:S(2)}, u32[]{:S(2)}) collective-permute-start(bf16[144,128]{1,0:T(8,128)(2,1)S(1)} %get-tuple-element.29), channel_id=1, source_target_pairs={{16,0},{32,16},{48,32},{64,48},{80,64},{96,80},{112,96},{0,112},{1... | collective-permute-start | bytes 110600 | tf_op jit(solution)/shard_map/ppermute | solution.py:671
  80.5 60.5 %copy-start = (bf16[64,128,128]{2,1,0:T(8,128)(2,1)S(1)}, bf16[64,128,128]{2,1,0:T(8,128)(2,1)}, u32[]{:S(2)}) copy-start(bf16[64,128,128]{2,1,0:T(8,128)(2,1)} %table_ref.1) | copy-start | bytes 6291460

commit v5 on v4

--- a/solution.py
+++ b/solution.py
@@ -257,7 +257,8 @@
     side_ref,
     pos_ref,
     rows_ref,
-    sum_ref,
+    sum0_ref,
+    sum1_ref,
     spot_ref,
     spot_sem,
 ):
@@ -285,7 +286,7 @@
 
     def clear(r, carry):
         for rank in range(CAP):
-            sum_ref[rank, r] = jnp.zeros((chans, cols), F32)
+            (sum0_ref, sum1_ref)[rank][r] = jnp.zeros((chans, cols), F32)
         return carry
 
     lax.fori_loop(0, hblocks, clear, 0, unroll=4)
@@ -308,17 +309,20 @@
     spot_copy.wait()
 
     def add(d, carry):
-        for rank in range(CAP):
+        rows, sums = [], []
+        for rank, sum_ref in enumerate((sum0_ref, sum1_ref)):
             pos = spot_ref[rank, d]
-            row = jnp.where(pos < 0, hblocks, pos)
+            rows.append(jnp.where(pos < 0, hblocks, pos))
             block = got_ref[d, rank * chans : (rank + 1) * chans, :]
-            sum_ref[rank, row] = sum_ref[rank, row] + block.astype(F32)
+            sums.append(sum_ref[rows[-1]] + block.astype(F32))
+        sum0_ref[rows[0]] = sums[0]
+        sum1_ref[rows[1]] = sums[1]
         return carry
 
     lax.fori_loop(0, devices, add, 0, unroll=16)
 
     def total_of(r):
-        return sum_ref[0, r] + sum_ref[1, r]
+        return sum0_ref[r] + sum1_ref[r]
 
     corners = jnp.zeros((up_ref.shape[0] - cols, lanes), F32)
     corner_row = lax.broadcasted_iota(jnp.int32, corners.shape, 0)
@@ -354,7 +358,8 @@
         out_specs=(vmem(),) * 5,
         scratch_shapes=[
             pltpu.VMEM((devices * META, cols), F32),
-            pltpu.VMEM((CAP, hblocks + 1, chans, cols), F32),
+            pltpu.VMEM((hblocks + 1, chans, cols), F32),
+            pltpu.VMEM((hblocks + 1, chans, cols), F32),
             pltpu.SMEM((8, devices), jnp.int32),
             pltpu.SemaphoreType.DMA,
         ],

time: 144 us -> 143 us (level)
  no operation moved by 1% of the time
where the time goes in v5:
time: 143 us
  blocking collectives  127 us (89%)
  Pallas kernels  14 us (10%)
  starting transfers between devices  1.75 us (1%)
    all_to_all x2, blocking collectives, exchange(): return lax.all_to_all(buffer, AXES, split_axis=0, concat_axis=0, tiled=True)  127 us
    pallas_call x1, Pallas kernels, forward_remap(): pl.pallas_call(functools.partial(forward_kernel, n_fy), out_shape=(jax.Sh...  4.44 us
    pallas_call x1, Pallas kernels, backward_remap(): pl.pallas_call(backward_kernel, out_shape=jax.ShapeDtypeStruct((blocks, c...  3.01 us
  transfers between devices with their start and end apart: 2, of which 0 were waited for; matrix products, arithmetic and copies ran while one was open for 0% of the time, Pallas kernels for 1%

profile of v5, /device:TPU:6, one launch (start us, length us, event | category | flops | bytes accessed | tf_op | source)
XLA Modules:
  0.0 143.3 jit_solution(17124510846060667225)
XLA Ops:
  0.0 0.1 add_convert_fusion
  0.1 4.4 %shard_map.109 = (bf16[128,136,128]{2,1,0:T(8,128)(2,1)S(1)}, s32[2,64]{1,0:T(2,128)S(1)}, bf16[256,384]{1,0:T(8,128)(2,1)S(1)}, bf16[256,384]{1,0:T(8,128)(2,1)S(1)}) custom-call(s32[2,64]{1,0:T(2,128)} %bitcast.11, s32[2,64]{1,0:T(2,128)} %bitcast.12, s32[2,64]{1,0:T(2,128)} %bitcast.13, s32[2,64]{1,0:T(2,128)} %bitcast.14, bf16[64,8192]{1,0:T(8,128)(2,1)} %x_hbm.1, ...), custom_call_target="tpu_custom_call" | custom-call | tf_op jit(solution)/shard_map/pallas_call | solution.py:216
  4.5 0.1 broadcast_in_dim.12.place_ref
  4.6 66.8 %all_to_all.10.got_ref = bf16[128,136,128]{2,1,0:T(8,128)(2,1)S(1)} all-to-all(bf16[128,136,128]{2,1,0:T(8,128)(2,1)S(1)} %get-tuple-element.20), channel_id=1, replica_groups=mesh['fx'=8,'fy'=16] {'fx','fy'}, dimensions={0} | all-to-all | bytes 8912896 | tf_op jit(solution)/shard_map/all_to_all | solution.py:638
  71.4 0.0 copy-start.1
  71.4 0.0 copy-start.2
  71.4 2.1 %shard_map.110 = (bf16[64,64,128]{2,1,0:T(8,128)(2,1)S(1)}, bf16[144,128]{1,0:T(8,128)(2,1)S(1)}, bf16[144,128]{1,0:T(8,128)(2,1)S(1)}, f32[4,32,128]{2,1,0:T(8,128)S(1)}, s32[8,128]{1,0:T(8,128)S(1)}) custom-call(bf16[128,136,128]{2,1,0:T(8,128)(2,1)S(1)} %all_to_all.10.got_ref), custom_call_target="tpu_custom_call" | custom-call | tf_op jit(solution)/shard_map/pallas_call | solution.py:348
  73.5 0.0 collective-permute-start
  73.6 1.7 %collective-permute-start.1 = (bf16[144,128]{1,0:T(8,128)(2,1)S(1)}, bf16[144,128]{1,0:T(8,128)(2,1)S(1)}, u32[]{:S(2)}, u32[]{:S(2)}) collective-permute-start(bf16[144,128]{1,0:T(8,128)(2,1)S(1)} %get-tuple-element.29), channel_id=1, source_target_pairs={{16,0},{32,16},{48,32},{64,48},{80,64},{96,80},{112,96},{0,112},{1... | collective-permute-start | bytes 110600 | tf_op jit(solution)/shard_map/ppermute | solution.py:676
  75.3 0.0 copy-done.1
  75.3 1.9 %shard_map.111 = (bf16[32,128,128]{2,1,0:T(8,128)(2,1)S(1)}, bf16[32,128,128]{2,1,0:T(8,128)(2,1)S(1)}) custom-call(bf16[64,64,128]{2,1,0:T(8,128)(2,1)S(1)} %get-tuple-element.23.field_ref, f32[4,32,128]{2,1,0:T(8,128)S(1)} %get-tuple-element.24.side_ref.sides_ref, bf16[256,384]{1,0:T(8,128)(2,1)S(1)} %get-tuple-element.25.k1_ref, f32[1,64]{1,0:T(1,128)S(1)} %bitcast.8), custom_call_target="tpu_custom_call" | custom-call | flops 603979776 | bytes 4194304 | tf_op jit(solution)/shard_map/pallas_call | solution.py:430
  77.2 0.0 collective-permute-done.above_ref
  77.2 0.0 collective-permute-done.1.below_ref
  77.2 0.0 copy-done.2
  77.2 2.6 %shard_map.112 = bf16[128,128,128]{2,1,0:T(8,128)(2,1)S(1)} custom-call(s32[8,128]{1,0:T(8,128)S(1)} %get-tuple-element.21.pos_hbm, s32[2,128]{1,0:T(2,128)S(1)} %broadcast_in_dim.12.place_ref, bf16[32,128,128]{2,1,0:T(8,128)(2,1)S(1)} %get-tuple-element.26.field_ref, bf16[32,128,128]{2,1,0:T(8,128)(2,1)S(1)} %get-tuple-element.27.hid_ref, ...), custom_call_target="tpu_custom_call" | custom-call | tf_op jit(solution)/shard_map/pallas_call | solution.py:545
  79.8 0.0 copy-start
  79.8 60.5 %all_to_all.11.got_ref = bf16[128,128,128]{2,1,0:T(8,128)(2,1)S(1)} all-to-all(bf16[128,128,128]{2,1,0:T(8,128)(2,1)S(1)} %shard_map.112), channel_id=1, replica_groups=mesh['fx'=8,'fy'=16] {'fx','fy'}, dimensions={0} | all-to-all | bytes 8388608 | tf_op jit(solution)/shard_map/all_to_all | solution.py:638
  140.3 0.0 copy-done
  140.3 3.0 %shard_map.113 = bf16[64,8192]{1,0:T(8,128)(2,1)} custom-call(s32[2,64]{1,0:T(2,128)S(1)} %get-tuple-element.18.return_hbm, bf16[128,128,128]{2,1,0:T(8,128)(2,1)S(1)} %all_to_all.11.got_ref, bf16[64,128,128]{2,1,0:T(8,128)(2,1)S(1)} %copy-done), custom_call_target="tpu_custom_call" | custom-call | tf_op jit(solution)/shard_map/pallas_call | solution.py:621
Async XLA Ops:
  71.4 3.9 %copy-start.1 = (f32[64]{0:T(128)S(1)}, f32[64]{0:T(128)}, u32[]{:S(2)}) copy-start(f32[64]{0:T(128)} %param.19) | copy-start | bytes 772
  71.4 5.7 %copy-start.2 = (f32[64]{0:T(128)S(1)}, f32[64]{0:T(128)}, u32[]{:S(2)}) copy-start(f32[64]{0:T(128)} %param.21) | copy-start | bytes 772
  73.5 3.6 %collective-permute-start = (bf16[144,128]{1,0:T(8,128)(2,1)S(1)}, bf16[144,128]{1,0:T(8,128)(2,1)S(1)}, u32[]{:S(2)}, u32[]{:S(2)}) collective-permute-start(bf16[144,128]{1,0:T(8,128)(2,1)S(1)} %get-tuple-element.28), channel_id=1, source_target_pairs={{0,16},{16,32},{32,48},{48,64},{64,80},{80,96},{96,112},{112,0},{1... | collective-permute-start | bytes 110600 | tf_op jit(solution)/shard_map/ppermute | solution.py:675
  73.6 3.6 %collective-permute-start.1 = (bf16[144,128]{1,0:T(8,128)(2,1)S(1)}, bf16[144,128]{1,0:T(8,128)(2,1)S(1)}, u32[]{:S(2)}, u32[]{:S(2)}) collective-permute-start(bf16[144,128]{1,0:T(8,128)(2,1)S(1)} %get-tuple-element.29), channel_id=1, source_target_pairs={{16,0},{32,16},{48,32},{64,48},{80,64},{96,80},{112,96},{0,112},{1... | collective-permute-start | bytes 110600 | tf_op jit(solution)/shard_map/ppermute | solution.py:676
  79.8 60.5 %copy-start = (bf16[64,128,128]{2,1,0:T(8,128)(2,1)S(1)}, bf16[64,128,128]{2,1,0:T(8,128)(2,1)}, u32[]{:S(2)}) copy-start(bf16[64,128,128]{2,1,0:T(8,128)(2,1)} %table_ref.1) | copy-start | bytes 6291460

commit v6 on v5

--- a/solution.py
+++ b/solution.py
@@ -446,8 +446,8 @@
     field_ref,
     hid_ref,
     sides_ref,
+    below_ref,
     above_ref,
-    below_ref,
     k1_ref,
     b1_ref,
     k2_ref,
@@ -538,7 +538,7 @@
     lax.fori_loop(0, devices, pick, 0, unroll=16)
 
 
-def outer_state(positions, place, field, hidden, sides, above, below, k1, b1, k2, b2):
+def outer_state(positions, place, field, hidden, sides, below, above, k1, b1, k2, b2):
     pairs, cols, lanes = field.shape
     chans = lanes // 2
     devices = positions.shape[1]
@@ -555,7 +555,7 @@
             pltpu.SemaphoreType.DMA,
         ],
         compiler_params=params(),
-    )(positions, place, field, hidden, sides, above, below, k1, b1, k2, b2)
+    )(positions, place, field, hidden, sides, below, above, k1, b1, k2, b2)
 
 
 def backward_kernel(
@@ -672,11 +672,11 @@
     send, place = lax.optimization_barrier((send, place))
     b1, b2 = bias_one[None], bias_two[None]
     field, up, down, sides, positions = sum_field(exchange(send), hblocks)
+    below = lax.ppermute(up, "fx", [((i + 1) % n_fx, i) for i in range(n_fx)])
     above = lax.ppermute(down, "fx", [(i, (i + 1) % n_fx) for i in range(n_fx)])
-    below = lax.ppermute(up, "fx", [((i + 1) % n_fx, i) for i in range(n_fx)])
     turned, hidden = inner_hidden(field, sides, w1, b1)
     send_back = outer_state(
-        positions, place, turned, hidden, sides, above, below, w1, b1, w2, b2
+        positions, place, turned, hidden, sides, below, above, w1, b1, w2, b2
     )
     return backward_remap(returns, exchange(send_back), back_table)
 

time: 143 us -> 143 us (level)
    ppermute x1, starting transfers between devices: 1.73 us -> 0.02 us  [local(): below = lax.ppermute(up, 'fx', [((i + 1) % n_fx, i) for i in range(n_fx)])]
  transfers between devices with their start and end apart: 2 -> 2, of which waited for: 0 -> 1; matrix products, arithmetic and copies ran while one was open for 0% -> 0% of each run, Pallas kernels for 1% -> 1%
where the time goes in v6:
time: 143 us
  blocking collectives  127 us (89%)
  Pallas kernels  14.1 us (10%)
    all_to_all x2, blocking collectives, exchange(): return lax.all_to_all(buffer, AXES, split_axis=0, concat_axis=0, tiled=True)  127 us
    pallas_call x1, Pallas kernels, forward_remap(): pl.pallas_call(functools.partial(forward_kernel, n_fy), out_shape=(jax.Sh...  4.45 us
    pallas_call x1, Pallas kernels, backward_remap(): pl.pallas_call(backward_kernel, out_shape=jax.ShapeDtypeStruct((blocks, c...  3.01 us
  transfers between devices with their start and end apart: 2, of which 1 were waited for; matrix products, arithmetic and copies ran while one was open for 0% of the time, Pallas kernels for 1%

profile of v6, /device:TPU:6, one launch (start us, length us, event | category | flops | bytes accessed | tf_op | source)
XLA Modules:
  0.0 142.8 jit_solution(7892293646669441345)
XLA Ops:
  0.0 0.1 add_convert_fusion
  0.1 4.4 %shard_map.109 = (bf16[128,136,128]{2,1,0:T(8,128)(2,1)S(1)}, s32[2,64]{1,0:T(2,128)S(1)}, bf16[256,384]{1,0:T(8,128)(2,1)S(1)}, bf16[256,384]{1,0:T(8,128)(2,1)S(1)}) custom-call(s32[2,64]{1,0:T(2,128)} %bitcast.11, s32[2,64]{1,0:T(2,128)} %bitcast.12, s32[2,64]{1,0:T(2,128)} %bitcast.13, s32[2,64]{1,0:T(2,128)} %bitcast.14, bf16[64,8192]{1,0:T(8,128)(2,1)} %x_hbm.1, ...), custom_call_target="tpu_custom_call" | custom-call | tf_op jit(solution)/shard_map/pallas_call | solution.py:216
  4.5 0.1 broadcast_in_dim.12.place_ref
  4.6 66.8 %all_to_all.10.got_ref = bf16[128,136,128]{2,1,0:T(8,128)(2,1)S(1)} all-to-all(bf16[128,136,128]{2,1,0:T(8,128)(2,1)S(1)} %get-tuple-element.20), channel_id=1, replica_groups=mesh['fx'=8,'fy'=16] {'fx','fy'}, dimensions={0} | all-to-all | bytes 8912896 | tf_op jit(solution)/shard_map/all_to_all | solution.py:638
  71.4 0.0 copy-start.1
  71.4 0.0 copy-start.2
  71.4 2.1 %shard_map.110 = (bf16[64,64,128]{2,1,0:T(8,128)(2,1)S(1)}, bf16[144,128]{1,0:T(8,128)(2,1)S(1)}, bf16[144,128]{1,0:T(8,128)(2,1)S(1)}, f32[4,32,128]{2,1,0:T(8,128)S(1)}, s32[8,128]{1,0:T(8,128)S(1)}) custom-call(bf16[128,136,128]{2,1,0:T(8,128)(2,1)S(1)} %all_to_all.10.got_ref), custom_call_target="tpu_custom_call" | custom-call | tf_op jit(solution)/shard_map/pallas_call | solution.py:348
  73.5 0.0 collective-permute-start
  73.6 0.5 collective-permute-start.1
  74.1 0.0 copy-done.1
  74.1 1.9 %shard_map.111 = (bf16[32,128,128]{2,1,0:T(8,128)(2,1)S(1)}, bf16[32,128,128]{2,1,0:T(8,128)(2,1)S(1)}) custom-call(bf16[64,64,128]{2,1,0:T(8,128)(2,1)S(1)} %get-tuple-element.23.field_ref, f32[4,32,128]{2,1,0:T(8,128)S(1)} %get-tuple-element.24.side_ref.sides_ref, bf16[256,384]{1,0:T(8,128)(2,1)S(1)} %get-tuple-element.25.k1_ref, f32[1,64]{1,0:T(1,128)S(1)} %bitcast.8), custom_call_target="tpu_custom_call" | custom-call | flops 603979776 | bytes 4194304 | tf_op jit(solution)/shard_map/pallas_call | solution.py:430
  75.9 0.0 collective-permute-done.below_ref
  75.9 1.0 collective-permute-done.1.above_ref
  77.0 0.0 copy-done.2
  77.0 2.6 %shard_map.112 = bf16[128,128,128]{2,1,0:T(8,128)(2,1)S(1)} custom-call(s32[8,128]{1,0:T(8,128)S(1)} %get-tuple-element.21.pos_hbm, s32[2,128]{1,0:T(2,128)S(1)} %broadcast_in_dim.12.place_ref, bf16[32,128,128]{2,1,0:T(8,128)(2,1)S(1)} %get-tuple-element.26.field_ref, bf16[32,128,128]{2,1,0:T(8,128)(2,1)S(1)} %get-tuple-element.27.hid_ref, ...), custom_call_target="tpu_custom_call" | custom-call | tf_op jit(solution)/shard_map/pallas_call | solution.py:545
  79.6 0.0 copy-start
  79.6 60.2 %all_to_all.11.got_ref = bf16[128,128,128]{2,1,0:T(8,128)(2,1)S(1)} all-to-all(bf16[128,128,128]{2,1,0:T(8,128)(2,1)S(1)} %shard_map.112), channel_id=1, replica_groups=mesh['fx'=8,'fy'=16] {'fx','fy'}, dimensions={0} | all-to-all | bytes 8388608 | tf_op jit(solution)/shard_map/all_to_all | solution.py:638
  139.8 0.0 copy-done
  139.8 3.0 %shard_map.113 = bf16[64,8192]{1,0:T(8,128)(2,1)} custom-call(s32[2,64]{1,0:T(2,128)S(1)} %get-tuple-element.18.return_hbm, bf16[128,128,128]{2,1,0:T(8,128)(2,1)S(1)} %all_to_all.11.got_ref, bf16[64,128,128]{2,1,0:T(8,128)(2,1)S(1)} %copy-done), custom_call_target="tpu_custom_call" | custom-call | tf_op jit(solution)/shard_map/pallas_call | solution.py:621
Async XLA Ops:
  71.4 2.6 %copy-start.1 = (f32[64]{0:T(128)S(1)}, f32[64]{0:T(128)}, u32[]{:S(2)}) copy-start(f32[64]{0:T(128)} %param.19) | copy-start | bytes 772
  71.4 5.5 %copy-start.2 = (f32[64]{0:T(128)S(1)}, f32[64]{0:T(128)}, u32[]{:S(2)}) copy-start(f32[64]{0:T(128)} %param.21) | copy-start | bytes 772
  73.5 2.4 %collective-permute-start = (bf16[144,128]{1,0:T(8,128)(2,1)S(1)}, bf16[144,128]{1,0:T(8,128)(2,1)S(1)}, u32[]{:S(2)}, u32[]{:S(2)}) collective-permute-start(bf16[144,128]{1,0:T(8,128)(2,1)S(1)} %get-tuple-element.28), channel_id=1, source_target_pairs={{16,0},{32,16},{48,32},{64,48},{80,64},{96,80},{112,96},{0,112},{1... | collective-permute-start | bytes 110600 | tf_op jit(solution)/shard_map/ppermute | solution.py:675
  73.6 3.4 %collective-permute-start.1 = (bf16[144,128]{1,0:T(8,128)(2,1)S(1)}, bf16[144,128]{1,0:T(8,128)(2,1)S(1)}, u32[]{:S(2)}, u32[]{:S(2)}) collective-permute-start(bf16[144,128]{1,0:T(8,128)(2,1)S(1)} %get-tuple-element.29), channel_id=1, source_target_pairs={{0,16},{16,32},{32,48},{48,64},{64,80},{80,96},{96,112},{112,0},{1... | collective-permute-start | bytes 110600 | tf_op jit(solution)/shard_map/ppermute | solution.py:676
  79.6 60.2 %copy-start = (bf16[64,128,128]{2,1,0:T(8,128)(2,1)S(1)}, bf16[64,128,128]{2,1,0:T(8,128)(2,1)}, u32[]{:S(2)}) copy-start(bf16[64,128,128]{2,1,0:T(8,128)(2,1)} %table_ref.1) | copy-start | bytes 6291460

commit v7 on v6

--- a/solution.py
+++ b/solution.py
@@ -394,7 +394,48 @@
     return jnp.concatenate([bias_ref[...], bias_ref[...]], axis=1)
 
 
-def inner_kernel(field_ref, side_ref, k1_ref, b1_ref, turned_ref, hid_ref, halo_ref):
+def column_ends(block):
+    cols = block.shape[0]
+    return (
+        block[0:16, :].astype(F32)[0:1, :],
+        block[cols - 16 : cols, :].astype(F32)[15:16, :],
+    )
+
+
+def side_columns(columns, weights_ref, bias, place_ref):
+    c = columns
+    left = taps(c[1], weights_ref, 0)
+    right = taps(c[4], weights_ref, 2)
+    before = taps(c[0], weights_ref, 0) + taps(c[1], weights_ref, 1) + taps(c[2], weights_ref, 2)
+    after = taps(c[3], weights_ref, 0) + taps(c[4], weights_ref, 1) + taps(c[5], weights_ref, 2)
+    before = jnp.where(place_ref[0:1, :] > 0, gelu(before + bias), 0.0)
+    after = jnp.where(place_ref[1:2, :] > 0, gelu(after + bias), 0.0)
+    return left, right, before, after
+
+
+def put_state(state_ref, g, out, field):
+    _, chans, cols = state_ref.shape
+    state = out + field.astype(F32)
+    state_ref[pl.ds(2 * g, 2)] = state.T.astype(BF16).reshape(2, chans, cols)
+
+
+def inner_kernel(
+    field_ref,
+    side_ref,
+    place_ref,
+    k1_ref,
+    b1_ref,
+    k2_ref,
+    b2_ref,
+    ends_ref,
+    hids_ref,
+    cols_ref,
+    state_ref,
+    turned_ref,
+    hid_ref,
+    column_ref,
+    halo_ref,
+):
     hblocks, chans, cols = field_ref.shape
     pairs = hblocks // 2
 
@@ -403,48 +444,93 @@
         return carry
 
     lax.fori_loop(0, pairs, turn, 0, unroll=True)
+    for n, k in enumerate((0, 1, 4, 5)):
+        column_ref[k, 0:pairs, :] = side_ref[n]
+
+    def inner_side(g, carry):
+        for k, end in enumerate(column_ends(turned_ref[g])):
+            column_ref[2 + k, pl.ds(g, 1), :] = end
+        return carry
+
+    lax.fori_loop(0, pairs, inner_side, 0, unroll=4)
     b1 = twice(b1_ref)
-    for n, (k, d) in enumerate(((1, 0), (2, 2))):
-        both = jnp.concatenate([side_ref[k, 0 : pairs - 1, :], side_ref[k, 1:pairs, :]], axis=1)
-        halo_ref[n, 1:pairs, :] = taps(both.astype(BF16), k1_ref, d)
+    b2 = twice(b2_ref)
+    columns = [
+        jnp.concatenate([column_ref[k, 0 : pairs - 1, :], column_ref[k, 1:pairs, :]], axis=1).astype(
+            BF16
+        )
+        for k in range(6)
+    ]
+    left, right, before, after = side_columns(columns, k1_ref, b1, place_ref)
+    halo_ref[0, 1:pairs, :] = left
+    halo_ref[1, 1:pairs, :] = right
+    cols_ref[...] = jnp.zeros_like(cols_ref)
+    for n, (column, d) in enumerate(((before, 0), (after, 2))):
+        cols_ref[n : n + 1, :] = column[0:1, :]
+        cols_ref[2 + n : 3 + n, :] = column[pairs - 2 : pairs - 1, :]
+        column_ref[n, 1:pairs, :] = column
+        both = jnp.concatenate(
+            [column_ref[n, 1 : pairs - 1, :], column_ref[n, 2:pairs, :]], axis=1
+        )
+        halo_ref[2 + n, 1 : pairs - 1, :] = taps(both.astype(BF16), k2_ref, d)
+
+    def halos(h, g):
+        return halo_ref[h, pl.ds(g, 1), :], halo_ref[h + 1, pl.ds(g, 1), :]
 
     def first(g, carry):
-        out = row_pair_conv(
-            turned_ref[g - 1],
-            turned_ref[g],
-            k1_ref,
-            b1,
-            halo_ref[0, pl.ds(g, 1), :],
-            halo_ref[1, pl.ds(g, 1), :],
-        )
+        out = row_pair_conv(turned_ref[g - 1], turned_ref[g], k1_ref, b1, *halos(0, g))
         hid_ref[g] = gelu(out).astype(BF16)
         return carry
 
     lax.fori_loop(1, pairs, first, 0, unroll=True)
 
-
-def inner_hidden(field, sides, k1, b1):
+    def second(g, carry):
+        out = row_pair_conv(hid_ref[g], hid_ref[g + 1], k2_ref, b2, *halos(2, g))
+        put_state(state_ref, g, out, turned_ref[g])
+        return carry
+
+    lax.fori_loop(1, pairs - 1, second, 0, unroll=True)
+    for n, g in enumerate((0, pairs - 1)):
+        ends_ref[n] = turned_ref[g]
+    for n, g in enumerate((1, pairs - 1)):
+        hids_ref[n] = hid_ref[g]
+
+
+def inner_state(field, sides, place, k1, b1, k2, b2):
     hblocks, chans, cols = field.shape
     pairs = hblocks // 2
-    shape = jax.ShapeDtypeStruct((pairs, cols, 2 * chans), BF16)
+    lanes = 2 * chans
+    two = jax.ShapeDtypeStruct((2, cols, lanes), BF16)
     return pl.pallas_call(
         inner_kernel,
-        out_shape=(shape, shape),
-        in_specs=[vmem()] * 4,
-        out_specs=(vmem(), vmem()),
-        scratch_shapes=[pltpu.VMEM((2, pairs + 8, 2 * chans), F32)],
+        out_shape=(
+            two,
+            two,
+            jax.ShapeDtypeStruct((8, lanes), F32),
+            jax.ShapeDtypeStruct((hblocks, chans, cols), BF16),
+        ),
+        in_specs=[vmem()] * 7,
+        out_specs=(vmem(),) * 4,
+        scratch_shapes=[
+            pltpu.VMEM((pairs, cols, lanes), BF16),
+            pltpu.VMEM((pairs, cols, lanes), BF16),
+            pltpu.VMEM((6, pairs + 8, lanes), F32),
+            pltpu.VMEM((4, pairs + 8, lanes), F32),
+        ],
         compiler_params=params(),
         cost_estimate=pl.CostEstimate(
-            flops=2 * 8192 * 9 * 64 * 64, bytes_accessed=4 << 20, transcendentals=1 << 19
+            flops=4 * 8192 * 9 * 64 * 64, bytes_accessed=4 << 20, transcendentals=1 << 19
         ),
-    )(field, sides, k1, b1)
+    )(field, sides, place, k1, b1, k2, b2)
 
 
 def outer_kernel(
     pos_hbm,
     place_ref,
-    field_ref,
-    hid_ref,
+    ends_ref,
+    hids_ref,
+    cols_ref,
+    inner_ref,
     sides_ref,
     below_ref,
     above_ref,
@@ -453,80 +539,58 @@
     k2_ref,
     b2_ref,
     send_ref,
-    side_ref,
-    halo_ref,
+    column_ref,
     state_ref,
     pos_ref,
     pos_sem,
 ):
     pos_copy = pltpu.make_async_copy(pos_hbm, pos_ref, pos_sem)
     pos_copy.start()
-    pairs, cols, lanes = field_ref.shape
-    chans = lanes // 2
+    hblocks, chans, cols = inner_ref.shape
+    pairs = hblocks // 2
     devices = pos_ref.shape[1]
-    groups = pairs + 1
+    state_ref[pl.ds(2, hblocks - 4)] = inner_ref[pl.ds(2, hblocks - 4)]
+    column_ref[...] = jnp.zeros_like(column_ref)
     above = above_ref[cols:, :].astype(F32)
     below = below_ref[cols:, :].astype(F32)
     for n, k in enumerate((0, 1, 4, 5)):
-        side_ref[k, 0:1, :] = above[n : n + 1, :]
-        side_ref[k, 1 : pairs + 1, :] = sides_ref[n]
-        side_ref[k, pairs + 1 : pairs + 2, :] = below[n : n + 1, :]
-
-    def ends(block):
-        return (
-            block[0:16, :].astype(F32)[0:1, :],
-            block[cols - 16 : cols, :].astype(F32)[15:16, :],
-        )
-
-    for k, (high, low) in enumerate(zip(ends(above_ref[0:cols, :]), ends(below_ref[0:cols, :]))):
-        side_ref[2 + k, 0:1, :] = high
-        side_ref[2 + k, pairs + 1 : pairs + 2, :] = low
-
-    def inner_side(g, carry):
-        for k, end in enumerate(ends(field_ref[g])):
-            side_ref[2 + k, pl.ds(g + 1, 1), :] = end
-        return carry
-
-    lax.fori_loop(0, pairs, inner_side, 0, unroll=4)
-
-    def paired(k):
-        return jnp.concatenate(
-            [side_ref[k, 0:groups, :], side_ref[k, 1 : groups + 1, :]], axis=1
-        ).astype(BF16)
-
+        column_ref[k, 0, 0:1, :] = above[n : n + 1, :]
+        column_ref[k, 0, 1:2, :] = sides_ref[n, pairs - 1 : pairs, :]
+        column_ref[k, 1, 0:1, :] = sides_ref[n, 0:1, :]
+        column_ref[k, 1, 1:2, :] = below[n : n + 1, :]
+    for part, row, block in (
+        (0, 0, above_ref[0:cols, :]),
+        (0, 1, ends_ref[1]),
+        (1, 0, ends_ref[0]),
+        (1, 1, below_ref[0:cols, :]),
+    ):
+        for k, end in enumerate(column_ends(block)):
+            column_ref[2 + k, part, row : row + 1, :] = end
     b1 = twice(b1_ref)
     b2 = twice(b2_ref)
-    c = [paired(k) for k in range(6)]
-    left = taps(c[1], k1_ref, 0)
-    right = taps(c[4], k1_ref, 2)
-    before = taps(c[0], k1_ref, 0) + taps(c[1], k1_ref, 1) + taps(c[2], k1_ref, 2) + b1
-    after = taps(c[3], k1_ref, 0) + taps(c[4], k1_ref, 1) + taps(c[5], k1_ref, 2) + b1
-    before = jnp.where(place_ref[0:1, :] > 0, gelu(before), 0.0)
-    after = jnp.where(place_ref[1:2, :] > 0, gelu(after), 0.0)
+    columns = [
+        jnp.concatenate([column_ref[k, 0], column_ref[k, 1]], axis=1).astype(BF16) for k in range(6)
+    ]
+    left, right, before, after = side_columns(columns, k1_ref, b1, place_ref)
+    top = lax.broadcasted_iota(jnp.int32, before.shape, 0) == 0
+    halos = []
     for n, (column, d) in enumerate(((before, 0), (after, 2))):
-        side_ref[n, 0:groups, :] = column
-        both = jnp.concatenate([side_ref[n, 0:pairs, :], side_ref[n, 1 : pairs + 1, :]], axis=1)
-        halo_ref[n, 0:pairs, :] = taps(both.astype(BF16), k2_ref, d)
-
-    def hidden(upper, lower, g):
-        out = row_pair_conv(upper, lower, k1_ref, b1, left[g : g + 1, :], right[g : g + 1, :])
-        return gelu(out).astype(BF16)
-
-    def second(g, upper, lower):
-        out = row_pair_conv(
-            upper, lower, k2_ref, b2, halo_ref[0, pl.ds(g, 1), :], halo_ref[1, pl.ds(g, 1), :]
-        )
-        state = out + field_ref[g].astype(F32)
-        state_ref[pl.ds(2 * g, 2)] = state.T.astype(BF16).reshape(2, chans, cols)
-
-    second(0, hidden(above_ref[0:cols, :], field_ref[0], 0), hid_ref[1])
-    second(pairs - 1, hid_ref[pairs - 1], hidden(field_ref[pairs - 1], below_ref[0:cols, :], pairs))
-
-    def inner(g, carry):
-        second(g, hid_ref[g], hid_ref[g + 1])
-        return carry
-
-    lax.fori_loop(1, pairs - 1, inner, 0, unroll=True)
+        upper = jnp.where(top, column, cols_ref[2 + n : 3 + n, :])
+        lower = jnp.where(top, cols_ref[n : n + 1, :], column)
+        both = jnp.concatenate([upper, lower], axis=1).astype(BF16)
+        halos.append(taps(both, k2_ref, d))
+
+    def hidden(upper, lower, row):
+        sides = left[row : row + 1, :], right[row : row + 1, :]
+        return gelu(row_pair_conv(upper, lower, k1_ref, b1, *sides)).astype(BF16)
+
+    def second(g, upper, lower, row):
+        sides = (halo[row : row + 1, :] for halo in halos)
+        out = row_pair_conv(upper, lower, k2_ref, b2, *sides)
+        put_state(state_ref, g, out, ends_ref[row])
+
+    second(0, hidden(above_ref[0:cols, :], ends_ref[0], 0), hids_ref[0], 0)
+    second(pairs - 1, hids_ref[1], hidden(ends_ref[1], below_ref[0:cols, :], 1), 1)
     pos_copy.wait()
 
     def pick(d, carry):
@@ -538,24 +602,22 @@
     lax.fori_loop(0, devices, pick, 0, unroll=16)
 
 
-def outer_state(positions, place, field, hidden, sides, below, above, k1, b1, k2, b2):
-    pairs, cols, lanes = field.shape
-    chans = lanes // 2
+def outer_state(positions, place, ends, hids, columns, inner, sides, below, above, k1, b1, k2, b2):
+    hblocks, chans, cols = inner.shape
     devices = positions.shape[1]
     return pl.pallas_call(
         outer_kernel,
         out_shape=jax.ShapeDtypeStruct((devices, CAP * chans, cols), BF16),
-        in_specs=[vmem()] * 11,
+        in_specs=[vmem()] * 13,
         out_specs=vmem(),
         scratch_shapes=[
-            pltpu.VMEM((6, pairs + 8, lanes), F32),
-            pltpu.VMEM((2, pairs + 8, lanes), F32),
-            pltpu.VMEM((2 * pairs, chans, cols), BF16),
+            pltpu.VMEM((6, 2, 8, 2 * chans), F32),
+            pltpu.VMEM((hblocks, chans, cols), BF16),
             pltpu.SMEM(positions.shape, jnp.int32),
             pltpu.SemaphoreType.DMA,
         ],
         compiler_params=params(),
-    )(positions, place, field, hidden, sides, below, above, k1, b1, k2, b2)
+    )(positions, place, ends, hids, columns, inner, sides, below, above, k1, b1, k2, b2)
 
 
 def backward_kernel(
@@ -674,9 +736,9 @@
     field, up, down, sides, positions = sum_field(exchange(send), hblocks)
     below = lax.ppermute(up, "fx", [((i + 1) % n_fx, i) for i in range(n_fx)])
     above = lax.ppermute(down, "fx", [(i, (i + 1) % n_fx) for i in range(n_fx)])
-    turned, hidden = inner_hidden(field, sides, w1, b1)
+    ends, hids, columns, inner = inner_state(field, sides, place, w1, b1, w2, b2)
     send_back = outer_state(
-        positions, place, turned, hidden, sides, below, above, w1, b1, w2, b2
+        positions, place, ends, hids, columns, inner, sides, below, above, w1, b1, w2, b2
     )
     return backward_remap(returns, exchange(send_back), back_table)
 

time: 143 us -> 142 us (level)
    pallas_call x1, Pallas kernels: 1.87 us -> 3.39 us  [inner_state(): pl.pallas_call(inner_kernel, out_shape=(two, two, jax.ShapeDtypeStruct((8...]
  transfers between devices with their start and end apart: 2 -> 2, of which waited for: 1 -> 0; matrix products, arithmetic and copies ran while one was open for 0% -> 0% of each run, Pallas kernels for 1% -> 2%
where the time goes in v7:
time: 142 us
  blocking collectives  127 us (89%)
  Pallas kernels  14.4 us (10%)
    all_to_all x2, blocking collectives, exchange(): return lax.all_to_all(buffer, AXES, split_axis=0, concat_axis=0, tiled=True)  127 us
    pallas_call x1, Pallas kernels, forward_remap(): pl.pallas_call(functools.partial(forward_kernel, n_fy), out_shape=(jax.Sh...  4.44 us
    pallas_call x1, Pallas kernels, inner_state(): pl.pallas_call(inner_kernel, out_shape=(two, two, jax.ShapeDtypeStruct((8...  3.39 us
    pallas_call x1, Pallas kernels, backward_remap(): pl.pallas_call(backward_kernel, out_shape=jax.ShapeDtypeStruct((blocks, c...  2.97 us
  transfers between devices with their start and end apart: 2, of which 0 were waited for; matrix products, arithmetic and copies ran while one was open for 0% of the time, Pallas kernels for 2%

profile of v7, /device:TPU:6, one launch (start us, length us, event | category | flops | bytes accessed | tf_op | source)
XLA Modules:
  0.0 141.8 jit_solution(6442174675047369690)
XLA Ops:
  0.0 0.1 add_convert_fusion
  0.1 4.4 %shard_map.109 = (bf16[128,136,128]{2,1,0:T(8,128)(2,1)S(1)}, s32[2,64]{1,0:T(2,128)S(1)}, bf16[256,384]{1,0:T(8,128)(2,1)S(1)}, bf16[256,384]{1,0:T(8,128)(2,1)S(1)}) custom-call(s32[2,64]{1,0:T(2,128)} %bitcast.12, s32[2,64]{1,0:T(2,128)} %bitcast.13, s32[2,64]{1,0:T(2,128)} %bitcast.14, s32[2,64]{1,0:T(2,128)} %bitcast.15, bf16[64,8192]{1,0:T(8,128)(2,1)} %x_hbm.1, ...), custom_call_target="tpu_custom_call" | custom-call | tf_op jit(solution)/shard_map/pallas_call | solution.py:216
  4.5 0.1 broadcast_in_dim.12.place_ref
  4.6 66.8 %all_to_all.10.got_ref = bf16[128,136,128]{2,1,0:T(8,128)(2,1)S(1)} all-to-all(bf16[128,136,128]{2,1,0:T(8,128)(2,1)S(1)} %get-tuple-element.22), channel_id=1, replica_groups=mesh['fx'=8,'fy'=16] {'fx','fy'}, dimensions={0} | all-to-all | bytes 8912896 | tf_op jit(solution)/shard_map/all_to_all | solution.py:700
  71.4 0.0 copy-start.1
  71.4 0.0 copy-start.2
  71.4 2.1 %shard_map.110 = (bf16[64,64,128]{2,1,0:T(8,128)(2,1)S(1)}, bf16[144,128]{1,0:T(8,128)(2,1)S(1)}, bf16[144,128]{1,0:T(8,128)(2,1)S(1)}, f32[4,32,128]{2,1,0:T(8,128)S(1)}, s32[8,128]{1,0:T(8,128)S(1)}) custom-call(bf16[128,136,128]{2,1,0:T(8,128)(2,1)S(1)} %all_to_all.10.got_ref), custom_call_target="tpu_custom_call" | custom-call | tf_op jit(solution)/shard_map/pallas_call | solution.py:348
  73.5 0.0 collective-permute-start
  73.6 0.5 collective-permute-start.1
  74.1 0.0 copy-done.1
  74.1 0.0 copy-done.2
  74.1 3.4 %shard_map.111 = (bf16[2,128,128]{2,1,0:T(8,128)(2,1)S(1)}, bf16[2,128,128]{2,1,0:T(8,128)(2,1)S(1)}, f32[8,128]{1,0:T(8,128)S(1)}, bf16[64,64,128]{2,1,0:T(8,128)(2,1)S(1)}) custom-call(bf16[64,64,128]{2,1,0:T(8,128)(2,1)S(1)} %get-tuple-element.25.field_ref, f32[4,32,128]{2,1,0:T(8,128)S(1)} %get-tuple-element.26.side_ref.sides_ref, ...), custom_call_target="tpu_custom_call" | custom-call | flops 1207959552 | bytes 4194304 | tf_op jit(solution)/shard_map/pallas_call | solution.py:504
  77.5 0.0 collective-permute-done.below_ref
  77.5 0.0 collective-permute-done.1.above_ref
  77.5 1.5 %shard_map.112 = bf16[128,128,128]{2,1,0:T(8,128)(2,1)S(1)} custom-call(s32[8,128]{1,0:T(8,128)S(1)} %get-tuple-element.23.pos_hbm, s32[2,128]{1,0:T(2,128)S(1)} %broadcast_in_dim.12.place_ref, bf16[2,128,128]{2,1,0:T(8,128)(2,1)S(1)} %get-tuple-element.29.ends_ref, bf16[2,128,128]{2,1,0:T(8,128)(2,1)S(1)} %get-tuple-element.30.hids_ref, ...), custom_call_target="tpu_custom_call" | custom-call | tf_op jit(solution)/shard_map/pallas_call | solution.py:608
  79.0 0.0 copy-start
  79.0 59.8 %all_to_all.11.got_ref = bf16[128,128,128]{2,1,0:T(8,128)(2,1)S(1)} all-to-all(bf16[128,128,128]{2,1,0:T(8,128)(2,1)S(1)} %shard_map.112), channel_id=1, replica_groups=mesh['fx'=8,'fy'=16] {'fx','fy'}, dimensions={0} | all-to-all | bytes 8388608 | tf_op jit(solution)/shard_map/all_to_all | solution.py:700
  138.8 0.0 copy-done
  138.8 3.0 %shard_map.113 = bf16[64,8192]{1,0:T(8,128)(2,1)} custom-call(s32[2,64]{1,0:T(2,128)S(1)} %get-tuple-element.20.return_hbm, bf16[128,128,128]{2,1,0:T(8,128)(2,1)S(1)} %all_to_all.11.got_ref, bf16[64,128,128]{2,1,0:T(8,128)(2,1)S(1)} %copy-done), custom_call_target="tpu_custom_call" | custom-call | tf_op jit(solution)/shard_map/pallas_call | solution.py:683
Async XLA Ops:
  71.4 2.6 %copy-start.1 = (f32[64]{0:T(128)S(1)}, f32[64]{0:T(128)}, u32[]{:S(2)}) copy-start(f32[64]{0:T(128)} %param.19) | copy-start | bytes 772
  71.4 2.6 %copy-start.2 = (f32[64]{0:T(128)S(1)}, f32[64]{0:T(128)}, u32[]{:S(2)}) copy-start(f32[64]{0:T(128)} %param.21) | copy-start | bytes 772
  73.5 3.9 %collective-permute-start = (bf16[144,128]{1,0:T(8,128)(2,1)S(1)}, bf16[144,128]{1,0:T(8,128)(2,1)S(1)}, u32[]{:S(2)}, u32[]{:S(2)}) collective-permute-start(bf16[144,128]{1,0:T(8,128)(2,1)S(1)} %get-tuple-element.33), channel_id=1, source_target_pairs={{16,0},{32,16},{48,32},{64,48},{80,64},{96,80},{112,96},{0,112},{1... | collective-permute-start | bytes 110600 | tf_op jit(solution)/shard_map/ppermute | solution.py:737
  73.6 3.9 %collective-permute-start.1 = (bf16[144,128]{1,0:T(8,128)(2,1)S(1)}, bf16[144,128]{1,0:T(8,128)(2,1)S(1)}, u32[]{:S(2)}, u32[]{:S(2)}) collective-permute-start(bf16[144,128]{1,0:T(8,128)(2,1)S(1)} %get-tuple-element.34), channel_id=1, source_target_pairs={{0,16},{16,32},{32,48},{48,64},{64,80},{80,96},{96,112},{112,0},{1... | collective-permute-start | bytes 110600 | tf_op jit(solution)/shard_map/ppermute | solution.py:738
  79.0 59.8 %copy-start = (bf16[64,128,128]{2,1,0:T(8,128)(2,1)S(1)}, bf16[64,128,128]{2,1,0:T(8,128)(2,1)}, u32[]{:S(2)}) copy-start(bf16[64,128,128]{2,1,0:T(8,128)(2,1)} %table_ref.1) | copy-start | bytes 6291460

commit v8 on v7

--- a/solution.py
+++ b/solution.py
@@ -251,19 +251,19 @@
 
 def sum_kernel(
     got_ref,
-    field_ref,
+    sum0_ref,
+    sum1_ref,
     up_ref,
     down_ref,
     side_ref,
     pos_ref,
     rows_ref,
-    sum0_ref,
-    sum1_ref,
     spot_ref,
     spot_sem,
 ):
     devices, _, cols = got_ref.shape
-    hblocks, chans, _ = field_ref.shape
+    hblocks, chans, _ = sum0_ref.shape
+    hblocks -= 1
     pairs = hblocks // 2
     lanes = 2 * chans
     rows_ref[...] = got_ref[:, CAP * chans :, :].reshape(devices * META, lanes).astype(F32)
@@ -333,33 +333,27 @@
             rest = jnp.where(corner_row == n, side_ref[n, g : g + 1, :], rest)
         ref[cols:, :] = rest.astype(BF16)
 
-    def finish(r, carry):
-        field_ref[r] = total_of(r).astype(BF16)
-        return carry
-
-    lax.fori_loop(0, hblocks, finish, 0, unroll=4)
-
 
 def sum_field(got, hblocks):
     devices, depth, cols = got.shape
     chans = (depth - META) // CAP
     pairs = hblocks // 2
     message = jax.ShapeDtypeStruct((cols + 16, 2 * chans), BF16)
+    sums = jax.ShapeDtypeStruct((hblocks + 1, chans, cols), F32)
     return pl.pallas_call(
         sum_kernel,
         out_shape=(
-            jax.ShapeDtypeStruct((hblocks, chans, cols), BF16),
+            sums,
+            sums,
             message,
             message,
             jax.ShapeDtypeStruct((4, pairs, 2 * chans), F32),
             jax.ShapeDtypeStruct((8, devices), jnp.int32),
         ),
         in_specs=[vmem()],
-        out_specs=(vmem(),) * 5,
+        out_specs=(vmem(),) * 6,
         scratch_shapes=[
             pltpu.VMEM((devices * META, cols), F32),
-            pltpu.VMEM((hblocks + 1, chans, cols), F32),
-            pltpu.VMEM((hblocks + 1, chans, cols), F32),
             pltpu.SMEM((8, devices), jnp.int32),
             pltpu.SemaphoreType.DMA,
         ],
@@ -420,7 +414,8 @@
 
 
 def inner_kernel(
-    field_ref,
+    sum0_ref,
+    sum1_ref,
     side_ref,
     place_ref,
     k1_ref,
@@ -436,11 +431,12 @@
     column_ref,
     halo_ref,
 ):
-    hblocks, chans, cols = field_ref.shape
+    hblocks, chans, cols = state_ref.shape
     pairs = hblocks // 2
 
     def turn(g, carry):
-        turned_ref[g] = field_ref[pl.ds(2 * g, 2)].reshape(2 * chans, cols).T
+        both = (sum0_ref[pl.ds(2 * g, 2)] + sum1_ref[pl.ds(2 * g, 2)]).astype(BF16)
+        turned_ref[g] = both.reshape(2 * chans, cols).T
         return carry
 
     lax.fori_loop(0, pairs, turn, 0, unroll=True)
@@ -496,8 +492,9 @@
         hids_ref[n] = hid_ref[g]
 
 
-def inner_state(field, sides, place, k1, b1, k2, b2):
-    hblocks, chans, cols = field.shape
+def inner_state(sum0, sum1, sides, place, k1, b1, k2, b2):
+    hblocks, chans, cols = sum0.shape
+    hblocks -= 1
     pairs = hblocks // 2
     lanes = 2 * chans
     two = jax.ShapeDtypeStruct((2, cols, lanes), BF16)
@@ -509,7 +506,7 @@
             jax.ShapeDtypeStruct((8, lanes), F32),
             jax.ShapeDtypeStruct((hblocks, chans, cols), BF16),
         ),
-        in_specs=[vmem()] * 7,
+        in_specs=[vmem()] * 8,
         out_specs=(vmem(),) * 4,
         scratch_shapes=[
             pltpu.VMEM((pairs, cols, lanes), BF16),
@@ -521,7 +518,7 @@
         cost_estimate=pl.CostEstimate(
             flops=4 * 8192 * 9 * 64 * 64, bytes_accessed=4 << 20, transcendentals=1 << 19
         ),
-    )(field, sides, place, k1, b1, k2, b2)
+    )(sum0, sum1, sides, place, k1, b1, k2, b2)
 
 
 def outer_kernel(
@@ -733,10 +730,10 @@
     )
     send, place = lax.optimization_barrier((send, place))
     b1, b2 = bias_one[None], bias_two[None]
-    field, up, down, sides, positions = sum_field(exchange(send), hblocks)
+    sum0, sum1, up, down, sides, positions = sum_field(exchange(send), hblocks)
     below = lax.ppermute(up, "fx", [((i + 1) % n_fx, i) for i in range(n_fx)])
     above = lax.ppermute(down, "fx", [(i, (i + 1) % n_fx) for i in range(n_fx)])
-    ends, hids, columns, inner = inner_state(field, sides, place, w1, b1, w2, b2)
+    ends, hids, columns, inner = inner_state(sum0, sum1, sides, place, w1, b1, w2, b2)
     send_back = outer_state(
         positions, place, ends, hids, columns, inner, sides, below, above, w1, b1, w2, b2
     )

time: 142 us -> 142 us (level)
  no operation moved by 1% of the time
where the time goes in v8:
time: 142 us
  blocking collectives  127 us (89%)
  Pallas kernels  14.2 us (10%)
    all_to_all x2, blocking collectives, exchange(): return lax.all_to_all(buffer, AXES, split_axis=0, concat_axis=0, tiled=True)  127 us
    pallas_call x1, Pallas kernels, forward_remap(): pl.pallas_call(functools.partial(forward_kernel, n_fy), out_shape=(jax.Sh...  4.45 us
    pallas_call x1, Pallas kernels, inner_state(): pl.pallas_call(inner_kernel, out_shape=(two, two, jax.ShapeDtypeStruct((8...  3.53 us
    pallas_call x1, Pallas kernels, backward_remap(): pl.pallas_call(backward_kernel, out_shape=jax.ShapeDtypeStruct((blocks, c...  2.97 us
  transfers between devices with their start and end apart: 2, of which 0 were waited for; matrix products, arithmetic and copies ran while one was open for 0% of the time, Pallas kernels for 2%

profile of v8, /device:TPU:6, one launch (start us, length us, event | category | flops | bytes accessed | tf_op | source)
XLA Modules:
  0.0 141.7 jit_solution(7360046858660669906)
XLA Ops:
  0.0 0.1 add_convert_fusion
  0.1 4.4 %shard_map.109 = (bf16[128,136,128]{2,1,0:T(8,128)(2,1)S(1)}, s32[2,64]{1,0:T(2,128)S(1)}, bf16[256,384]{1,0:T(8,128)(2,1)S(1)}, bf16[256,384]{1,0:T(8,128)(2,1)S(1)}) custom-call(s32[2,64]{1,0:T(2,128)} %bitcast.12, s32[2,64]{1,0:T(2,128)} %bitcast.13, s32[2,64]{1,0:T(2,128)} %bitcast.14, s32[2,64]{1,0:T(2,128)} %bitcast.15, bf16[64,8192]{1,0:T(8,128)(2,1)} %x_hbm.1, ...), custom_call_target="tpu_custom_call" | custom-call | tf_op jit(solution)/shard_map/pallas_call | solution.py:216
  4.5 0.1 broadcast_in_dim.12.place_ref
  4.6 66.8 %all_to_all.10.got_ref = bf16[128,136,128]{2,1,0:T(8,128)(2,1)S(1)} all-to-all(bf16[128,136,128]{2,1,0:T(8,128)(2,1)S(1)} %get-tuple-element.23), channel_id=1, replica_groups=mesh['fx'=8,'fy'=16] {'fx','fy'}, dimensions={0} | all-to-all | bytes 8912896 | tf_op jit(solution)/shard_map/all_to_all | solution.py:697
  71.4 0.0 copy-start.1
  71.4 0.0 copy-start.2
  71.4 1.8 %shard_map.110 = (f32[65,64,128]{2,1,0:T(8,128)S(1)}, f32[65,64,128]{2,1,0:T(8,128)S(1)}, bf16[144,128]{1,0:T(8,128)(2,1)S(1)}, bf16[144,128]{1,0:T(8,128)(2,1)S...) custom-call(bf16[128,136,128]{2,1,0:T(8,128)(2,1)S(1)} %all_to_all.10.got_ref), custom_call_target="tpu_custom_call" | custom-call | tf_op jit(solution)/shard_map/pallas_call | solution.py:343
  73.3 0.0 collective-permute-start
  73.3 0.5 collective-permute-start.1
  73.8 0.0 copy-done.1
  73.8 0.0 copy-done.2
  73.8 3.5 %shard_map.111 = (bf16[2,128,128]{2,1,0:T(8,128)(2,1)S(1)}, bf16[2,128,128]{2,1,0:T(8,128)(2,1)S(1)}, f32[8,128]{1,0:T(8,128)S(1)}, bf16[64,64,128]{2,1,0:T(8,128)(2,1)S(1)}) custom-call(f32[65,64,128]{2,1,0:T(8,128)S(1)} %get-tuple-element.26.sum0_ref, f32[65,64,128]{2,1,0:T(8,128)S(1)} %get-tuple-element.27.sum1_ref, ...), custom_call_target="tpu_custom_call" | custom-call | flops 1207959552 | bytes 4194304 | tf_op jit(solution)/shard_map/pallas_call | solution.py:501
  77.3 0.0 collective-permute-done.below_ref
  77.3 0.0 collective-permute-done.1.above_ref
  77.3 1.5 %shard_map.112 = bf16[128,128,128]{2,1,0:T(8,128)(2,1)S(1)} custom-call(s32[8,128]{1,0:T(8,128)S(1)} %get-tuple-element.24.pos_hbm, s32[2,128]{1,0:T(2,128)S(1)} %broadcast_in_dim.12.place_ref, bf16[2,128,128]{2,1,0:T(8,128)(2,1)S(1)} %get-tuple-element.31.ends_ref, bf16[2,128,128]{2,1,0:T(8,128)(2,1)S(1)} %get-tuple-element.32.hids_ref, ...), custom_call_target="tpu_custom_call" | custom-call | tf_op jit(solution)/shard_map/pallas_call | solution.py:605
  78.8 0.0 copy-start
  78.8 59.9 %all_to_all.11.got_ref = bf16[128,128,128]{2,1,0:T(8,128)(2,1)S(1)} all-to-all(bf16[128,128,128]{2,1,0:T(8,128)(2,1)S(1)} %shard_map.112), channel_id=1, replica_groups=mesh['fx'=8,'fy'=16] {'fx','fy'}, dimensions={0} | all-to-all | bytes 8388608 | tf_op jit(solution)/shard_map/all_to_all | solution.py:697
  138.7 0.0 copy-done
  138.7 3.0 %shard_map.113 = bf16[64,8192]{1,0:T(8,128)(2,1)} custom-call(s32[2,64]{1,0:T(2,128)S(1)} %get-tuple-element.21.return_hbm, bf16[128,128,128]{2,1,0:T(8,128)(2,1)S(1)} %all_to_all.11.got_ref, bf16[64,128,128]{2,1,0:T(8,128)(2,1)S(1)} %copy-done), custom_call_target="tpu_custom_call" | custom-call | tf_op jit(solution)/shard_map/pallas_call | solution.py:680
Async XLA Ops:
  71.4 2.4 %copy-start.1 = (f32[64]{0:T(128)S(1)}, f32[64]{0:T(128)}, u32[]{:S(2)}) copy-start(f32[64]{0:T(128)} %param.19) | copy-start | bytes 772
  71.4 2.4 %copy-start.2 = (f32[64]{0:T(128)S(1)}, f32[64]{0:T(128)}, u32[]{:S(2)}) copy-start(f32[64]{0:T(128)} %param.21) | copy-start | bytes 772
  73.3 4.1 %collective-permute-start = (bf16[144,128]{1,0:T(8,128)(2,1)S(1)}, bf16[144,128]{1,0:T(8,128)(2,1)S(1)}, u32[]{:S(2)}, u32[]{:S(2)}) collective-permute-start(bf16[144,128]{1,0:T(8,128)(2,1)S(1)} %get-tuple-element.35), channel_id=1, source_target_pairs={{16,0},{32,16},{48,32},{64,48},{80,64},{96,80},{112,96},{0,112},{1... | collective-permute-start | bytes 110600 | tf_op jit(solution)/shard_map/ppermute | solution.py:734
  73.3 4.0 %collective-permute-start.1 = (bf16[144,128]{1,0:T(8,128)(2,1)S(1)}, bf16[144,128]{1,0:T(8,128)(2,1)S(1)}, u32[]{:S(2)}, u32[]{:S(2)}) collective-permute-start(bf16[144,128]{1,0:T(8,128)(2,1)S(1)} %get-tuple-element.36), channel_id=1, source_target_pairs={{0,16},{16,32},{32,48},{48,64},{64,80},{80,96},{96,112},{112,0},{1... | collective-permute-start | bytes 110600 | tf_op jit(solution)/shard_map/ppermute | solution.py:735
  78.8 59.9 %copy-start = (bf16[64,128,128]{2,1,0:T(8,128)(2,1)S(1)}, bf16[64,128,128]{2,1,0:T(8,128)(2,1)}, u32[]{:S(2)}) copy-start(bf16[64,128,128]{2,1,0:T(8,128)(2,1)} %table_ref.1) | copy-start | bytes 6291460

commit v9 on v8

--- a/solution.py
+++ b/solution.py
@@ -8,7 +8,7 @@
 from jax.sharding import PartitionSpec as P
 
 CAP = 2
-PAD = 8
+PAD = 24
 META = 8
 AXES = ("fx", "fy")
 F32 = jnp.float32

time: 142 us -> 142 us (level)
  no operation moved by 1% of the time
where the time goes in v9:
time: 142 us
  blocking collectives  127 us (89%)
  Pallas kernels  14.2 us (10%)
    all_to_all x2, blocking collectives, exchange(): return lax.all_to_all(buffer, AXES, split_axis=0, concat_axis=0, tiled=True)  127 us
    pallas_call x1, Pallas kernels, forward_remap(): pl.pallas_call(functools.partial(forward_kernel, n_fy), out_shape=(jax.Sh...  4.45 us
    pallas_call x1, Pallas kernels, inner_state(): pl.pallas_call(inner_kernel, out_shape=(two, two, jax.ShapeDtypeStruct((8...  3.52 us
    pallas_call x1, Pallas kernels, backward_remap(): pl.pallas_call(backward_kernel, out_shape=jax.ShapeDtypeStruct((blocks, c...  2.98 us
  transfers between devices with their start and end apart: 2, of which 0 were waited for; matrix products, arithmetic and copies ran while one was open for 0% of the time, Pallas kernels for 2%

profile of v9, /device:TPU:6, one launch (start us, length us, event | category | flops | bytes accessed | tf_op | source)
XLA Modules:
  0.0 141.7 jit_solution(7621733407639106933)
XLA Ops:
  0.0 0.1 add_convert_fusion
  0.1 4.4 %shard_map.109 = (bf16[128,136,128]{2,1,0:T(8,128)(2,1)S(1)}, s32[2,64]{1,0:T(2,128)S(1)}, bf16[256,384]{1,0:T(8,128)(2,1)S(1)}, bf16[256,384]{1,0:T(8,128)(2,1)S(1)}) custom-call(s32[2,64]{1,0:T(2,128)} %bitcast.12, s32[2,64]{1,0:T(2,128)} %bitcast.13, s32[2,64]{1,0:T(2,128)} %bitcast.14, s32[2,64]{1,0:T(2,128)} %bitcast.15, bf16[64,8192]{1,0:T(8,128)(2,1)} %x_hbm.1, ...), custom_call_target="tpu_custom_call" | custom-call | tf_op jit(solution)/shard_map/pallas_call | solution.py:216
  4.5 0.1 broadcast_in_dim.12.place_ref
  4.6 66.8 %all_to_all.10.got_ref = bf16[128,136,128]{2,1,0:T(8,128)(2,1)S(1)} all-to-all(bf16[128,136,128]{2,1,0:T(8,128)(2,1)S(1)} %get-tuple-element.23), channel_id=1, replica_groups=mesh['fx'=8,'fy'=16] {'fx','fy'}, dimensions={0} | all-to-all | bytes 8912896 | tf_op jit(solution)/shard_map/all_to_all | solution.py:697
  71.4 0.0 copy-start.1
  71.4 0.0 copy-start.2
  71.4 1.8 %shard_map.110 = (f32[65,64,128]{2,1,0:T(8,128)S(1)}, f32[65,64,128]{2,1,0:T(8,128)S(1)}, bf16[144,128]{1,0:T(8,128)(2,1)S(1)}, bf16[144,128]{1,0:T(8,128)(2,1)S...) custom-call(bf16[128,136,128]{2,1,0:T(8,128)(2,1)S(1)} %all_to_all.10.got_ref), custom_call_target="tpu_custom_call" | custom-call | tf_op jit(solution)/shard_map/pallas_call | solution.py:343
  73.3 0.0 collective-permute-start
  73.3 0.5 collective-permute-start.1
  73.8 0.0 copy-done.1
  73.8 0.0 copy-done.2
  73.8 3.5 %shard_map.111 = (bf16[2,128,128]{2,1,0:T(8,128)(2,1)S(1)}, bf16[2,128,128]{2,1,0:T(8,128)(2,1)S(1)}, f32[8,128]{1,0:T(8,128)S(1)}, bf16[64,64,128]{2,1,0:T(8,128)(2,1)S(1)}) custom-call(f32[65,64,128]{2,1,0:T(8,128)S(1)} %get-tuple-element.26.sum0_ref, f32[65,64,128]{2,1,0:T(8,128)S(1)} %get-tuple-element.27.sum1_ref, ...), custom_call_target="tpu_custom_call" | custom-call | flops 1207959552 | bytes 4194304 | tf_op jit(solution)/shard_map/pallas_call | solution.py:501
  77.3 0.0 collective-permute-done.below_ref
  77.3 0.0 collective-permute-done.1.above_ref
  77.3 1.5 %shard_map.112 = bf16[128,128,128]{2,1,0:T(8,128)(2,1)S(1)} custom-call(s32[8,128]{1,0:T(8,128)S(1)} %get-tuple-element.24.pos_hbm, s32[2,128]{1,0:T(2,128)S(1)} %broadcast_in_dim.12.place_ref, bf16[2,128,128]{2,1,0:T(8,128)(2,1)S(1)} %get-tuple-element.31.ends_ref, bf16[2,128,128]{2,1,0:T(8,128)(2,1)S(1)} %get-tuple-element.32.hids_ref, ...), custom_call_target="tpu_custom_call" | custom-call | tf_op jit(solution)/shard_map/pallas_call | solution.py:605
  78.8 0.0 copy-start
  78.8 59.9 %all_to_all.11.got_ref = bf16[128,128,128]{2,1,0:T(8,128)(2,1)S(1)} all-to-all(bf16[128,128,128]{2,1,0:T(8,128)(2,1)S(1)} %shard_map.112), channel_id=1, replica_groups=mesh['fx'=8,'fy'=16] {'fx','fy'}, dimensions={0} | all-to-all | bytes 8388608 | tf_op jit(solution)/shard_map/all_to_all | solution.py:697
  138.7 0.0 copy-done
  138.7 3.0 %shard_map.113 = bf16[64,8192]{1,0:T(8,128)(2,1)} custom-call(s32[2,64]{1,0:T(2,128)S(1)} %get-tuple-element.21.return_hbm, bf16[128,128,128]{2,1,0:T(8,128)(2,1)S(1)} %all_to_all.11.got_ref, bf16[64,128,128]{2,1,0:T(8,128)(2,1)S(1)} %copy-done), custom_call_target="tpu_custom_call" | custom-call | tf_op jit(solution)/shard_map/pallas_call | solution.py:680
Async XLA Ops:
  71.4 2.3 %copy-start.1 = (f32[64]{0:T(128)S(1)}, f32[64]{0:T(128)}, u32[]{:S(2)}) copy-start(f32[64]{0:T(128)} %param.19) | copy-start | bytes 772
  71.4 2.4 %copy-start.2 = (f32[64]{0:T(128)S(1)}, f32[64]{0:T(128)}, u32[]{:S(2)}) copy-start(f32[64]{0:T(128)} %param.21) | copy-start | bytes 772
  73.3 4.1 %collective-permute-start = (bf16[144,128]{1,0:T(8,128)(2,1)S(1)}, bf16[144,128]{1,0:T(8,128)(2,1)S(1)}, u32[]{:S(2)}, u32[]{:S(2)}) collective-permute-start(bf16[144,128]{1,0:T(8,128)(2,1)S(1)} %get-tuple-element.35), channel_id=1, source_target_pairs={{16,0},{32,16},{48,32},{64,48},{80,64},{96,80},{112,96},{0,112},{1... | collective-permute-start | bytes 110600 | tf_op jit(solution)/shard_map/ppermute | solution.py:734
  73.3 4.0 %collective-permute-start.1 = (bf16[144,128]{1,0:T(8,128)(2,1)S(1)}, bf16[144,128]{1,0:T(8,128)(2,1)S(1)}, u32[]{:S(2)}, u32[]{:S(2)}) collective-permute-start(bf16[144,128]{1,0:T(8,128)(2,1)S(1)} %get-tuple-element.36), channel_id=1, source_target_pairs={{0,16},{16,32},{32,48},{48,64},{64,80},{80,96},{96,112},{112,0},{1... | collective-permute-start | bytes 110600 | tf_op jit(solution)/shard_map/ppermute | solution.py:735
  78.8 59.9 %copy-start = (bf16[64,128,128]{2,1,0:T(8,128)(2,1)S(1)}, bf16[64,128,128]{2,1,0:T(8,128)(2,1)}, u32[]{:S(2)}) copy-start(bf16[64,128,128]{2,1,0:T(8,128)(2,1)} %table_ref.1) | copy-start | bytes 6291460
